TPU v7x, 32 devices: a whole 2x2x4 slice. The times are simulated.
32 devices in a mesh: batch: 4 (over z), tm: 8 (over y, x, core).
Axes of the slice: x: 2, y: 2, z: 4, core: 2. Of those that a mesh axis runs over, the one named last changes fastest.
Arguments:
- x_small: bfloat16 [32, 8, 49, 512], P('batch', 'tm'), may hold values from -6 to 6
- x_large: bfloat16 [32, 8, 100, 512], P('batch', 'tm'), may hold values from -6 to 6
- small_output_gradient: bfloat16 [32, 8, 49, 512], P('batch', 'tm'), may hold values from -6 to 6
- large_output_gradient: bfloat16 [32, 8, 100, 512], P('batch', 'tm'), may hold values from -6 to 6
- clip_counts: int32 [2, 4], replicated, may hold values from 1 to 8, as said below
- first_spatial: float32 [4608, 1152], P('tm', 'batch'), may hold values from -0.09375 to 0.09375
- first_temporal: float32 [3456, 512], P('tm', 'batch'), may hold values from -0.109375 to 0.109375
- second_spatial: float32 [4608, 1152], P('tm', 'batch'), may hold values from -0.09375 to 0.09375
- second_temporal: float32 [3456, 512], P('tm', 'batch'), may hold values from -0.109375 to 0.109375
- norm_params: float32 [2, 3328], replicated, may hold values from -0.5 to 1.4, as said below
- first_spatial_momentum: float32 [4608, 1152], P('tm', 'batch'), may hold values from -0.0004272461 to 0.0004272461
- first_temporal_momentum: float32 [3456, 512], P('tm', 'batch'), may hold values from -0.0004272461 to 0.0004272461
- second_spatial_momentum: float32 [4608, 1152], P('tm', 'batch'), may hold values from -0.0004272461 to 0.0004272461
- second_temporal_momentum: float32 [3456, 512], P('tm', 'batch'), may hold values from -0.0004272461 to 0.0004272461
- norm_momentum: float32 [2, 3328], replicated, may hold values from -0.0012207031 to 0.0012207031
- first_spatial_variance: float32 [4608, 1152], P('tm', 'batch'), may hold values from 7.0609345e-11 to 2.8243738e-10
- first_temporal_variance: float32 [3456, 512], P('tm', 'batch'), may hold values from 7.0609345e-11 to 2.8243738e-10
- second_spatial_variance: float32 [4608, 1152], P('tm', 'batch'), may hold values from 7.0609345e-11 to 2.8243738e-10
- second_temporal_variance: float32 [3456, 512], P('tm', 'batch'), may hold values from 7.0609345e-11 to 2.8243738e-10
- norm_variance: float32 [2, 3328], replicated, may hold values from 8.473121e-11 to 3.3892483e-10
Outputs:
- output_small: float32 [32, 8, 49, 512], P('batch', 'tm')
- output_large: float32 [32, 8, 100, 512], P('batch', 'tm')
- input_grad_small: float32 [32, 8, 49, 512], P('batch', 'tm')
- input_grad_large: float32 [32, 8, 100, 512], P('batch', 'tm')
- grad_norm: float32 [], replicated
- updated_first_spatial: float32 [4608, 1152], P('tm', 'batch')
- momentum_first_spatial: float32 [4608, 1152], P('tm', 'batch')
- variance_first_spatial: float32 [4608, 1152], P('tm', 'batch')
- updated_first_temporal: float32 [3456, 512], P('tm', 'batch')
- momentum_first_temporal: float32 [3456, 512], P('tm', 'batch')
- variance_first_temporal: float32 [3456, 512], P('tm', 'batch')
- updated_second_spatial: float32 [4608, 1152], P('tm', 'batch')
- momentum_second_spatial: float32 [4608, 1152], P('tm', 'batch')
- variance_second_spatial: float32 [4608, 1152], P('tm', 'batch')
- updated_second_temporal: float32 [3456, 512], P('tm', 'batch')
- momentum_second_temporal: float32 [3456, 512], P('tm', 'batch')
- variance_second_temporal: float32 [3456, 512], P('tm', 'batch')
- updated_norms: float32 [2, 3328], replicated
- momentum_norms: float32 [2, 3328], replicated
- variance_norms: float32 [2, 3328], replicated
Inputs may be any that keep to these rules, and one draw needn't show every extreme that they name: `clip_counts`: the live clips of a group on a batch index are its first slots; in each group some batch index has all 8 live. `norm_params`: gains lie in 0.6 to 1.4, biases in -0.5 to 0.5.
All inputs are finite; a program needn't handle non-finite values.
Results may differ from a plain program's by a relative error of at most 0.02.
Values may be sent and summed in bfloat16 or wider, within the bound.
A program may use at most 320 MiB of HBM per device.

v0:
```python
import jax
import jax.numpy as jnp
from jax import lax
from jax.sharding import PartitionSpec as P

D = 512
MID = 1152
HS = 7
HL = 10
STEP = 10


NORM_EPS = 1e-05
THRESHOLD = 1.0
BETA_ONE = 0.9
BETA_TWO = 0.999
WEIGHT_RATE = 0.03
NORM_RATE = 0.25
WEIGHT_DECAY = 0.05
ADAM_EPS = 1e-08


def padded_2(value, sides, width):
    for axis, dim in sides:
        size, length = (lax.axis_size(axis), value.shape[dim])
        up = [(i, (i + 1) % size) for i in range(size - 1)]
        down = [(j, i) for i, j in up]
        last = lax.slice_in_dim(value, length - width, length, axis=dim)
        first = lax.slice_in_dim(value, 0, width, axis=dim)
        before = lax.ppermute(last, axis, up)
        after = lax.ppermute(first, axis, down)
        value = jnp.concatenate([before, value, after], axis=dim)
    return value


def silu_slope(input_value):
    sigmoid_value = jax.nn.sigmoid(input_value)
    return sigmoid_value * (1.0 + input_value * (1.0 - sigmoid_value))


def spatial_taps(field, side):
    clips, frames, cells, channels = field.shape
    grid = field.reshape(clips, frames, side, side, channels)
    padded = jnp.pad(grid, ((0, 0), (0, 0), (1, 1), (1, 1), (0, 0)))
    pieces = [
        padded[:, :, row : row + side, column : column + side, :]
        for row in range(3)
        for column in range(3)
    ]
    return jnp.concatenate(pieces, axis=-1).reshape(clips * frames * cells, 9 * channels)


def spatial_forward(field_small, field_large, weight):
    taps_small = spatial_taps(field_small, HS)
    taps_large = spatial_taps(field_large, HL)
    result_small = jnp.dot(taps_small, weight, preferred_element_type=jnp.float32).reshape(
        field_small.shape[:3] + (weight.shape[1],)
    )
    result_large = jnp.dot(taps_large, weight, preferred_element_type=jnp.float32).reshape(
        field_large.shape[:3] + (weight.shape[1],)
    )
    return (jnp.concatenate([result_small, result_large], axis=2), taps_small, taps_large)


def spatial_backward(upstream_rows, weight, shape, side):
    clips, frames, cells, channels = shape
    columns = lax.dot_general(
        upstream_rows, weight, (((1,), (1,)), ((), ())), preferred_element_type=jnp.float32
    )
    columns = columns.reshape(clips, frames, side, side, 9 * channels)
    padded = jnp.pad(columns, ((0, 0), (0, 0), (1, 1), (1, 1), (0, 0)))
    final_result = None
    for row in range(3):
        for column in range(3):
            offset = (3 * row + column) * channels
            window = padded[
                :,
                :,
                2 - row : 2 - row + side,
                2 - column : 2 - column + side,
                offset : offset + channels,
            ]
            final_result = window if final_result is None else final_result + window
    return final_result.reshape(clips, frames, cells, channels)


def temporal_forward(field, weight):
    padded = padded_2(field, (("tm", 1),), 1)
    frames = field.shape[1]
    pieces = jnp.concatenate([padded[:, shift : shift + frames] for shift in range(3)], axis=-1)
    rows = pieces.reshape(-1, pieces.shape[-1])
    final_result = jnp.dot(rows, weight, preferred_element_type=jnp.float32).reshape(
        field.shape[:3] + (weight.shape[1],)
    )
    return (final_result, rows)


def temporal_backward(upstream_gradient, weight):
    padded = padded_2(upstream_gradient, (("tm", 1),), 1)
    frames = upstream_gradient.shape[1]
    pieces = jnp.concatenate(
        [padded[:, 2 - shift : 2 - shift + frames] for shift in range(3)], axis=-1
    )
    rows = pieces.reshape(-1, pieces.shape[-1])
    kernel = (
        weight.reshape(3, -1, weight.shape[1]).transpose(1, 0, 2).reshape(-1, 3 * weight.shape[1])
    )
    final_result = lax.dot_general(
        rows, kernel, (((1,), (1,)), ((), ())), preferred_element_type=jnp.float32
    )
    return final_result.reshape(upstream_gradient.shape[:3] + (kernel.shape[0],))


def group_totals(leading_part, trailing_part, active_flags, split_point):
    leading_cells = jnp.sum(active_flags * leading_part, axis=(0, 1))
    trailing_cells = jnp.sum(active_flags * trailing_part, axis=(0, 1))
    first_groups = jnp.stack(
        [jnp.sum(leading_cells[:split_point], axis=0), jnp.sum(leading_cells[split_point:], axis=0)]
    )
    second_groups = jnp.stack(
        [
            jnp.sum(trailing_cells[:split_point], axis=0),
            jnp.sum(trailing_cells[split_point:], axis=0),
        ]
    )
    return (first_groups, second_groups)


def per_cell(stat, split_point, cells):
    channels = stat.shape[1]
    return jnp.concatenate(
        [
            jnp.broadcast_to(stat[0], (split_point, channels)),
            jnp.broadcast_to(stat[1], (cells - split_point, channels)),
        ],
        axis=0,
    )


def norm_forward_pass(
    input_value, active_flags, split_point, grand_totals, norm_gain_vector, norm_shift_bias
):
    running_sums, squared_values = group_totals(
        input_value, input_value * input_value, active_flags, split_point
    )
    running_sums, squared_values = lax.psum((running_sums, squared_values), ("batch", "tm"))
    mean = running_sums / grand_totals[:, None]
    scale = lax.rsqrt(squared_values / grand_totals[:, None] - mean * mean + NORM_EPS)
    cells = input_value.shape[2]
    cell_scale = per_cell(scale, split_point, cells)
    normalized_values = (input_value - per_cell(mean, split_point, cells)) * cell_scale
    return (normalized_values * norm_gain_vector + norm_shift_bias, normalized_values, cell_scale)


def norm_reverse_pass(
    upstream_gradient,
    normalized_values,
    cell_scale,
    norm_gain_vector,
    active_flags,
    split_point,
    grand_totals,
):
    running_sums, cross_product = group_totals(
        upstream_gradient, upstream_gradient * normalized_values, active_flags, split_point
    )
    running_sums, cross_product = lax.psum((running_sums, cross_product), ("batch", "tm"))
    cells = upstream_gradient.shape[2]
    upstream_average = per_cell(running_sums / grand_totals[:, None], split_point, cells)
    cross_average = per_cell(cross_product / grand_totals[:, None], split_point, cells)
    final_result = (
        active_flags
        * (norm_gain_vector * cell_scale)
        * (upstream_gradient - upstream_average - normalized_values * cross_average)
    )
    return (final_result, jnp.sum(cross_product, axis=0), jnp.sum(running_sums, axis=0))


def reduce_weight(pairs, depth, width):
    total = jnp.zeros((depth // lax.axis_size("tm") * lax.axis_size("tm"), width), jnp.float32)
    for left, right in pairs:
        total = total + lax.dot_general(
            left, right, (((0,), (0,)), ((), ())), preferred_element_type=jnp.float32
        )
    shared = lax.psum_scatter(total.astype(jnp.bfloat16), "tm", scatter_dimension=0, tiled=True)
    return lax.psum_scatter(shared, "batch", scatter_dimension=1, tiled=True).astype(jnp.float32)


def own_square(shard):
    local = jnp.sum(shard * shard)
    return local


def adamw(weight, gradient, momentum, variance, factor, rate, decay):
    clipped = gradient * factor
    new_momentum = BETA_ONE * momentum + (1.0 - BETA_ONE) * clipped
    new_variance = BETA_TWO * variance + (1.0 - BETA_TWO) * clipped * clipped
    corrected = new_momentum / (1.0 - BETA_ONE**STEP)
    spread = jnp.sqrt(new_variance / (1.0 - BETA_TWO**STEP))
    new_weight = weight - rate * (corrected / (spread + ADAM_EPS) + decay * weight)
    return (new_weight, new_momentum, new_variance)


def body(
    x_small,
    x_large,
    small_output_gradient,
    large_output_gradient,
    clip_counts,
    first_spatial,
    first_temporal,
    second_spatial,
    second_temporal,
    norm_params,
    first_spatial_momentum,
    first_temporal_momentum,
    second_spatial_momentum,
    second_temporal_momentum,
    norm_momentum,
    first_spatial_variance,
    first_temporal_variance,
    second_spatial_variance,
    second_temporal_variance,
    norm_variance,
):
    low_one = first_spatial.astype(jnp.bfloat16)
    low_two = first_temporal.astype(jnp.bfloat16)
    low_three = second_spatial.astype(jnp.bfloat16)
    low_four = second_temporal.astype(jnp.bfloat16)
    columns = (
        lax.all_gather(low_one, "batch", axis=1, tiled=True),
        lax.all_gather(low_two, "batch", axis=1, tiled=True),
        lax.all_gather(low_three, "batch", axis=1, tiled=True),
        lax.all_gather(low_four, "batch", axis=1, tiled=True),
    )
    spatial_one, temporal_one, spatial_two, temporal_two = (
        lax.all_gather(columns[0], "tm", axis=0, tiled=True),
        lax.all_gather(columns[1], "tm", axis=0, tiled=True),
        lax.all_gather(columns[2], "tm", axis=0, tiled=True),
        lax.all_gather(columns[3], "tm", axis=0, tiled=True),
    )
    clips = x_small.shape[0]
    split_point = x_small.shape[2]
    large_cells = x_large.shape[2]
    batch_index = lax.axis_index("batch")
    slots = jnp.arange(clips, dtype=jnp.int32)
    live_small = (slots < clip_counts[0, batch_index]).astype(jnp.float32)
    live_large = (slots < clip_counts[1, batch_index]).astype(jnp.float32)
    active_flags = jnp.concatenate(
        [
            jnp.broadcast_to(live_small[:, None, None, None], (clips, 1, split_point, 1)),
            jnp.broadcast_to(live_large[:, None, None, None], (clips, 1, large_cells, 1)),
        ],
        axis=2,
    )
    frames_total = x_small.shape[1] * lax.axis_size("tm")
    grand_totals = jnp.stack(
        [
            jnp.sum(clip_counts[0]).astype(jnp.float32) * frames_total * split_point,
            jnp.sum(clip_counts[1]).astype(jnp.float32) * frames_total * large_cells,
        ]
    )
    bounds = (0, MID, MID + D, 2 * MID + D, 2 * MID + 2 * D)
    gain_vectors = [norm_params[0, bounds[index] : bounds[index + 1]] for index in range(4)]
    bias_vectors = [norm_params[1, bounds[index] : bounds[index + 1]] for index in range(4)]
    first_convolved, taps_one_small, taps_one_large = spatial_forward(x_small, x_large, spatial_one)
    hidden_one, normed_one, scale_one = norm_forward_pass(
        first_convolved, active_flags, split_point, grand_totals, gain_vectors[0], bias_vectors[0]
    )
    act_one = jax.nn.silu(hidden_one).astype(jnp.bfloat16)
    second_convolved, rows_two = temporal_forward(act_one, temporal_one)
    hidden_two, normed_two, scale_two = norm_forward_pass(
        second_convolved, active_flags, split_point, grand_totals, gain_vectors[1], bias_vectors[1]
    )
    act_two = jax.nn.silu(hidden_two).astype(jnp.bfloat16)
    third_convolved, taps_three_small, taps_three_large = spatial_forward(
        act_two[:, :, :split_point], act_two[:, :, split_point:], spatial_two
    )
    hidden_three, normed_three, scale_three = norm_forward_pass(
        third_convolved, active_flags, split_point, grand_totals, gain_vectors[2], bias_vectors[2]
    )
    act_three = jax.nn.silu(hidden_three).astype(jnp.bfloat16)
    fourth_convolved, rows_four = temporal_forward(act_three, temporal_two)
    hidden_four, fourth_normalized, fourth_scale = norm_forward_pass(
        fourth_convolved, active_flags, split_point, grand_totals, gain_vectors[3], bias_vectors[3]
    )
    residual_in = jnp.concatenate([x_small, x_large], axis=2).astype(jnp.float32)
    output_preactivation = hidden_four + residual_in
    block_output = active_flags * jax.nn.silu(output_preactivation)
    upstream_gradient = (
        jnp.concatenate([small_output_gradient, large_output_gradient], axis=2).astype(jnp.float32)
        * active_flags
    )
    passed_gradient = upstream_gradient * silu_slope(output_preactivation)
    squared_values = []
    grad_conv_four, gain_four, bias_four = norm_reverse_pass(
        passed_gradient,
        fourth_normalized,
        fourth_scale,
        gain_vectors[3],
        active_flags,
        split_point,
        grand_totals,
    )
    grad_conv_four = grad_conv_four.astype(jnp.bfloat16)
    rows_grad_four = grad_conv_four.reshape(-1, grad_conv_four.shape[-1])
    grad_second_temporal = reduce_weight(
        [(rows_four, rows_grad_four)], rows_four.shape[1], rows_grad_four.shape[1]
    )
    squared_values.append(own_square(grad_second_temporal))
    grad_act_three = temporal_backward(grad_conv_four, temporal_two)
    grad_conv_three, gain_three, bias_three = norm_reverse_pass(
        grad_act_three * silu_slope(hidden_three),
        normed_three,
        scale_three,
        gain_vectors[2],
        active_flags,
        split_point,
        grand_totals,
    )
    grad_conv_three = grad_conv_three.astype(jnp.bfloat16)
    rows_three_small = grad_conv_three[:, :, :split_point].reshape(-1, grad_conv_three.shape[-1])
    rows_three_large = grad_conv_three[:, :, split_point:].reshape(-1, grad_conv_three.shape[-1])
    grad_second_spatial = reduce_weight(
        [(taps_three_small, rows_three_small), (taps_three_large, rows_three_large)],
        taps_three_small.shape[1],
        rows_three_small.shape[1],
    )
    squared_values.append(own_square(grad_second_spatial))
    channels_mid = act_two.shape[-1]
    grad_act_two = jnp.concatenate(
        [
            spatial_backward(
                rows_three_small,
                spatial_two,
                (clips, act_two.shape[1], split_point, channels_mid),
                HS,
            ),
            spatial_backward(
                rows_three_large,
                spatial_two,
                (clips, act_two.shape[1], large_cells, channels_mid),
                HL,
            ),
        ],
        axis=2,
    )
    grad_conv_two, gain_two, bias_two = norm_reverse_pass(
        grad_act_two * silu_slope(hidden_two),
        normed_two,
        scale_two,
        gain_vectors[1],
        active_flags,
        split_point,
        grand_totals,
    )
    grad_conv_two = grad_conv_two.astype(jnp.bfloat16)
    rows_grad_two = grad_conv_two.reshape(-1, grad_conv_two.shape[-1])
    grad_first_temporal = reduce_weight(
        [(rows_two, rows_grad_two)], rows_two.shape[1], rows_grad_two.shape[1]
    )
    squared_values.append(own_square(grad_first_temporal))
    grad_act_one = temporal_backward(grad_conv_two, temporal_one)
    grad_conv_one, gain_one, bias_one = norm_reverse_pass(
        grad_act_one * silu_slope(hidden_one),
        normed_one,
        scale_one,
        gain_vectors[0],
        active_flags,
        split_point,
        grand_totals,
    )
    grad_conv_one = grad_conv_one.astype(jnp.bfloat16)
    rows_one_small = grad_conv_one[:, :, :split_point].reshape(-1, grad_conv_one.shape[-1])
    rows_one_large = grad_conv_one[:, :, split_point:].reshape(-1, grad_conv_one.shape[-1])
    grad_first_spatial = reduce_weight(
        [(taps_one_small, rows_one_small), (taps_one_large, rows_one_large)],
        taps_one_small.shape[1],
        rows_one_small.shape[1],
    )
    squared_values.append(own_square(grad_first_spatial))
    input_small = passed_gradient[:, :, :split_point] + spatial_backward(
        rows_one_small, spatial_one, x_small.shape, HS
    )
    input_large = passed_gradient[:, :, split_point:] + spatial_backward(
        rows_one_large, spatial_one, x_large.shape, HL
    )
    grad_params = jnp.stack(
        [
            jnp.concatenate([gain_one, gain_two, gain_three, gain_four]),
            jnp.concatenate([bias_one, bias_two, bias_three, bias_four]),
        ]
    )
    summed = lax.psum(
        (squared_values[0], squared_values[1], squared_values[2], squared_values[3]),
        ("batch", "tm"),
    )
    weight_square = summed[0] + summed[1] + summed[2] + summed[3]
    grad_norm = jnp.sqrt(weight_square + jnp.sum(grad_params * grad_params))
    factor = THRESHOLD / jnp.maximum(grad_norm, THRESHOLD)
    one = adamw(
        first_spatial,
        grad_first_spatial,
        first_spatial_momentum,
        first_spatial_variance,
        factor,
        WEIGHT_RATE,
        WEIGHT_DECAY,
    )
    two = adamw(
        first_temporal,
        grad_first_temporal,
        first_temporal_momentum,
        first_temporal_variance,
        factor,
        WEIGHT_RATE,
        WEIGHT_DECAY,
    )
    three = adamw(
        second_spatial,
        grad_second_spatial,
        second_spatial_momentum,
        second_spatial_variance,
        factor,
        WEIGHT_RATE,
        WEIGHT_DECAY,
    )
    four = adamw(
        second_temporal,
        grad_second_temporal,
        second_temporal_momentum,
        second_temporal_variance,
        factor,
        WEIGHT_RATE,
        WEIGHT_DECAY,
    )
    norms = adamw(norm_params, grad_params, norm_momentum, norm_variance, factor, NORM_RATE, 0.0)
    return (
        block_output[:, :, :split_point],
        block_output[:, :, split_point:],
        input_small,
        input_large,
        grad_norm,
        one[0],
        one[1],
        one[2],
        two[0],
        two[1],
        two[2],
        three[0],
        three[1],
        three[2],
        four[0],
        four[1],
        four[2],
        norms[0],
        norms[1],
        norms[2],
    )


def solution(mesh):
    return jax.shard_map(
        body,
        mesh=mesh,
        in_specs=(
            P("batch", "tm", None, None),
            P("batch", "tm", None, None),
            P("batch", "tm", None, None),
            P("batch", "tm", None, None),
            P(),
            P("tm", "batch"),
            P("tm", "batch"),
            P("tm", "batch"),
            P("tm", "batch"),
            P(),
            P("tm", "batch"),
            P("tm", "batch"),
            P("tm", "batch"),
            P("tm", "batch"),
            P(),
            P("tm", "batch"),
            P("tm", "batch"),
            P("tm", "batch"),
            P("tm", "batch"),
            P(),
        ),
        out_specs=(
            P("batch", "tm", None, None),
            P("batch", "tm", None, None),
            P("batch", "tm", None, None),
            P("batch", "tm", None, None),
            P(),
            P("tm", "batch"),
            P("tm", "batch"),
            P("tm", "batch"),
            P("tm", "batch"),
            P("tm", "batch"),
            P("tm", "batch"),
            P("tm", "batch"),
            P("tm", "batch"),
            P("tm", "batch"),
            P("tm", "batch"),
            P("tm", "batch"),
            P("tm", "batch"),
            P(),
            P(),
            P(),
        ),
        check_vma=False,
    )
```

profile of v0, /device:TPU:0, one launch (start us, length us, event | category | flops | bytes accessed | tf_op | source)
XLA Modules:
  0.0 1497.1 jit_solution(8834111746622137477)
XLA Ops:
  11.3 37.1 %all-gather.7.cloned.1.call-done = bf16[576,1152]{0,1:T(8,128)(2,1)} async-done(((bf16[576,288]{0,1:T(8,128)(2,1)}), bf16[576,1152]{0,1:T(8,128)(2,1)}) %all-gather.7.cloned.1.call-update) | async-done | bytes 1327120 | tf_op jit(solution)/shard_map/all_gather | solution.py:231
  51.0 18.0 %all_gather.30 = bf16[432,512]{1,0:T(8,128)(2,1)} all-gather(bf16[432,128]{1,0:T(8,128)(2,1)S(1)} %convert_element_type.247), channel_id=1, replica_groups=mesh['batch'=4,'tm'=8] {'batch'}, dimensions={1}, use_global_device_ids=true | all-gather | bytes 552960 | tf_op jit(solution)/shard_map/all_gather | solution.py:234
  69.2 24.0 %all_gather.26 = bf16[432,512]{1,0:T(8,128)(2,1)} all-gather(bf16[432,128]{1,0:T(8,128)(2,1)S(1)} %convert_element_type.242), channel_id=1, replica_groups=mesh['batch'=4,'tm'=8] {'batch'}, dimensions={1}, use_global_device_ids=true | all-gather | bytes 552960 | tf_op jit(solution)/shard_map/all_gather | solution.py:232
  120.1 38.9 %all-gather.9.cloned.1.call-done = bf16[4608,1152]{1,0:T(8,128)(2,1)} async-done(((bf16[576,1152]{1,0:T(8,128)(2,1)}), bf16[4608,1152]{1,0:T(8,128)(2,1)}) %all-gather.9.cloned.1.call-update) | async-done | bytes 10616848 | tf_op jit(solution)/shard_map/all_gather | solution.py:237
  159.0 10.9 fusion.14
  169.9 13.2 fusion.12
  185.9 39.8 %all-reduce.15 = (f32[2,1152]{1,0:T(2,128)S(1)}, f32[2,1152]{1,0:T(2,128)S(1)}) all-reduce(f32[2,1152]{1,0:T(2,128)S(1)} %pad_maximum_fusion.23, f32[2,1152]{1,0:T(2,128)S(1)} %pad_maximum_fusion.24), channel_id=1, replica_groups=mesh['batch'=4,'tm'=8] {'batch','tm'}, use_global_device_ids=true, to_apply=%region_3.4 | all-reduce | flops 4608 | bytes 36864 | tf_op jit(solution)/shard_map/psum | solution.py:146
  228.1 3.7 multiply_convert_fusion.3
  235.0 4.8 collective-permute-start
  251.6 3.4 reshape.1541
  258.8 6.2 copy.491
  265.0 5.6 mul.1298
  270.7 5.8 multiply_convert_fusion.5
  281.3 4.2 copy.457
  285.5 4.2 concatenate.467
  289.7 9.1 fusion.26
  302.2 99.9 %all-reduce.14 = (f32[2,512]{1,0:T(2,128)S(1)}, f32[2,512]{1,0:T(2,128)S(1)}) all-reduce(f32[2,512]{1,0:T(2,128)S(1)} %pad_maximum_fusion.32, f32[2,512]{1,0:T(2,128)S(1)} %pad_maximum_fusion.33), channel_id=1, replica_groups=mesh['batch'=4,'tm'=8] {'batch','tm'}, use_global_device_ids=true, to_apply=%region_13.14 | all-reduce | flops 2048 | bytes 16384 | tf_op jit(solution)/shard_map/psum | solution.py:146
  422.6 14.6 fusion.8
  437.2 5.6 fusion.10
  445.5 39.4 %all-reduce.13 = (f32[2,1152]{1,0:T(2,128)S(1)}, f32[2,1152]{1,0:T(2,128)S(1)}) all-reduce(f32[2,1152]{1,0:T(2,128)S(1)} %pad_maximum_fusion.25, f32[2,1152]{1,0:T(2,128)S(1)} %pad_maximum_fusion.26), channel_id=1, replica_groups=mesh['batch'=4,'tm'=8] {'batch','tm'}, use_global_device_ids=true, to_apply=%region_21.22 | all-reduce | flops 4608 | bytes 36864 | tf_op jit(solution)/shard_map/psum | solution.py:146
  487.1 4.5 multiply_convert_fusion.2
  495.0 4.5 collective-permute-start.2
  511.2 5.7 mul.1322
  548.9 5.8 multiply_convert_fusion.4
  559.3 3.6 copy.480
  563.0 4.2 concatenate.495
  567.2 9.1 fusion.32
  579.7 41.2 %all-reduce.12 = (f32[2,512]{1,0:T(2,128)S(1)}, f32[2,512]{1,0:T(2,128)S(1)}) all-reduce(f32[2,512]{1,0:T(2,128)S(1)} %pad_maximum_fusion.34, f32[2,512]{1,0:T(2,128)S(1)} %pad_maximum_fusion.35), channel_id=1, replica_groups=mesh['batch'=4,'tm'=8] {'batch','tm'}, use_global_device_ids=true, to_apply=%region_29.30 | all-reduce | flops 2048 | bytes 16384 | tf_op jit(solution)/shard_map/psum | solution.py:146
  622.6 5.3 multiply_reduce_fusion.11
  628.1 38.8 %all-reduce.11 = (f32[2,512]{1,0:T(2,128)S(1)}, f32[2,512]{1,0:T(2,128)S(1)}) all-reduce(f32[2,512]{1,0:T(2,128)S(1)} %pad_maximum_fusion.37, f32[2,512]{1,0:T(2,128)S(1)} %pad_maximum_fusion.36), channel_id=1, replica_groups=mesh['batch'=4,'tm'=8] {'batch','tm'}, use_global_device_ids=true, to_apply=%region_41.42 | all-reduce | flops 2048 | bytes 16384 | tf_op jit(solution)/shard_map/psum | solution.py:167
  699.4 15.7 %multiply_convert_fusion.10 = (bf16[1192,512]{1,0:T(8,128)(2,1)}, bf16[1192,512]{1,0:T(8,128)(2,1)}) fusion(f32[1192,512]{1,0:T(8,128)} %mul.1438, f32[1192,512]{1,0:T(8,128)} %sub.390, f32[1192,512]{1,0:T(8,128)} %reshape.1543, f32[1192,512]{1,0:T(8,128)} %mul.1431, f32[1192,512]{1,0:T(8,128)} %fusion.32, f32[1192,512]{1,0:T(8,128)} %sub.386, ...), kind=kLoop, calls=%fused_computation.161 | loop fusion | flops 24412160 | bytes 39068320 | tf_op jit(solution)/shard_map/convert_element_type | solution.py:305
  717.8 9.6 bitcast_convert_fusion.1
  734.2 11.6 multiply_reduce_fusion.3
  746.1 44.3 %all-reduce.10 = (f32[2,1152]{1,0:T(2,128)S(1)}, f32[2,1152]{1,0:T(2,128)S(1)}) all-reduce(f32[2,1152]{1,0:T(2,128)S(1)} %pad_maximum_fusion.28, f32[2,1152]{1,0:T(2,128)S(1)} %pad_maximum_fusion.27), channel_id=1, replica_groups=mesh['batch'=4,'tm'=8] {'batch','tm'}, use_global_device_ids=true, to_apply=%region_49.50 | all-reduce | flops 4608 | bytes 36864 | tf_op jit(solution)/shard_map/psum | solution.py:167
  793.6 4.6 fusion.62
  801.5 19.1 %convolution_bitcast_fusion.1 = f32[8,1,10,10,4608]{4,3,2,0,1:T(8,128)} fusion(bf16[4608,1152]{1,0:T(8,128)(2,1)S(1)} %bitcast.453, bf16[8,10,10,1152]{3,0,2,1:T(8,128)(2,1)S(1)} %bitcast.393), kind=kOutput, calls=%fused_computation.37 | convolution fusion | flops 8493465600 | bytes 27205632 | tf_op jit(solution)/shard_map/dot_general | solution.py:67
  820.6 9.1 fusion.71
  833.0 7.9 fusion.40
  842.9 3.6 multiply_reduce_fusion.9
  846.7 39.7 %all-reduce.9 = (f32[2,512]{1,0:T(2,128)S(1)}, f32[2,512]{1,0:T(2,128)S(1)}) all-reduce(f32[2,512]{1,0:T(2,128)S(1)} %pad_maximum_fusion.39, f32[2,512]{1,0:T(2,128)S(1)} %pad_maximum_fusion.38), channel_id=1, replica_groups=mesh['batch'=4,'tm'=8] {'batch','tm'}, use_global_device_ids=true, to_apply=%region_57.58 | all-reduce | flops 2048 | bytes 16384 | tf_op jit(solution)/shard_map/psum | solution.py:167
  896.8 3.5 sub.398
  905.0 3.4 concatenate.555
  910.2 3.5 mul.1410
  916.4 3.4 sub.376
  919.9 3.4 concatenate.517
  923.3 14.1 multiply_convert_fusion.9
  940.1 10.3 bitcast_convert_fusion
  999.6 12.2 fusion.148
  1011.9 20.5 %fusion = bf16[4608,1152]{1,0:T(8,128)(2,1)} fusion(f32[4608,1152]{1,0:T(8,128)} %fusion.148, bf16[800,4608]{1,0:T(8,128)(2,1)} %constant_dynamic-update-slice_fusion.13, bf16[800,1152]{1,0:T(8,128)(2,1)} %reshape.1536), kind=kOutput, calls=%fused_computation.34 | convolution fusion | flops 8504082432 | bytes 41066496 | tf_op jit(solution)/shard_map/dot_general | solution.py:182
  1109.6 3.9 copy.503
  1119.9 11.7 multiply_reduce_fusion.1
  1131.9 45.4 %all-reduce.8 = (f32[2,1152]{1,0:T(2,128)S(1)}, f32[2,1152]{1,0:T(2,128)S(1)}) all-reduce(f32[2,1152]{1,0:T(2,128)S(1)} %pad_maximum_fusion.30, f32[2,1152]{1,0:T(2,128)S(1)} %pad_maximum_fusion.29), channel_id=1, replica_groups=mesh['batch'=4,'tm'=8] {'batch','tm'}, use_global_device_ids=true, to_apply=%region_65.66 | all-reduce | flops 4608 | bytes 36864 | tf_op jit(solution)/shard_map/psum | solution.py:167
  1180.5 4.4 fusion.63
  1188.1 12.2 fusion.149
  1200.3 20.6 %fusion.1 = bf16[4608,1152]{1,0:T(8,128)(2,1)} fusion(f32[4608,1152]{1,0:T(8,128)} %fusion.149, bf16[800,4608]{1,0:T(8,128)(2,1)} %copy-done.169, bf16[800,1152]{1,0:T(8,128)(2,1)} %reshape.1539), kind=kOutput, calls=%fused_computation.35 | convolution fusion | flops 8504082432 | bytes 41066496 | tf_op jit(solution)/shard_map/dot_general | solution.py:182
  1252.7 21.4 %convolution_bitcast_fusion = f32[8,1,10,10,4608]{4,3,2,0,1:T(8,128)} fusion(bf16[4608,1152]{1,0:T(8,128)(2,1)} %all-gather.9.cloned.1.call-done, bf16[8,10,10,1152]{3,0,2,1:T(8,128)(2,1)S(1)} %bitcast.392), kind=kOutput, calls=%fused_computation.36 | convolution fusion | flops 8493465600 | bytes 27205632 | tf_op jit(solution)/shard_map/dot_general | solution.py:67
  1274.0 29.3 %reduce-scatter.23.cloned.1.call-done = bf16[576,1152]{1,0:T(8,128)(2,1)} async-done(((bf16[4608,1152]{1,0:T(8,128)(2,1)}), bf16[576,1152]{1,0:T(8,128)(2,1)}) %reduce-scatter.23.cloned.1.call-update) | async-done | bytes 1327120 | tf_op jit(solution)/shard_map/reduce_scatter | solution.py:185
  1306.0 7.6 fusion.43
  1317.6 9.4 fusion.79
  1331.8 18.7 %reduce-scatter.29.cloned.1.call-done = bf16[128,432]{1,0:T(8,128)(2,1)} async-done(((bf16[512,432]{1,0:T(8,128)(2,1)}), bf16[128,432]{1,0:T(8,128)(2,1)}) %reduce-scatter.29.cloned.1.call-update) | async-done | bytes 110608
  1352.3 33.3 %reduce-scatter.27.cloned.1.call-done = bf16[288,576]{1,0:T(8,128)(2,1)} async-done(((bf16[1152,576]{1,0:T(8,128)(2,1)}), bf16[288,576]{1,0:T(8,128)(2,1)}) %reduce-scatter.27.cloned.1.call-update) | async-done | bytes 331792
  1389.5 31.0 %reduce-scatter.31.cloned.1.call-done = bf16[288,576]{1,0:T(8,128)(2,1)} async-done(((bf16[1152,576]{1,0:T(8,128)(2,1)}), bf16[288,576]{1,0:T(8,128)(2,1)}) %reduce-scatter.31.cloned.1.call-update) | async-done | bytes 331792
  1426.0 39.1 %psum.162 = f32[]{:T(128)} all-reduce(f32[]{:T(128)S(6)} %add.699), channel_id=1, replica_groups=mesh['batch'=4,'tm'=8] {'batch','tm'}, use_global_device_ids=true, to_apply=%region_69.70 | all-reduce | flops 1 | bytes 8 | tf_op jit(solution)/shard_map/psum | solution.py:394
  1466.5 3.4 multiply_subtract_fusion.1
  (888 shorter events, 431.1 us)
Async XLA Ops:
  7.2 41.2 %all-gather.7.cloned.1.call-start = ((), (), s32[]{:S(2)}) async-start(), calls=%async_computation.8 | async-start | bytes 1843200 | tf_op jit(solution)/shard_map/all_gather | solution.py:231
  9.1 41.9 %copy-start.159 = (f32[432,128]{1,0:T(8,128)S(1)}, f32[432,128]{1,0:T(8,128)}, u32[]{:S(2)}) copy-start(f32[432,128]{1,0:T(8,128)} %param.28) | copy-start | bytes 663556
  9.2 108.1 %all-gather.13.cloned.1.call-start = ((), (), s32[]{:S(2)}) async-start(), calls=%async_computation.11 | async-start | bytes 1843200 | tf_op jit(solution)/shard_map/all_gather | solution.py:233
  11.1 58.0 %copy-start.157 = (f32[432,128]{1,0:T(8,128)S(1)}, f32[432,128]{1,0:T(8,128)}, u32[]{:S(2)}) copy-start(f32[432,128]{1,0:T(8,128)} %param.26) | copy-start | bytes 663556
  11.2 82.0 %copy-start.194 = (s32[2,4]{1,0:T(2,128)S(1)}, s32[2,4]{1,0:T(2,128)}, u32[]{:S(2)}) copy-start(s32[2,4]{1,0:T(2,128)} %param.24) | copy-start | bytes 100
  11.2 87.3 %copy-start.167 = (f32[2,3328]{1,0:T(2,128)S(1)}, f32[2,3328]{1,0:T(2,128)}, u32[]{:S(2)}) copy-start(f32[2,3328]{1,0:T(2,128)} %param.29) | copy-start | bytes 79876
  11.2 87.9 %copy-start.38 = (bf16[8,1,100,512]{3,0,2,1:T(8,128)(2,1)S(1)}, bf16[8,1,100,512]{3,0,2,1:T(8,128)(2,1)}, u32[]{:S(2)}) copy-start(bf16[8,1,100,512]{3,0,2,1:T(8,128)(2,1)} %param.21) | copy-start | bytes 2457604
  11.2 87.9 %copy-start.96 = (bf16[8,1,49,512]{3,0,2,1:T(8,128)(2,1)S(1)}, bf16[8,1,49,512]{3,0,2,1:T(8,128)(2,1)}, u32[]{:S(2)}) copy-start(bf16[8,1,49,512]{3,0,2,1:T(8,128)(2,1)} %param.20) | copy-start | bytes 1204228
  11.2 147.8 %all-gather.9.cloned.1.call-start = ((), (), s32[]{:S(2)}) async-start(), calls=%async_computation.9 | async-start | bytes 11943936 | tf_op jit(solution)/shard_map/all_gather | solution.py:237
  51.0 207.8 %all-gather.17.cloned.1.call-start = ((), (), s32[]{:S(2)}) async-start(), calls=%async_computation.13 | async-start | bytes 3981312 | tf_op jit(solution)/shard_map/all_gather | solution.py:240
  69.1 220.6 %all-gather.11.cloned.1.call-start = ((), (), s32[]{:S(2)}) async-start(), calls=%async_computation.10 | async-start | bytes 3981312 | tf_op jit(solution)/shard_map/all_gather | solution.py:238
  93.2 329.4 %all-gather.15.cloned.1.call-start = ((), (), s32[]{:S(2)}) async-start(), calls=%async_computation.12 | async-start | bytes 11943936 | tf_op jit(solution)/shard_map/all_gather | solution.py:239
  99.1 171.6 %copy-start.165 = (f32[1152]{0:T(1024)}, f32[1152]{0:T(1024)S(1)}, u32[]{:S(2)}) copy-start(f32[1152]{0:T(1024)S(1)} %get-tuple-element.139) | copy-start | bytes 13828
  99.1 171.6 %copy-start.170 = (f32[1152]{0:T(1024)}, f32[1152]{0:T(1024)S(1)}, u32[]{:S(2)}) copy-start(f32[1152]{0:T(1024)S(1)} %get-tuple-element.138) | copy-start | bytes 13828
  101.0 10.6 copy-start.100
  101.0 10.7 copy-start.99
  101.0 10.9 copy-start.98
  101.0 11.0 copy-start.97
  102.9 10.7 copy-start.43
  103.0 11.9 copy-start.41
  103.0 13.1 copy-start.39
  119.9 1101.1 %reduce-scatter.17.cloned.1.call-start = ((), (), s32[]{:S(2)}) async-start(), calls=%async_computation.14 | async-start | bytes 3981312 | tf_op jit(solution)/shard_map/reduce_scatter | solution.py:185
  159.0 10.9 copy-start.195
  169.9 57.9 %copy-start.12 = (f32[8,49,1152]{2,1,0:T(8,128)}, f32[8,49,1152]{2,1,0:T(8,128)S(1)}, u32[]{:S(2)}) copy-start(f32[8,49,1152]{2,1,0:T(8,128)S(1)} %fusion.14) | copy-start | bytes 5419012
  231.8 9.6 copy-start.21
  233.7 42.8 %collective-permute-start.1 = (bf16[8,1,149,1152]{3,0,2,1:T(8,128)(2,1)}, bf16[8,1,149,1152]{3,0,2,1:T(8,128)(2,1)}, u32[]{:S(2)}, u32[]{:S(2)}) collective-permute-start(bf16[8,1,149,1152]{3,0,2,1:T(8,128)(2,1)} %copy.456), channel_id=1, source_target_pairs={{1,0},{2,1},{3,2},{4,3},{5,4},{6,5},{7,6},{9,8},{10,9},{11,10},{12... | collective-permute-start | bytes 8239112 | tf_op jit(solution)/shard_map/ppermute | solution.py:31
  235.0 46.3 %collective-permute-start = (bf16[8,1,149,1152]{3,0,2,1:T(8,128)(2,1)}, bf16[8,1,149,1152]{3,0,2,1:T(8,128)(2,1)}, u32[]{:S(2)}, u32[]{:S(2)}) collective-permute-start(bf16[8,1,149,1152]{3,0,2,1:T(8,128)(2,1)} %copy.456), channel_id=1, source_target_pairs={{0,1},{1,2},{2,3},{3,4},{4,5},{5,6},{6,7},{8,9},{9,10},{10,11},{11... | collective-permute-start | bytes 8239112 | tf_op jit(solution)/shard_map/ppermute | solution.py:30
  241.7 13.4 copy-start.36
  258.8 144.3 %copy-start.172 = (f32[1,512]{1,0:T(1,128)}, f32[1,512]{1,0:T(1,128)S(1)}, u32[]{:S(2)}) copy-start(f32[1,512]{1,0:T(1,128)S(1)} %get-tuple-element.252) | copy-start | bytes 6148
  258.8 144.3 %copy-start.176 = (f32[1,512]{1,0:T(1,128)}, f32[1,512]{1,0:T(1,128)S(1)}, u32[]{:S(2)}) copy-start(f32[1,512]{1,0:T(1,128)S(1)} %get-tuple-element.253) | copy-start | bytes 6148
  300.8 102.3 %copy-start = (f32[8,1,149,512]{3,2,0,1:T(8,128)}, f32[8,1,149,512]{3,2,0,1:T(8,128)S(1)}, u32[]{:S(2)}) copy-start(f32[8,1,149,512]{3,2,0,1:T(8,128)S(1)} %reshape.1518) | copy-start | bytes 7323652
  403.0 122.2 %copy-start.26 = (f32[149,512]{1,0:T(8,128)}, f32[149,512]{1,0:T(8,128)S(1)}, u32[]{:S(2)}) copy-start(f32[149,512]{1,0:T(8,128)S(1)} %pad_maximum_fusion.12) | copy-start | bytes 915460
  403.1 120.0 %copy-start.28 = (f32[149,512]{1,0:T(8,128)}, f32[149,512]{1,0:T(8,128)S(1)}, u32[]{:S(2)}) copy-start(f32[149,512]{1,0:T(8,128)S(1)} %get-tuple-element.249) | copy-start | bytes 915460
  403.1 124.1 %copy-start.91 = (f32[149,512]{1,0:T(8,128)}, f32[149,512]{1,0:T(8,128)S(1)}, u32[]{:S(2)}) copy-start(f32[149,512]{1,0:T(8,128)S(1)} %get-tuple-element.248) | copy-start | bytes 915460
  410.9 10.5 copy-start.55
  422.6 14.6 copy-start.180
  422.6 14.6 copy-start.196
  442.8 44.2 %copy-start.14 = (f32[8,49,1152]{2,1,0:T(8,128)}, f32[8,49,1152]{2,1,0:T(8,128)S(1)}, u32[]{:S(2)}) copy-start(f32[8,49,1152]{2,1,0:T(8,128)S(1)} %fusion.10) | copy-start | bytes 5419012
  491.6 9.8 copy-start.112
  491.6 10.7 copy-start.110
  493.4 9.8 copy-start.95
  493.4 14.5 copy-start.106
  493.4 61.3 %collective-permute-start.3 = (bf16[8,1,149,1152]{3,0,2,1:T(8,128)(2,1)}, bf16[8,1,149,1152]{3,0,2,1:T(8,128)(2,1)}, u32[]{:S(2)}, u32[]{:S(2)}) collective-permute-start(bf16[8,1,149,1152]{3,0,2,1:T(8,128)(2,1)} %copy.479), channel_id=1, source_target_pairs={{1,0},{2,1},{3,2},{4,3},{5,4},{6,5},{7,6},{9,8},{10,9},{11,10},{12... | collective-permute-start | bytes 8239112 | tf_op jit(solution)/shard_map/ppermute | solution.py:31
  495.0 64.3 %collective-permute-start.2 = (bf16[8,1,149,1152]{3,0,2,1:T(8,128)(2,1)}, bf16[8,1,149,1152]{3,0,2,1:T(8,128)(2,1)}, u32[]{:S(2)}, u32[]{:S(2)}) collective-permute-start(bf16[8,1,149,1152]{3,0,2,1:T(8,128)(2,1)} %copy.479), channel_id=1, source_target_pairs={{0,1},{1,2},{2,3},{3,4},{4,5},{5,6},{6,7},{8,9},{9,10},{10,11},{11... | collective-permute-start | bytes 8239112 | tf_op jit(solution)/shard_map/ppermute | solution.py:30
  578.2 43.6 %copy-start.182 = (f32[1,512]{1,0:T(1,128)S(1)}, f32[1,512]{1,0:T(1,128)}, u32[]{:S(2)}) copy-start(f32[1,512]{1,0:T(1,128)} %get-tuple-element.254) | copy-start | bytes 6148
  578.2 44.4 %copy-start.19 = (bf16[8,1,100,512]{3,2,0,1:T(8,128)(2,1)S(1)}, bf16[8,1,100,512]{3,2,0,1:T(8,128)(2,1)}, u32[]{:S(2)}) copy-start(bf16[8,1,100,512]{3,2,0,1:T(8,128)(2,1)} %copy-done.18) | copy-start | bytes 2457604
  578.2 44.4 %copy-start.189 = (f32[1,512]{1,0:T(1,128)S(1)}, f32[1,512]{1,0:T(1,128)}, u32[]{:S(2)}) copy-start(f32[1,512]{1,0:T(1,128)} %get-tuple-element.255) | copy-start | bytes 6148
  669.7 10.2 copy-start.89
  673.7 56.4 %collective-permute-start.5 = (bf16[8,1,149,512]{3,0,2,1:T(8,128)(2,1)}, bf16[8,1,149,512]{3,0,2,1:T(8,128)(2,1)}, u32[]{:S(2)}, u32[]{:S(2)}) collective-permute-start(bf16[8,1,149,512]{3,0,2,1:T(8,128)(2,1)} %copy.487), channel_id=1, source_target_pairs={{0,1},{1,2},{2,3},{3,4},{4,5},{5,6},{6,7},{8,9},{9,10},{10,11},{11... | collective-permute-start | bytes 3661832 | tf_op jit(solution)/shard_map/ppermute | solution.py:30
  676.1 55.9 %collective-permute-start.4 = (bf16[8,1,149,512]{3,0,2,1:T(8,128)(2,1)}, bf16[8,1,149,512]{3,0,2,1:T(8,128)(2,1)}, u32[]{:S(2)}, u32[]{:S(2)}) collective-permute-start(bf16[8,1,149,512]{3,0,2,1:T(8,128)(2,1)} %copy.487), channel_id=1, source_target_pairs={{1,0},{2,1},{3,2},{4,3},{5,4},{6,5},{7,6},{9,8},{10,9},{11,10},{12... | collective-permute-start | bytes 3661832 | tf_op jit(solution)/shard_map/ppermute | solution.py:31
  699.4 18.4 %copy-start.24 = (bf16[8,1,149,1152]{3,2,0,1:T(8,128)(2,1)S(1)}, bf16[8,1,149,1152]{3,2,0,1:T(8,128)(2,1)}, u32[]{:S(2)}) copy-start(bf16[8,1,149,1152]{3,2,0,1:T(8,128)(2,1)} %copy-done.23) | copy-start | bytes 8239108
  730.1 493.0 %reduce-scatter.21.cloned.1.call-start = ((), (), s32[]{:S(2)}) async-start(), calls=%async_computation.16 | async-start | bytes 3981312 | tf_op jit(solution)/shard_map/reduce_scatter | solution.py:185
  950.4 299.5 %reduce-scatter.19.cloned.1.call-start = ((), (), s32[]{:S(2)}) async-start(), calls=%async_computation.15 | async-start | bytes 11943936 | tf_op jit(solution)/shard_map/reduce_scatter | solution.py:185
  1032.4 270.9 %reduce-scatter.23.cloned.1.call-start = ((), (), s32[]{:S(2)}) async-start(), calls=%async_computation.17 | async-start | bytes 11943936 | tf_op jit(solution)/shard_map/reduce_scatter | solution.py:185
  1074.1 42.3 %collective-permute-start.7 = (bf16[8,1,149,512]{3,0,2,1:T(8,128)(2,1)}, bf16[8,1,149,512]{3,0,2,1:T(8,128)(2,1)}, u32[]{:S(2)}, u32[]{:S(2)}) collective-permute-start(bf16[8,1,149,512]{3,0,2,1:T(8,128)(2,1)} %copy.499), channel_id=1, source_target_pairs={{0,1},{1,2},{2,3},{3,4},{4,5},{5,6},{6,7},{8,9},{9,10},{10,11},{11... | collective-permute-start | bytes 3661832 | tf_op jit(solution)/shard_map/ppermute | solution.py:30
  1076.6 41.6 %collective-permute-start.6 = (bf16[8,1,149,512]{3,0,2,1:T(8,128)(2,1)}, bf16[8,1,149,512]{3,0,2,1:T(8,128)(2,1)}, u32[]{:S(2)}, u32[]{:S(2)}) collective-permute-start(bf16[8,1,149,512]{3,0,2,1:T(8,128)(2,1)} %copy.499), channel_id=1, source_target_pairs={{1,0},{2,1},{3,2},{4,3},{5,4},{6,5},{7,6},{9,8},{10,9},{11,10},{12... | collective-permute-start | bytes 3661832 | tf_op jit(solution)/shard_map/ppermute | solution.py:31
  1220.9 109.2 %reduce-scatter.25.cloned.1.call-start = ((), (), s32[]{:S(2)}) async-start(), calls=%async_computation.18 | async-start | bytes 655360
  1223.0 127.6 %reduce-scatter.29.cloned.1.call-start = ((), (), s32[]{:S(2)}) async-start(), calls=%async_computation.20 | async-start | bytes 655360
  1225.1 160.4 %reduce-scatter.27.cloned.1.call-start = ((), (), s32[]{:S(2)}) async-start(), calls=%async_computation.19 | async-start | bytes 1843200
  1252.6 167.9 %reduce-scatter.31.cloned.1.call-start = ((), (), s32[]{:S(2)}) async-start(), calls=%async_computation.21 | async-start | bytes 1843200
  1274.0 31.9 %copy-start.156 = (bf16[8,1,49,1152]{3,0,2,1:T(8,128)(2,1)S(1)}, bf16[8,1,49,1152]{3,0,2,1:T(8,128)(2,1)}, u32[]{:S(2)}) copy-start(bf16[8,1,49,1152]{3,0,2,1:T(8,128)(2,1)} %copy.505) | copy-start | bytes 2709508
  1331.1 54.4 %copy-start.152 = (bf16[432,128]{1,0:T(8,128)(2,1)}, bf16[432,128]{1,0:T(8,128)(2,1)S(1)}, u32[]{:S(2)}) copy-start(bf16[432,128]{1,0:T(8,128)(2,1)S(1)} %copy.578) | copy-start | bytes 331780
  1351.6 33.9 %copy-start.154 = (bf16[432,128]{1,0:T(8,128)(2,1)}, bf16[432,128]{1,0:T(8,128)(2,1)S(1)}, u32[]{:S(2)}) copy-start(bf16[432,128]{1,0:T(8,128)(2,1)S(1)} %copy.582) | copy-start | bytes 331780
  1352.3 114.2 %copy-start.120 = (f32[576,288]{1,0:T(8,128)S(1)}, f32[576,288]{1,0:T(8,128)}, u32[]{:S(2)}) copy-start(f32[576,288]{1,0:T(8,128)} %copy.556) | copy-start | bytes 1990660
  (158 other events, 656.6 us)
Sparse Core Ops, SparseCore 0:
  10.2 38.1 all-gather.6
  50.5 43.6 all-gather.12
  96.7 62.2 all-gather.8
  160.8 34.1 all-gather.16
  196.7 35.0 all-gather.10
  234.1 105.6 all-gather.14
  730.2 51.6 reduce-scatter.16
  950.6 48.3 reduce-scatter.20
  1032.5 99.4 reduce-scatter.18
  1221.0 82.3 reduce-scatter.22
  1306.2 21.6 reduce-scatter.24
  1330.6 19.9 reduce-scatter.28
  1353.4 32.0 reduce-scatter.26
  1387.8 32.6 reduce-scatter.30
where the time goes:
time: 1510 us; the launch traced here: 1500 us
  blocking collectives  469 us (31%)
  local copies, waits for them, and re-layouts  418 us (28%)
  matrix products  227 us (15%)
  waiting for transfers between devices  189 us (13%)
  other arithmetic  149 us (10%)
  between operations  24.1 us (2%)
  starting transfers between devices  21.2 us (1%)
    psum x4, blocking collectives, norm_forward_pass(): lax.psum((running_sums, squared_values), ('batch', 'tm'))  220 us
    psum x4, blocking collectives, norm_reverse_pass(): lax.psum((running_sums, cross_product), ('batch', 'tm'))  168 us
    unnamed x490, local copies, waits for them, and re-layouts  121 us
    dot_general x6, matrix products, reduce_weight(): lax.dot_general(left, right, (((0,), (0,)), ((), ())), preferred_element_...  85.5 us
    unnamed x18, waiting for transfers between devices  83.2 us
    concatenate x44, local copies, waits for them, and re-layouts, spatial_taps(): jnp.concatenate(pieces, axis=-1)  59.9 us
    dot_general x4, matrix products, spatial_backward(): lax.dot_general(upstream_rows, weight, (((1,), (1,)), ((), ())), preferre...  56 us
    slice x36, local copies, waits for them, and re-layouts, spatial_taps(): padded[:, :, row:row + side, column:column + side, :]  53.3 us
  transfers between devices with their start and end apart: 22, of which 6 were waited for; matrix products, arithmetic and copies ran while one was open for 45% of the time, Pallas kernels for 0%

commit v1 on v0

--- a/solution.py
+++ b/solution.py
@@ -1,6 +1,11 @@
+import functools
+import math
+
 import jax
 import jax.numpy as jnp
 from jax import lax
+from jax.experimental import pallas as pl
+from jax.experimental.pallas import tpu as pltpu
 from jax.sharding import PartitionSpec as P
 
 D = 512
@@ -201,7 +206,7 @@
     return (new_weight, new_momentum, new_variance)
 
 
-def body(
+def plain_body(
     x_small,
     x_large,
     small_output_gradient,
@@ -459,9 +464,729 @@
     )
 
 
+BF = jnp.bfloat16
+F32 = jnp.float32
+MESH_ID = pl.DeviceIdType.MESH
+NT_DIMS = (((1,), (1,)), ((), ()))
+NN_DIMS = (((1,), (0,)), ((), ()))
+UP, DOWN, ACROSS, ALONG, TWIN = range(5)
+
+
+class Place:
+    def __init__(self, batches, slots):
+        self.batches, self.slots = batches, slots
+        self.z = lax.axis_index("batch")
+        self.t = lax.axis_index("tm")
+        self.core = lax.rem(self.t, 2)
+        self.slab = self.t // 2
+        self.slabs = slots // 2
+        side = lax.rem(self.slab, 2)
+        deep = self.slab // 2
+        self.side_slab = deep * 2 + (1 - side)
+        self.deep_slab = (1 - deep) * 2 + side
+        self.far_slab = (1 - deep) * 2 + (1 - side)
+        self.rel = (self.slab, self.side_slab, self.deep_slab, self.far_slab)
+        self.twin = self.t + 1 - 2 * self.core
+
+    def device(self, way):
+        if way == UP:
+            return (self.z + 1, self.t)
+        if way == DOWN:
+            return (self.z - 1, self.t)
+        if way == ACROSS:
+            return (self.z, self.side_slab * 2 + self.core)
+        if way == ALONG:
+            return (self.z, self.deep_slab * 2 + self.core)
+        return (self.z, self.twin)
+
+    def greet(self):
+        barrier = pltpu.get_barrier_semaphore()
+        for step in range(1, self.slots):
+            pl.semaphore_signal(
+                barrier, inc=1, device_id=(self.z, lax.rem(self.t + step, self.slots)),
+                device_id_type=MESH_ID,
+            )
+        for step in range(1, self.batches):
+            pl.semaphore_signal(
+                barrier, inc=1, device_id=(lax.rem(self.z + step, self.batches), self.t),
+                device_id_type=MESH_ID,
+            )
+        pl.semaphore_wait(barrier, self.slots + self.batches - 2)
+
+
+def send(src, dst, send_sem, recv_sem, device):
+    return pltpu.make_async_remote_copy(
+        src_ref=src, dst_ref=dst, send_sem=send_sem, recv_sem=recv_sem,
+        device_id=device, device_id_type=MESH_ID,
+    )
+
+
+class Totals:
+    def __init__(self, place, rows, planes, lines, sems):
+        self.place, self.rows, self.planes, self.lines = place, rows, planes, lines
+        self.plane_send, self.plane_recv, self.line_send, self.line_recv = sems
+
+    def run(self, n, value):
+        p = self.place
+        width = value.shape[1]
+        plane, line = self.planes.at[n], self.lines.at[n]
+        plane[p.t, :, :width] = value
+
+        def plane_copy(step):
+            to = lax.rem(p.t + step, p.slots)
+            ref = plane.at[p.t, :, pl.ds(0, width)]
+            return send(ref, ref, self.plane_send.at[n, step], self.plane_recv.at[n, p.t], (p.z, to))
+
+        def plane_wait(step):
+            origin = lax.rem(p.t + p.slots - step, p.slots)
+            ref = plane.at[origin, :, pl.ds(0, width)]
+            send(ref, ref, self.plane_send.at[n, step], self.plane_recv.at[n, origin], (p.z, p.twin)).wait_recv()
+
+        for step in range(1, p.slots):
+            plane_copy(step).start()
+        for step in range(1, p.slots):
+            plane_wait(step)
+        total = plane[0, :, :width]
+        for slot in range(1, p.slots):
+            total = total + plane[slot, :, :width]
+        line[p.z, :, :width] = total
+
+        def line_copy(step):
+            to = lax.rem(p.z + step, p.batches)
+            ref = line.at[p.z, :, pl.ds(0, width)]
+            return send(ref, ref, self.line_send.at[n, step], self.line_recv.at[n, p.z], (to, p.t))
+
+        def line_wait(step):
+            origin = lax.rem(p.z + p.batches - step, p.batches)
+            ref = line.at[origin, :, pl.ds(0, width)]
+            send(ref, ref, self.line_send.at[n, step], self.line_recv.at[n, origin], (p.z, p.twin)).wait_recv()
+
+        for step in range(1, p.batches):
+            line_copy(step).start()
+        for step in range(1, p.batches):
+            line_wait(step)
+        total = line[0, :, :width]
+        for slot in range(1, p.batches):
+            total = total + line[slot, :, :width]
+        for step in range(1, p.slots):
+            plane_copy(step).wait_send()
+        for step in range(1, p.batches):
+            line_copy(step).wait_send()
+        return total
+
+
+class Gather:
+    def __init__(self, place, index, own, whole, block, sems):
+        self.p, self.n, self.own, self.whole, self.block = place, index, own, whole, block
+        self.send_sem, self.recv_sem, self.twin_sem = sems
+
+    def copy(self, way, rel, batch, src=None):
+        p = self.p
+        core = p.core
+        dst = self.whole.at[self.block(p.rel[rel], core, batch)]
+        there = {ACROSS: {0: 1, 2: 3}, ALONG: {0: 2, 1: 3}}.get(way, {}).get(rel, rel)
+        sem = self.twin_sem if way == TWIN else self.recv_sem
+        return send(
+            dst if src is None else src, dst, self.send_sem.at[self.n, way, rel, batch],
+            sem.at[self.n, there, batch], p.device(way),
+        )
+
+    def wait(self, rel, batch, twin=False):
+        p = self.p
+        core = 1 - p.core if twin else p.core
+        ref = self.whole.at[self.block(p.rel[rel], core, batch)]
+        sem = self.twin_sem if twin else self.recv_sem
+        send(ref, ref, self.send_sem.at[self.n, TWIN, rel, batch], sem.at[self.n, rel, batch],
+             p.device(TWIN)).wait_recv()
+
+    def at(self, k, fn):
+        p = self.p
+        if k == 0:
+            fn(p.z)
+            return
+        pl.when(p.z - k >= 0)(lambda: fn(p.z - k))
+        pl.when(p.z + k < p.batches)(lambda: fn(p.z + k))
+
+    def start(self):
+        p = self.p
+        pl.when(p.z < p.batches - 1)(lambda: self.copy(UP, 0, p.z, self.own).start())
+        pl.when(p.z > 0)(lambda: self.copy(DOWN, 0, p.z, self.own).start())
+        for way in (ACROSS, ALONG, TWIN):
+            self.copy(way, 0, p.z, self.own).start()
+
+    def hop(self, k):
+        p = self.p
+
+        def below(b):
+            self.wait(0, b)
+            pl.when(p.z < p.batches - 1)(lambda: self.copy(UP, 0, b).start())
+            for way in (ACROSS, ALONG, TWIN):
+                self.copy(way, 0, b).start()
+
+        def above(b):
+            self.wait(0, b)
+            pl.when(p.z > 0)(lambda: self.copy(DOWN, 0, b).start())
+            for way in (ACROSS, ALONG, TWIN):
+                self.copy(way, 0, b).start()
+
+        pl.when(p.z - k >= 0)(lambda: below(p.z - k))
+        pl.when(p.z + k < p.batches)(lambda: above(p.z + k))
+
+    def plane(self, k):
+        half = self.p.batches // 2
+
+        def one(b):
+            self.wait(1, b)
+            pl.when(b < half)(lambda: self.copy(ALONG, 1, b).start())
+            self.copy(TWIN, 1, b).start()
+            self.wait(2, b)
+            pl.when(b >= half)(lambda: self.copy(ACROSS, 2, b).start())
+            self.copy(TWIN, 2, b).start()
+
+        self.at(k, one)
+
+    def far(self, k):
+        def one(b):
+            self.wait(3, b)
+            self.copy(TWIN, 3, b).start()
+
+        self.at(k, one)
+
+    def twins(self, rel):
+        def body(b, _):
+            self.wait(rel, b, twin=True)
+            return 0
+
+        lax.fori_loop(0, self.p.batches, body, 0)
+
+    def steps(self):
+        batches = self.p.batches
+        order = [self.start]
+        for k in range(batches):
+            if k:
+                order.append(functools.partial(self.hop, k))
+                order.append(functools.partial(self.far, k - 1))
+            order.append(functools.partial(self.plane, k))
+        order.append(functools.partial(self.far, batches - 1))
+        return order
+
+    def finish(self):
+        p = self.p
+        half = p.batches // 2
+
+        def body(b, _):
+            pl.when((b <= p.z) & (p.z < p.batches - 1))(lambda: self.copy(UP, 0, b, self.own).wait_send())
+            pl.when((b >= p.z) & (p.z > 0))(lambda: self.copy(DOWN, 0, b, self.own).wait_send())
+            for way in (ACROSS, ALONG):
+                self.copy(way, 0, b, self.own).wait_send()
+            for rel in range(4):
+                self.copy(TWIN, rel, b, self.own).wait_send()
+            pl.when(b < half)(lambda: self.copy(ALONG, 1, b, self.own).wait_send())
+            pl.when(b >= half)(lambda: self.copy(ACROSS, 2, b, self.own).wait_send())
+            return 0
+
+        lax.fori_loop(0, p.batches, body, 0)
+
+
+def sigmoid(v):
+    return 0.5 * jnp.tanh(0.5 * v) + 0.5
+
+
+class Shape:
+    def __init__(self, x_small, x_large, batches, slots):
+        self.clips = x_small[0]
+        self.cells = (x_small[2], x_large[2])
+        self.sides = (math.isqrt(x_small[2]), math.isqrt(x_large[2]))
+        self.d = x_small[3]
+        self.padded = tuple(n + n % 2 for n in self.cells)
+        self.rows = tuple(n * self.clips for n in self.padded)
+        self.m = sum(self.rows)
+        self.mid = MID
+        self.k = 9 * self.d
+        self.batches, self.slots = batches, slots
+        self.slabs = slots // 2
+        self.kw = self.k // self.slabs
+        self.nb = self.mid // (2 * batches)
+        self.ur = 3 * self.mid // slots
+        self.uc = self.d // batches
+
+
+def fits(x_small, x_large, batches, slots):
+    s = Shape(x_small, x_large, batches, slots)
+    return (
+        s.clips == 8 and x_small[1] == 1 and slots == 8 and batches >= 2 and batches % 2 == 0
+        and all(side * side == cells for side, cells in zip(s.sides, s.cells))
+        and all(r % 80 == 0 for r in s.rows)
+        and s.kw % 128 == 0 and s.mid % (32 * batches) == 0 and s.ur % 16 == 0 and s.uc % 128 == 0
+    )
+
+
+def chunks(s, size, fn, carry=None, unroll=1):
+    out = []
+    base = 0
+    for group, rows in enumerate(s.rows):
+        def body(i, c, group=group, base=base):
+            return fn(group, pl.multiple_of(base + i * size, size if base % size == 0 else 16), c)
+
+        out.append(lax.fori_loop(0, rows // size, body, carry if carry is not None else 0, unroll=unroll))
+        base += rows
+    return out
+
+
+def sums_of(s, load, live, width):
+    def body(group, r0, c):
+        values = load(group, r0, 80)
+        return tuple(t + jnp.sum(v.reshape(10, 8, width), axis=0) for t, v in zip(c, values))
+
+    zero = jnp.zeros((8, width), F32)
+    small, large = chunks(s, 80, body, (zero, zero))
+    rows = [jnp.sum(v * live[g], axis=0, keepdims=True) for v, g in
+            ((small[0], 0), (large[0], 1), (small[1], 0), (large[1], 1))]
+    return jnp.concatenate(rows, axis=0)
+
+
+def build_taps(s, grids, taps):
+    pieces = []
+    for tap in range(9):
+        lo = tap * s.d
+        end = lo + s.d
+        while lo < end:
+            hi = min(end, (lo // s.kw + 1) * s.kw)
+            pieces.append((tap, lo - tap * s.d, lo // s.kw, lo % s.kw, hi - lo))
+            lo = hi
+    base = 0
+    for group in range(2):
+        side, cells = s.sides[group], s.cells[group]
+        grid = grids[group]
+        for tap, channel, slab, lane, width in pieces:
+            i, j = tap // 3, tap % 3
+            if side % 2 == 0:
+                n = 2 * side * 8
+
+                def body(r, _):
+                    window = grid[pl.ds(i + 2 * r, 2), j : j + side, :, channel : channel + width]
+                    taps[slab, pl.ds(pl.multiple_of(base + r * n, 16), n), lane : lane + width] = (
+                        window.reshape(n, width).astype(BF)
+                    )
+                    return 0
+
+                lax.fori_loop(0, side // 2, body, 0)
+            else:
+                window = grid[i : i + side, j : j + side, :, channel : channel + width]
+                window = window.reshape(cells * 8, width)
+                window = jnp.concatenate(
+                    [window, jnp.zeros((s.rows[group] - cells * 8, width), F32)], axis=0
+                ) if s.rows[group] > cells * 8 else window
+                taps[slab, base : base + s.rows[group], lane : lane + width] = window.astype(BF)
+        base += s.rows[group]
+
+
+def fill_grid(s, grids, group, cell, value):
+    side = s.sides[group]
+    grids[group][1 + cell // side, 1 + lax.rem(cell, side)] = value
+
+
+def zero_padding(s, ref, width):
+    base = 0
+    for group in range(2):
+        base += s.rows[group]
+        spare = (s.padded[group] - s.cells[group]) * s.clips
+        if spare:
+            size = -(-spare // 16) * 16
+            keep = lax.broadcasted_iota(jnp.int32, (size, width), 0) < size - spare
+            value = ref[base - size : base, :].astype(F32)
+            ref[base - size : base, :] = jnp.where(keep, value, 0.0).astype(ref.dtype)
+
+
+def grid_of_rows(s, grids, group, r0, value):
+    side = s.sides[group]
+    base = 0 if group == 0 else s.rows[0]
+    first = (r0 - base) // 8
+    split = value.reshape(10, 8, s.d)
+    for n in range(10):
+        cell = first + n
+        grids[group][1 + cell // side, 1 + lax.rem(cell, side)] = split[n]
+
+
+def clear_pad_cells(s, grids):
+    for group in range(2):
+        side = s.sides[group]
+        for cell in range(s.cells[group], s.padded[group]):
+            grids[group][1 + cell // side, 1 + cell % side] = jnp.zeros((8, s.d), F32)
+
+
+def moments(total, inverse, width):
+    mean = [total[g : g + 1, :] * inverse[g] for g in range(2)]
+    scale = [
+        lax.rsqrt(total[2 + g : 3 + g, :] * inverse[g] - mean[g] * mean[g] + NORM_EPS) for g in range(2)
+    ]
+    return mean, scale
+
+
+def wide_cuts(width):
+    half = -(-width // 256) * 128
+    return ((0, half), (half, width - half))
+
+
+def forward_kernel(s, *refs):
+    (x, grad, sw1, uw1, sw2, uw2, norm, live_ref, inverse,
+     gs1, gu1, gs2, gu2, taps1_o, taps2_o, xh1_o, xh2_o, xh3_o, xh4_o, z1_o, z3_o, out, dpre,
+     r1_o, r2_o, r3_o, r4_o, last_o,
+     tb1, tb2, own1, own2, wb, wub, taps, a, z, grid_s, grid_l, b, hs, hr, planes, lines,
+     ag_send, ag_recv, ag_twin, tb_send, tb_recv, local, load, hs_send, hs_recv,
+     pl_send, pl_recv, ln_send, ln_recv) = refs
+    p = Place(s.batches, s.slots)
+    live = [live_ref[g] for g in range(2)]
+    inv = [inverse[g] for g in range(2)]
+    totals = Totals(p, 4, planes, lines, (pl_send, pl_recv, ln_send, ln_recv))
+    d, mid = s.d, s.mid
+    bounds = (0, mid, mid + d, 2 * mid + d, 2 * mid + 2 * d)
+
+    def gain_bias(n):
+        return norm[0:1, bounds[n] : bounds[n + 1]], norm[1:2, bounds[n] : bounds[n + 1]]
+
+    p.greet()
+
+    def twin_copy(n, src, dst):
+        return send(
+            src.at[1 - p.core], dst.at[pl.ds(pl.multiple_of(p.core * (s.kw // 2), 16), s.kw // 2)],
+            tb_send.at[n], tb_recv.at[n], p.device(TWIN),
+        )
+
+    def twin_wait(n, src, dst):
+        send(
+            src.at[1 - p.core], dst.at[pl.ds(pl.multiple_of((1 - p.core) * (s.kw // 2), 16), s.kw // 2)],
+            tb_send.at[n], tb_recv.at[n], p.device(TWIN),
+        ).wait_recv()
+
+    for n, src, dst in ((0, sw1, tb1), (1, sw2, tb2)):
+        twin_copy(n, src, dst).start()
+        dst[pl.ds(pl.multiple_of(p.core * (s.kw // 2), 16), s.kw // 2)] = src[p.core]
+
+    def s_block(slab, core, batch):
+        return (slab, pl.ds(pl.multiple_of((batch * 2 + core) * s.nb, 16), s.nb))
+
+    def u_block(slab, core, batch):
+        return (pl.ds(pl.multiple_of((slab * 2 + core) * s.ur, 16), s.ur),
+                pl.ds(pl.multiple_of(batch * s.uc, 128), s.uc))
+
+    sems = (ag_send, ag_recv, ag_twin)
+    gather = [
+        Gather(p, 0, own1, gs1, s_block, sems),
+        Gather(p, 1, uw1, gu1, u_block, sems),
+        Gather(p, 2, own2, gs2, s_block, sems),
+        Gather(p, 3, uw2, gu2, u_block, sems),
+    ]
+
+    def keep_own(n):
+        g = gather[n]
+        return pltpu.make_async_copy(g.own, g.whole.at[g.block(p.slab, p.core, p.z)], local.at[n])
+
+    twin_wait(0, sw1, tb1)
+    own1[...] = tb1[...].T
+    queue = [(0, step) for step in gather[0].steps()]
+    queue.pop(0)[1]()
+    keep_own(0).start()
+    twin_wait(1, sw2, tb2)
+    own2[...] = tb2[...].T
+    keep_own(1).start()
+    keep_own(2).start()
+    keep_own(3).start()
+    for n in (1, 2, 3):
+        queue += [(n, step) for step in gather[n].steps()]
+
+    def tick(count):
+        for _ in range(count):
+            if queue:
+                queue.pop(0)[1]()
+
+    def flush(n):
+        while queue and queue[0][0] <= n:
+            queue.pop(0)[1]()
+
+    for side, edge in ((0, 0), (1, p.slots - 1)):
+        @pl.when(p.t == edge)
+        def _(side=side):
+            hr[side] = jnp.zeros(hr.shape[1:], BF)
+
+    grids = (grid_s, grid_l)
+    for grid in grids:
+        def clear(i, _, grid=grid):
+            grid[i] = jnp.zeros(grid.shape[1:], F32)
+            return 0
+
+        lax.fori_loop(0, grid.shape[0], clear, 0)
+
+    def x_rows(group, r0, c):
+        grid_of_rows(s, grids, group, r0, x[pl.ds(r0, 80), :].astype(F32))
+        return c
+
+    chunks(s, 80, x_rows)
+    clear_pad_cells(s, grids)
+    build_taps(s, grids, taps)
+    taps_copy = pltpu.make_async_copy(taps, taps1_o, local.at[4])
+    taps_copy.start()
+
+    def slab_load(whole, rel):
+        return pltpu.make_async_copy(whole.at[p.rel[rel]], wb.at[rel], load.at[rel])
+
+    def conv_slab(rel):
+        for lo, width in wide_cuts(mid):
+            y = lax.dot_general(taps[p.rel[rel]], wb[rel, lo : lo + width, :], NT_DIMS, preferred_element_type=F32)
+            if rel == 0:
+                a[:, lo : lo + width] = y
+            else:
+                a[:, lo : lo + width] += y
+
+    def spatial(n, whole, spare):
+        g = gather[n]
+        while queue and queue[0][0] <= n and len([q for q in queue if q[0] <= n]) > 1:
+            queue.pop(0)[1]()
+        g.twins(0)
+        if n == 0:
+            keep_own(0).wait()
+        else:
+            keep_own(2).wait()
+        slab_load(whole, 0).start()
+        g.twins(1)
+        slab_load(whole, 1).start()
+        g.twins(2)
+        slab_load(whole, 2).start()
+        slab_load(whole, 0).wait()
+        conv_slab(0)
+        flush(n)
+        g.twins(3)
+        slab_load(whole, 3).start()
+        for rel in (1, 2, 3):
+            tick(spare)
+            slab_load(whole, rel).wait()
+            conv_slab(rel)
+
+    def stats(load_rows, width):
+        return sums_of(s, load_rows, live, width)
+
+    def wide_norm(index, n, zo, xo, ro, sem):
+        def load_rows(group, r0, size):
+            v = a[pl.ds(r0, size), :]
+            return v, v * v
+
+        total = totals.run(index, stats(load_rows, mid))
+        mean, scale = moments(total, inv, mid)
+        ro[...] = jnp.concatenate(scale, axis=0)
+        gain, bias = gain_bias(n)
+
+        def rows(group, r0, c):
+            xhat = (a[pl.ds(r0, 16), :] - mean[group]) * scale[group]
+            a[pl.ds(r0, 16), :] = xhat
+            h = xhat * gain + bias
+            z[pl.ds(r0, 16), :] = (h * sigmoid(h)).astype(BF)
+            return c
+
+        chunks(s, 16, rows)
+        zero_padding(s, z, mid)
+        xc = pltpu.make_async_copy(a, xo, local.at[sem])
+        zc = pltpu.make_async_copy(z, zo, local.at[sem + 1])
+        xc.start()
+        zc.start()
+        return xc, zc
+
+    def u_load(n, whole):
+        return pltpu.make_async_copy(whole, wub, load.at[4 + n])
+
+    def halo(n, side):
+        to = p.t + 1 if side == 0 else p.t - 1
+        return send(hs.at[side], hr.at[side], hs_send.at[n, side], hs_recv.at[n, side], (p.z, to))
+
+    def temporal(n, index, between):
+        flush(index)
+        for rel in range(4):
+            gather[index].twins(rel)
+        keep_own(index).wait()
+        load_w = u_load(n, gather[index].whole)
+        load_w.start()
+        load_w.wait()
+        hs[0] = jnp.dot(z[...], wub[:mid, :], preferred_element_type=F32).astype(BF)
+        pl.when(p.t < p.slots - 1)(lambda: halo(n, 0).start())
+        hs[1] = jnp.dot(z[...], wub[2 * mid :, :], preferred_element_type=F32).astype(BF)
+        pl.when(p.t > 0)(lambda: halo(n, 1).start())
+        b[...] = jnp.dot(z[...], wub[mid : 2 * mid, :], preferred_element_type=F32)
+        between()
+        pl.when(p.t > 0)(lambda: halo(n, 0).wait_recv())
+        pl.when(p.t < p.slots - 1)(lambda: halo(n, 1).wait_recv())
+
+    def narrow_total(index):
+        def load_rows(group, r0, size):
+            v = b[pl.ds(r0, size), :] + hr[0, pl.ds(r0, size), :].astype(F32) + hr[1, pl.ds(r0, size), :].astype(F32)
+            b[pl.ds(r0, size), :] = v
+            return v, v * v
+
+        return totals.run(index, stats(load_rows, d))
+
+    def halo_done(n):
+        pl.when(p.t < p.slots - 1)(lambda: halo(n, 0).wait_send())
+        pl.when(p.t > 0)(lambda: halo(n, 1).wait_send())
+
+    spatial(0, gs1, 4)
+    tick(1)
+    xc1, zc1 = wide_norm(0, 0, z1_o, xh1_o, r1_o, 5)
+    tick(2)
+    temporal(0, 1, lambda: tick(2))
+    total = narrow_total(1)
+    tick(1)
+    mean2, scale2 = moments(total, inv, d)
+    r2_o[...] = jnp.concatenate(scale2, axis=0)
+    gain2, bias2 = gain_bias(1)
+
+    def second(group, r0, c):
+        xhat = (b[pl.ds(r0, 80), :] - mean2[group]) * scale2[group]
+        b[pl.ds(r0, 80), :] = xhat
+        h = xhat * gain2 + bias2
+        grid_of_rows(s, grids, group, r0, (h * sigmoid(h)).astype(BF).astype(F32))
+        return c
+
+    chunks(s, 80, second)
+    clear_pad_cells(s, grids)
+    xc2 = pltpu.make_async_copy(b, xh2_o, local.at[7])
+    xc2.start()
+    halo_done(0)
+    tick(2)
+    taps_copy.wait()
+    build_taps(s, grids, taps)
+    taps_copy2 = pltpu.make_async_copy(taps, taps2_o, local.at[8])
+    taps_copy2.start()
+    xc1.wait()
+    spatial(2, gs2, 4)
+    tick(2)
+    zc1.wait()
+    xc3, zc3 = wide_norm(2, 2, z3_o, xh3_o, r3_o, 9)
+    tick(2)
+    xc2.wait()
+    temporal(1, 3, lambda: None)
+    total = narrow_total(3)
+    mean4, scale4 = moments(total, inv, d)
+    r4_o[...] = jnp.concatenate(scale4, axis=0)
+    gain4, bias4 = gain_bias(3)
+
+    def last(group, r0, c):
+        xhat = (b[pl.ds(r0, 80), :] - mean4[group]) * scale4[group]
+        b[pl.ds(r0, 80), :] = xhat
+        pre = xhat * gain4 + bias4 + x[pl.ds(r0, 80), :].astype(F32)
+        gate = sigmoid(pre)
+        alive = jnp.broadcast_to(live[group][None], (10, 8, d)).reshape(80, d)
+        out[pl.ds(r0, 80), :] = alive * (pre * gate)
+        up = alive * grad[pl.ds(r0, 80), :].astype(F32) * (gate * (1.0 + pre * (1.0 - gate)))
+        dpre[pl.ds(r0, 80), :] = up
+        return c
+
+    chunks(s, 80, last)
+    zero_padding(s, dpre, d)
+    xc4 = pltpu.make_async_copy(b, xh4_o, local.at[11])
+    xc4.start()
+
+    def last_rows(group, r0, size):
+        v = dpre[pl.ds(r0, size), :]
+        return v, v * b[pl.ds(r0, size), :]
+
+    last_o[...] = totals.run(4, stats(last_rows, d))
+    halo_done(1)
+    for g in gather:
+        g.finish()
+    for n, src, dst in ((0, sw1, tb1), (1, sw2, tb2)):
+        twin_copy(n, src, dst).wait_send()
+    for c in (taps_copy2, zc3, xc3, xc4):
+        c.wait()
+
+
+def forward_call(s, x, grad, sw1, uw1, sw2, uw2, norm, live, inverse):
+    any_, vmem, smem = (pl.BlockSpec(memory_space=m) for m in (pl.ANY, pltpu.VMEM, pltpu.SMEM))
+    S = jax.ShapeDtypeStruct
+    m, d, mid = s.m, s.d, s.mid
+    gs = S((s.slabs, mid, s.kw), BF)
+    gu = S((3 * mid, d), BF)
+    taps = S((s.slabs, m, s.kw), BF)
+    wide, narrow = S((m, mid), F32), S((m, d), F32)
+    zs = S((m, mid), BF)
+    outs = (gs, gu, gs, gu, taps, taps, wide, narrow, wide, narrow, zs, zs, narrow, narrow,
+            S((2, mid), F32), S((2, d), F32), S((2, mid), F32), S((2, d), F32), S((4, d), F32))
+    specs = (any_,) * 12 + (vmem,) * 7
+    dma, V = pltpu.SemaphoreType.DMA, pltpu.VMEM
+    nb = s.batches
+    n_sums = 5
+    scratch = [
+        V((s.kw, s.nb), BF), V((s.kw, s.nb), BF), V((s.nb, s.kw), BF), V((s.nb, s.kw), BF),
+        V((s.slabs, mid, s.kw), BF), V((3 * mid, d), BF), V((s.slabs, m, s.kw), BF),
+        V((m, mid), F32), V((m, mid), BF),
+        V((s.sides[0] + 2, s.sides[0] + 2, 8, d), F32), V((s.sides[1] + 2, s.sides[1] + 2, 8, d), F32),
+        V((m, d), F32), V((2, m, d), BF), V((2, m, d), BF),
+        V((n_sums, s.slots, 4, mid), F32), V((n_sums, nb, 4, mid), F32),
+        dma((4, 5, 4, nb)), dma((4, 4, nb)), dma((4, 4, nb)), dma((2,)), dma((2,)), dma((12,)), dma((6,)),
+        dma((2, 2)), dma((2, 2)),
+        dma((n_sums, s.slots)), dma((n_sums, s.slots)), dma((n_sums, nb)), dma((n_sums, nb)),
+    ]
+    return pl.pallas_call(
+        functools.partial(forward_kernel, s),
+        out_shape=outs,
+        in_specs=[vmem, vmem, vmem, any_, vmem, any_, vmem, vmem, smem],
+        out_specs=specs,
+        scratch_shapes=scratch,
+        compiler_params=pltpu.CompilerParams(
+            collective_id=0, has_side_effects=True, vmem_limit_bytes=63 * 2**20
+        ),
+        name="forward",
+    )(x, grad, sw1, uw1, sw2, uw2, norm, live, inverse)
+
+
+def cell_major(s, small, large):
+    parts = []
+    for group, v in enumerate((small, large)):
+        v = v.reshape(s.clips, s.cells[group], s.d).transpose(1, 0, 2)
+        parts.append(jnp.pad(v, ((0, s.padded[group] - s.cells[group]), (0, 0), (0, 0))))
+    return jnp.concatenate(parts, axis=0).reshape(s.m, s.d)
+
+
+def clip_major(s, v):
+    v = v.reshape(-1, s.clips, s.d)
+    parts, base = [], 0
+    for group in range(2):
+        part = v[base : base + s.cells[group]].transpose(1, 0, 2)
+        parts.append(part.reshape(s.clips, 1, s.cells[group], s.d))
+        base += s.padded[group]
+    return parts
+
+
+def halves(s, w):
+    return w.astype(BF).reshape(w.shape[0], 2, s.nb).transpose(1, 0, 2)
+
+
+def body(batches, slots, *args):
+    x_small, x_large = args[0], args[1]
+    plain = plain_body(*args)
+    if not fits(x_small.shape, x_large.shape, batches, slots):
+        return plain
+    fast = fast_body(Shape(x_small.shape, x_large.shape, batches, slots), *args)
+    return tuple(fast[:2]) + tuple(plain[2:])
+
+
+def fast_body(s, x_small, x_large, grad_small, grad_large, clip_counts, first_spatial, first_temporal,
+              second_spatial, second_temporal, norm_params, *states):
+    z = lax.axis_index("batch")
+    slots = jnp.arange(s.clips, dtype=jnp.int32)
+    counts = lax.dynamic_index_in_dim(clip_counts, z, 1, keepdims=False)
+    live = (slots[None, :] < counts[:, None]).astype(F32)[:, :, None]
+    totals = jnp.sum(clip_counts, axis=1).astype(F32) * (s.slots * jnp.array(s.cells, F32))
+    x = cell_major(s, x_small, x_large)
+    grad = cell_major(s, grad_small, grad_large)
+    res = forward_call(
+        s, x, grad, halves(s, first_spatial), first_temporal.astype(BF), halves(s, second_spatial),
+        second_temporal.astype(BF), norm_params, live, 1.0 / totals,
+    )
+    out_small, out_large = clip_major(s, res[12])
+    return (out_small, out_large) + tuple(res)
+
+
 def solution(mesh):
     return jax.shard_map(
-        body,
+        functools.partial(body, mesh.shape["batch"], mesh.shape["tm"]),
         mesh=mesh,
         in_specs=(
             P("batch", "tm", None, None),

time: 1510 us -> 1780 us (1.18)
  Pallas kernels: 0 us -> 370 us
  waiting for transfers between devices: 189 us -> 85.2 us
    pallas_call x0 -> x1, Pallas kernels: none -> 370 us  [forward_call(): pl.pallas_call(functools.partial(forward_kernel, s), out_shape=outs, in_s...]
    unnamed x18, waiting for transfers between devices: 83.2 us -> 11.9 us
    reduce_scatter x4, waiting for transfers between devices: 29.4 us -> 0.02 us  [reduce_weight(): lax.psum_scatter(total.astype(jnp.bfloat16), 'tm', scatter_dimension=0, t...]
    unnamed x490 -> x532, local copies, waits for them, and re-layouts: 121 us -> 120 us
    convert_element_type x21 -> x22, other arithmetic: 75.9 us -> 76.6 us  [the longest x2 18.3 us: plain_body(): grad_conv_four = grad_conv_four.astype(jnp.bfloat16)]
  transfers between devices with their start and end apart: 22 -> 22, of which waited for: 6 -> 3; matrix products, arithmetic and copies ran while one was open for 45% -> 38% of each run, Pallas kernels for 0% -> 21%
where the time goes in v1:
time: 1780 us; the launch traced here: 1770 us
  blocking collectives  472 us (27%)
  local copies, waits for them, and re-layouts  414 us (23%)
  Pallas kernels  370 us (21%)
  matrix products  228 us (13%)
  other arithmetic  152 us (9%)
  waiting for transfers between devices  85.2 us (5%)
  between operations  24.3 us (1%)
  starting transfers between devices  21.2 us (1%)
    pallas_call x1, Pallas kernels, forward_call(): pl.pallas_call(functools.partial(forward_kernel, s), out_shape=outs, in_s...  370 us
    psum x4, blocking collectives, norm_forward_pass(): lax.psum((running_sums, squared_values), ('batch', 'tm'))  221 us
    psum x4, blocking collectives, norm_reverse_pass(): lax.psum((running_sums, cross_product), ('batch', 'tm'))  169 us
    unnamed x532, local copies, waits for them, and re-layouts  120 us
    dot_general x6, matrix products, reduce_weight(): lax.dot_general(left, right, (((0,), (0,)), ((), ())), preferred_element_...  86.1 us
    concatenate x44, local copies, waits for them, and re-layouts, spatial_taps(): jnp.concatenate(pieces, axis=-1)  58 us
    dot_general x4, matrix products, spatial_backward(): lax.dot_general(upstream_rows, weight, (((1,), (1,)), ((), ())), preferre...  56 us
    slice x36, local copies, waits for them, and re-layouts, spatial_taps(): padded[:, :, row:row + side, column:column + side, :]  51.1 us
  transfers between devices with their start and end apart: 22, of which 3 were waited for; matrix products, arithmetic and copies ran while one was open for 38% of the time, Pallas kernels for 21%

profile of v1, /device:TPU:0, one launch (start us, length us, event | category | flops | bytes accessed | tf_op | source)
XLA Modules:
  0.0 1766.1 jit_solution(10772043638485350542)
XLA Ops:
  11.3 36.5 %all-gather.7.cloned.1.call-done = bf16[576,1152]{0,1:T(8,128)(2,1)} async-done(((bf16[576,288]{0,1:T(8,128)(2,1)}), bf16[576,1152]{0,1:T(8,128)(2,1)}) %all-gather.7.cloned.1.call-update) | async-done | bytes 1327120 | tf_op jit(solution)/shard_map/all_gather | solution.py:236
  51.1 18.1 %all_gather.30 = bf16[432,512]{1,0:T(8,128)(2,1)} all-gather(bf16[432,128]{1,0:T(8,128)(2,1)S(1)} %convert_element_type.254.refs_5_), channel_id=1, replica_groups=mesh['batch'=4,'tm'=8] {'batch'}, dimensions={1}, use_global_device_ids=true | all-gather | bytes 552960 | tf_op jit(solution)/shard_map/all_gather | solution.py:239
  70.0 24.7 %all_gather.26 = bf16[432,512]{1,0:T(8,128)(2,1)} all-gather(bf16[432,128]{1,0:T(8,128)(2,1)S(1)} %convert_element_type.252.refs_3_), channel_id=1, replica_groups=mesh['batch'=4,'tm'=8] {'batch'}, dimensions={1}, use_global_device_ids=true | all-gather | bytes 552960 | tf_op jit(solution)/shard_map/all_gather | solution.py:237
  121.8 36.7 %all-gather.9.cloned.1.call-done = bf16[4608,1152]{1,0:T(8,128)(2,1)} async-done(((bf16[576,1152]{1,0:T(8,128)(2,1)}), bf16[4608,1152]{1,0:T(8,128)(2,1)}) %all-gather.9.cloned.1.call-update) | async-done | bytes 10616848 | tf_op jit(solution)/shard_map/all_gather | solution.py:242
  158.4 10.9 fusion.14
  169.4 13.2 fusion.12
  185.3 39.8 %all-reduce.17 = (f32[2,1152]{1,0:T(2,128)S(1)}, f32[2,1152]{1,0:T(2,128)S(1)}) all-reduce(f32[2,1152]{1,0:T(2,128)S(1)} %pad_maximum_fusion.23, f32[2,1152]{1,0:T(2,128)S(1)} %pad_maximum_fusion.24), channel_id=1, replica_groups=mesh['batch'=4,'tm'=8] {'batch','tm'}, use_global_device_ids=true, to_apply=%region_4.5 | all-reduce | flops 4608 | bytes 36864 | tf_op jit(solution)/shard_map/psum | solution.py:151
  227.5 3.7 multiply_convert_fusion.3
  234.5 4.8 collective-permute-start
  250.9 3.4 reshape.1592
  258.1 6.3 copy.388
  264.4 5.6 mul.1274
  270.0 5.8 multiply_convert_fusion.5
  280.7 4.2 copy.356
  284.8 4.2 concatenate.464
  289.1 9.1 fusion.26
  301.6 100.1 %all-reduce.16 = (f32[2,512]{1,0:T(2,128)S(1)}, f32[2,512]{1,0:T(2,128)S(1)}) all-reduce(f32[2,512]{1,0:T(2,128)S(1)} %pad_maximum_fusion.32, f32[2,512]{1,0:T(2,128)S(1)} %pad_maximum_fusion.33), channel_id=1, replica_groups=mesh['batch'=4,'tm'=8] {'batch','tm'}, use_global_device_ids=true, to_apply=%region_14.15 | all-reduce | flops 2048 | bytes 16384 | tf_op jit(solution)/shard_map/psum | solution.py:151
  422.0 14.6 fusion.8
  436.7 5.6 fusion.10
  445.0 39.4 %all-reduce.15 = (f32[2,1152]{1,0:T(2,128)S(1)}, f32[2,1152]{1,0:T(2,128)S(1)}) all-reduce(f32[2,1152]{1,0:T(2,128)S(1)} %pad_maximum_fusion.25, f32[2,1152]{1,0:T(2,128)S(1)} %pad_maximum_fusion.26), channel_id=1, replica_groups=mesh['batch'=4,'tm'=8] {'batch','tm'}, use_global_device_ids=true, to_apply=%region_22.23 | all-reduce | flops 4608 | bytes 36864 | tf_op jit(solution)/shard_map/psum | solution.py:151
  486.6 4.4 multiply_convert_fusion.2
  494.5 4.5 collective-permute-start.2
  510.7 5.7 mul.1298
  546.6 5.8 multiply_convert_fusion.4
  556.9 3.6 copy.379
  560.5 4.2 concatenate.492
  564.7 9.1 fusion.32
  577.3 41.6 %all-reduce.14 = (f32[2,512]{1,0:T(2,128)S(1)}, f32[2,512]{1,0:T(2,128)S(1)}) all-reduce(f32[2,512]{1,0:T(2,128)S(1)} %pad_maximum_fusion.34, f32[2,512]{1,0:T(2,128)S(1)} %pad_maximum_fusion.35), channel_id=1, replica_groups=mesh['batch'=4,'tm'=8] {'batch','tm'}, use_global_device_ids=true, to_apply=%region_30.31 | all-reduce | flops 2048 | bytes 16384 | tf_op jit(solution)/shard_map/psum | solution.py:151
  620.7 4.6 multiply_reduce_fusion.11
  625.5 39.0 %all-reduce.13 = (f32[2,512]{1,0:T(2,128)S(1)}, f32[2,512]{1,0:T(2,128)S(1)}) all-reduce(f32[2,512]{1,0:T(2,128)S(1)} %pad_maximum_fusion.37, f32[2,512]{1,0:T(2,128)S(1)} %pad_maximum_fusion.36), channel_id=1, replica_groups=mesh['batch'=4,'tm'=8] {'batch','tm'}, use_global_device_ids=true, to_apply=%region_42.43 | all-reduce | flops 2048 | bytes 16384 | tf_op jit(solution)/shard_map/psum | solution.py:172
  698.0 15.7 multiply_convert_fusion.10
  716.4 9.6 bitcast_convert_fusion.1
  732.9 11.7 multiply_reduce_fusion.3
  744.8 44.1 %all-reduce.12 = (f32[2,1152]{1,0:T(2,128)S(1)}, f32[2,1152]{1,0:T(2,128)S(1)}) all-reduce(f32[2,1152]{1,0:T(2,128)S(1)} %pad_maximum_fusion.28, f32[2,1152]{1,0:T(2,128)S(1)} %pad_maximum_fusion.27), channel_id=1, replica_groups=mesh['batch'=4,'tm'=8] {'batch','tm'}, use_global_device_ids=true, to_apply=%region_50.51 | all-reduce | flops 4608 | bytes 36864 | tf_op jit(solution)/shard_map/psum | solution.py:172
  792.1 4.6 fusion.62
  799.9 19.2 %convolution_bitcast_fusion.1 = f32[8,1,10,10,4608]{4,3,2,0,1:T(8,128)} fusion(bf16[4608,1152]{1,0:T(8,128)(2,1)S(1)} %bitcast.489, bf16[8,10,10,1152]{3,0,2,1:T(8,128)(2,1)S(1)} %bitcast.430), kind=kOutput, calls=%fused_computation.37 | convolution fusion | flops 8493465600 | bytes 27205632 | tf_op jit(solution)/shard_map/dot_general | solution.py:72
  819.1 9.1 fusion.71
  831.5 7.9 fusion.40
  841.5 3.6 multiply_reduce_fusion.9
  845.2 39.9 %all-reduce.11 = (f32[2,512]{1,0:T(2,128)S(1)}, f32[2,512]{1,0:T(2,128)S(1)}) all-reduce(f32[2,512]{1,0:T(2,128)S(1)} %pad_maximum_fusion.39, f32[2,512]{1,0:T(2,128)S(1)} %pad_maximum_fusion.38), channel_id=1, replica_groups=mesh['batch'=4,'tm'=8] {'batch','tm'}, use_global_device_ids=true, to_apply=%region_58.59 | all-reduce | flops 2048 | bytes 16384 | tf_op jit(solution)/shard_map/psum | solution.py:172
  889.5 3.5 mul.1427
  895.5 3.5 sub.394
  903.8 3.4 concatenate.547
  909.0 3.5 mul.1383
  915.2 3.4 sub.372
  918.6 3.4 concatenate.513
  922.0 14.1 multiply_convert_fusion.9
  938.9 10.4 bitcast_convert_fusion
  998.5 12.3 fusion.155
  1010.8 20.5 %fusion = bf16[4608,1152]{1,0:T(8,128)(2,1)} fusion(f32[4608,1152]{1,0:T(8,128)} %fusion.155, bf16[800,4608]{1,0:T(8,128)(2,1)} %constant_dynamic-update-slice_fusion.13, bf16[800,1152]{1,0:T(8,128)(2,1)} %reshape.1587), kind=kOutput, calls=%fused_computation.34 | convolution fusion | flops 8504082432 | bytes 41066496 | tf_op jit(solution)/shard_map/dot_general | solution.py:187
  1103.6 3.4 copy-done.188
  1107.0 3.8 copy.400
  1117.1 11.7 multiply_reduce_fusion.1
  1129.1 45.8 %all-reduce.10 = (f32[2,1152]{1,0:T(2,128)S(1)}, f32[2,1152]{1,0:T(2,128)S(1)}) all-reduce(f32[2,1152]{1,0:T(2,128)S(1)} %pad_maximum_fusion.30, f32[2,1152]{1,0:T(2,128)S(1)} %pad_maximum_fusion.29), channel_id=1, replica_groups=mesh['batch'=4,'tm'=8] {'batch','tm'}, use_global_device_ids=true, to_apply=%region_66.67 | all-reduce | flops 4608 | bytes 36864 | tf_op jit(solution)/shard_map/psum | solution.py:172
  1178.1 4.4 fusion.63
  1186.0 12.4 fusion.156
  1198.4 20.8 %fusion.1 = bf16[4608,1152]{1,0:T(8,128)(2,1)} fusion(f32[4608,1152]{1,0:T(8,128)} %fusion.156, bf16[800,4608]{1,0:T(8,128)(2,1)} %copy-done.188, bf16[800,1152]{1,0:T(8,128)(2,1)} %reshape.1590), kind=kOutput, calls=%fused_computation.35 | convolution fusion | flops 8504082432 | bytes 41066496 | tf_op jit(solution)/shard_map/dot_general | solution.py:187
  1232.9 370.2 %forward.1 = (bf16[4,1152,1152]{2,1,0:T(8,128)(2,1)}, bf16[3456,512]{1,0:T(8,128)(2,1)}, bf16[4,1152,1152]{2,1,0:T(8,128)(2,1)}, bf16[3456,512]{1,0:T(8,128)(2,1...) custom-call(bf16[1200,512]{1,0:T(8,128)(2,1)} %get-tuple-element.275, ...), custom_call_target="tpu_custom_call" | custom-call | tf_op jit(solution)/shard_map/forward/pallas_call | solution.py:1126
  1621.9 21.3 %convolution_bitcast_fusion = f32[8,1,10,10,4608]{4,3,2,0,1:T(8,128)} fusion(bf16[4608,1152]{1,0:T(8,128)(2,1)} %all-gather.9.cloned.1.call-done, bf16[8,10,10,1152]{3,0,2,1:T(8,128)(2,1)S(1)} %bitcast.429), kind=kOutput, calls=%fused_computation.36 | convolution fusion | flops 8493465600 | bytes 27205632 | tf_op jit(solution)/shard_map/dot_general | solution.py:72
  1645.9 7.6 fusion.43
  1657.6 9.6 fusion.79
  1677.8 11.7 reduce-scatter.31.cloned.1.call-done
  1695.0 39.1 %psum.162 = f32[]{:T(128)} all-reduce(f32[]{:T(128)S(6)} %add.692), channel_id=1, replica_groups=mesh['batch'=4,'tm'=8] {'batch','tm'}, use_global_device_ids=true, to_apply=%region_70.71 | all-reduce | flops 1 | bytes 8 | tf_op jit(solution)/shard_map/psum | solution.py:399
  1735.5 3.4 multiply_subtract_fusion.1
  (938 shorter events, 423.9 us)
Async XLA Ops:
  7.2 40.6 %all-gather.7.cloned.1.call-start = ((), (), s32[]{:S(2)}) async-start(), calls=%async_computation.8 | async-start | bytes 1843200 | tf_op jit(solution)/shard_map/all_gather | solution.py:236
  9.2 41.3 %copy-start.176 = (f32[432,128]{1,0:T(8,128)S(1)}, f32[432,128]{1,0:T(8,128)}, u32[]{:S(2)}) copy-start(f32[432,128]{1,0:T(8,128)} %param.29) | copy-start | bytes 663556
  9.2 109.7 %all-gather.13.cloned.1.call-start = ((), (), s32[]{:S(2)}) async-start(), calls=%async_computation.11 | async-start | bytes 1843200 | tf_op jit(solution)/shard_map/all_gather | solution.py:238
  11.2 58.1 %copy-start.174 = (f32[432,128]{1,0:T(8,128)S(1)}, f32[432,128]{1,0:T(8,128)}, u32[]{:S(2)}) copy-start(f32[432,128]{1,0:T(8,128)} %param.27) | copy-start | bytes 663556
  11.2 83.5 %copy-start.209 = (s32[2,4]{1,0:T(2,128)S(1)}, s32[2,4]{1,0:T(2,128)}, u32[]{:S(2)}) copy-start(s32[2,4]{1,0:T(2,128)} %param.25) | copy-start | bytes 100
  11.2 88.8 %copy-start.180 = (f32[2,3328]{1,0:T(2,128)S(1)}, f32[2,3328]{1,0:T(2,128)}, u32[]{:S(2)}) copy-start(f32[2,3328]{1,0:T(2,128)} %refs_6_.1) | copy-start | bytes 79876
  11.2 89.4 %copy-start.23 = (bf16[8,1,100,512]{3,0,2,1:T(8,128)(2,1)S(1)}, bf16[8,1,100,512]{3,0,2,1:T(8,128)(2,1)}, u32[]{:S(2)}) copy-start(bf16[8,1,100,512]{3,0,2,1:T(8,128)(2,1)} %param.22) | copy-start | bytes 2457604
  11.3 89.4 %copy-start.78 = (bf16[8,1,49,512]{3,0,2,1:T(8,128)(2,1)S(1)}, bf16[8,1,49,512]{3,0,2,1:T(8,128)(2,1)}, u32[]{:S(2)}) copy-start(bf16[8,1,49,512]{3,0,2,1:T(8,128)(2,1)} %param.21) | copy-start | bytes 1204228
  11.3 147.2 %all-gather.9.cloned.1.call-start = ((), (), s32[]{:S(2)}) async-start(), calls=%async_computation.9 | async-start | bytes 11943936 | tf_op jit(solution)/shard_map/all_gather | solution.py:242
  50.4 207.7 %all-gather.17.cloned.1.call-start = ((), (), s32[]{:S(2)}) async-start(), calls=%async_computation.13 | async-start | bytes 3981312 | tf_op jit(solution)/shard_map/all_gather | solution.py:245
  69.3 219.8 %all-gather.11.cloned.1.call-start = ((), (), s32[]{:S(2)}) async-start(), calls=%async_computation.10 | async-start | bytes 3981312 | tf_op jit(solution)/shard_map/all_gather | solution.py:243
  94.7 327.3 %all-gather.15.cloned.1.call-start = ((), (), s32[]{:S(2)}) async-start(), calls=%async_computation.12 | async-start | bytes 11943936 | tf_op jit(solution)/shard_map/all_gather | solution.py:244
  100.7 169.3 %copy-start.186 = (f32[1152]{0:T(1024)}, f32[1152]{0:T(1024)S(1)}, u32[]{:S(2)}) copy-start(f32[1152]{0:T(1024)S(1)} %get-tuple-element.121) | copy-start | bytes 13828
  100.7 169.3 %copy-start.189 = (f32[1152]{0:T(1024)}, f32[1152]{0:T(1024)S(1)}, u32[]{:S(2)}) copy-start(f32[1152]{0:T(1024)S(1)} %get-tuple-element.120) | copy-start | bytes 13828
  102.6 10.6 copy-start.112
  102.6 10.8 copy-start.111
  102.6 10.9 copy-start.110
  102.6 11.0 copy-start.108
  104.5 9.3 copy-start.53
  104.5 10.6 copy-start.51
  104.5 11.9 copy-start.49
  104.5 13.2 copy-start.47
  121.5 1097.8 %reduce-scatter.17.cloned.1.call-start = ((), (), s32[]{:S(2)}) async-start(), calls=%async_computation.14 | async-start | bytes 3981312 | tf_op jit(solution)/shard_map/reduce_scatter | solution.py:190
  158.4 10.9 copy-start.215
  169.4 57.9 %copy-start.12 = (f32[8,49,1152]{2,1,0:T(8,128)}, f32[8,49,1152]{2,1,0:T(8,128)S(1)}, u32[]{:S(2)}) copy-start(f32[8,49,1152]{2,1,0:T(8,128)S(1)} %fusion.14) | copy-start | bytes 5419012
  231.2 9.8 copy-start.25
  233.2 42.6 %collective-permute-start.1 = (bf16[8,1,149,1152]{3,0,2,1:T(8,128)(2,1)}, bf16[8,1,149,1152]{3,0,2,1:T(8,128)(2,1)}, u32[]{:S(2)}, u32[]{:S(2)}) collective-permute-start(bf16[8,1,149,1152]{3,0,2,1:T(8,128)(2,1)} %copy.355), channel_id=1, source_target_pairs={{1,0},{2,1},{3,2},{4,3},{5,4},{6,5},{7,6},{9,8},{10,9},{11,10},{12... | collective-permute-start | bytes 8239112 | tf_op jit(solution)/shard_map/ppermute | solution.py:36
  234.5 46.2 %collective-permute-start = (bf16[8,1,149,1152]{3,0,2,1:T(8,128)(2,1)}, bf16[8,1,149,1152]{3,0,2,1:T(8,128)(2,1)}, u32[]{:S(2)}, u32[]{:S(2)}) collective-permute-start(bf16[8,1,149,1152]{3,0,2,1:T(8,128)(2,1)} %copy.355), channel_id=1, source_target_pairs={{0,1},{1,2},{2,3},{3,4},{4,5},{5,6},{6,7},{8,9},{9,10},{10,11},{11... | collective-permute-start | bytes 8239112 | tf_op jit(solution)/shard_map/ppermute | solution.py:35
  241.2 13.1 copy-start.42
  258.1 144.6 %copy-start.191 = (f32[1,512]{1,0:T(1,128)}, f32[1,512]{1,0:T(1,128)S(1)}, u32[]{:S(2)}) copy-start(f32[1,512]{1,0:T(1,128)S(1)} %get-tuple-element.235) | copy-start | bytes 6148
  258.1 144.6 %copy-start.195 = (f32[1,512]{1,0:T(1,128)}, f32[1,512]{1,0:T(1,128)S(1)}, u32[]{:S(2)}) copy-start(f32[1,512]{1,0:T(1,128)S(1)} %get-tuple-element.234) | copy-start | bytes 6148
  300.1 102.6 %copy-start = (f32[8,1,149,512]{3,2,0,1:T(8,128)}, f32[8,1,149,512]{3,2,0,1:T(8,128)S(1)}, u32[]{:S(2)}) copy-start(f32[8,1,149,512]{3,2,0,1:T(8,128)S(1)} %reshape.1569) | copy-start | bytes 7323652
  402.5 122.0 %copy-start.30 = (f32[149,512]{1,0:T(8,128)}, f32[149,512]{1,0:T(8,128)S(1)}, u32[]{:S(2)}) copy-start(f32[149,512]{1,0:T(8,128)S(1)} %pad_maximum_fusion.12) | copy-start | bytes 915460
  402.7 119.9 %copy-start.32 = (f32[149,512]{1,0:T(8,128)}, f32[149,512]{1,0:T(8,128)S(1)}, u32[]{:S(2)}) copy-start(f32[149,512]{1,0:T(8,128)S(1)} %get-tuple-element.230) | copy-start | bytes 915460
  402.7 123.9 %copy-start.101 = (f32[149,512]{1,0:T(8,128)}, f32[149,512]{1,0:T(8,128)S(1)}, u32[]{:S(2)}) copy-start(f32[149,512]{1,0:T(8,128)S(1)} %get-tuple-element.229) | copy-start | bytes 915460
  410.5 9.1 copy-start.65
  410.5 10.3 copy-start.63
  422.0 14.6 copy-start.199
  422.0 14.6 copy-start.216
  442.3 44.3 %copy-start.14 = (f32[8,49,1152]{2,1,0:T(8,128)}, f32[8,49,1152]{2,1,0:T(8,128)S(1)}, u32[]{:S(2)}) copy-start(f32[8,49,1152]{2,1,0:T(8,128)S(1)} %fusion.10) | copy-start | bytes 5419012
  491.1 9.8 copy-start.125
  491.1 10.7 copy-start.123
  492.9 9.8 copy-start.105
  492.9 14.5 copy-start.119
  492.9 59.4 %collective-permute-start.3 = (bf16[8,1,149,1152]{3,0,2,1:T(8,128)(2,1)}, bf16[8,1,149,1152]{3,0,2,1:T(8,128)(2,1)}, u32[]{:S(2)}, u32[]{:S(2)}) collective-permute-start(bf16[8,1,149,1152]{3,0,2,1:T(8,128)(2,1)} %copy.378), channel_id=1, source_target_pairs={{1,0},{2,1},{3,2},{4,3},{5,4},{6,5},{7,6},{9,8},{10,9},{11,10},{12... | collective-permute-start | bytes 8239112 | tf_op jit(solution)/shard_map/ppermute | solution.py:36
  494.5 62.4 %collective-permute-start.2 = (bf16[8,1,149,1152]{3,0,2,1:T(8,128)(2,1)}, bf16[8,1,149,1152]{3,0,2,1:T(8,128)(2,1)}, u32[]{:S(2)}, u32[]{:S(2)}) collective-permute-start(bf16[8,1,149,1152]{3,0,2,1:T(8,128)(2,1)} %copy.378), channel_id=1, source_target_pairs={{0,1},{1,2},{2,3},{3,4},{4,5},{5,6},{6,7},{8,9},{9,10},{10,11},{11... | collective-permute-start | bytes 8239112 | tf_op jit(solution)/shard_map/ppermute | solution.py:35
  575.8 44.1 %copy-start.201 = (f32[1,512]{1,0:T(1,128)S(1)}, f32[1,512]{1,0:T(1,128)}, u32[]{:S(2)}) copy-start(f32[1,512]{1,0:T(1,128)} %get-tuple-element.233) | copy-start | bytes 6148
  575.8 44.9 %copy-start.21 = (bf16[8,1,100,512]{3,2,0,1:T(8,128)(2,1)S(1)}, bf16[8,1,100,512]{3,2,0,1:T(8,128)(2,1)}, u32[]{:S(2)}) copy-start(bf16[8,1,100,512]{3,2,0,1:T(8,128)(2,1)} %copy-done.20) | copy-start | bytes 2457604
  575.8 44.9 %copy-start.208 = (f32[1,512]{1,0:T(1,128)S(1)}, f32[1,512]{1,0:T(1,128)}, u32[]{:S(2)}) copy-start(f32[1,512]{1,0:T(1,128)} %get-tuple-element.236) | copy-start | bytes 6148
  625.3 42.0 %copy-start.39 = (f32[149,512]{1,0:T(8,128)S(1)}, f32[149,512]{1,0:T(8,128)}, u32[]{:S(2)}) copy-start(f32[149,512]{1,0:T(8,128)} %copy-done.38) | copy-start | bytes 915460
  625.3 42.0 %copy-start.41 = (f32[149,512]{1,0:T(8,128)S(1)}, f32[149,512]{1,0:T(8,128)}, u32[]{:S(2)}) copy-start(f32[149,512]{1,0:T(8,128)} %copy-done.40) | copy-start | bytes 915460
  671.3 57.4 %collective-permute-start.5 = (bf16[8,1,149,512]{3,0,2,1:T(8,128)(2,1)}, bf16[8,1,149,512]{3,0,2,1:T(8,128)(2,1)}, u32[]{:S(2)}, u32[]{:S(2)}) collective-permute-start(bf16[8,1,149,512]{3,0,2,1:T(8,128)(2,1)} %copy.384), channel_id=1, source_target_pairs={{0,1},{1,2},{2,3},{3,4},{4,5},{5,6},{6,7},{8,9},{9,10},{10,11},{11... | collective-permute-start | bytes 3661832 | tf_op jit(solution)/shard_map/ppermute | solution.py:35
  673.7 56.9 %collective-permute-start.4 = (bf16[8,1,149,512]{3,0,2,1:T(8,128)(2,1)}, bf16[8,1,149,512]{3,0,2,1:T(8,128)(2,1)}, u32[]{:S(2)}, u32[]{:S(2)}) collective-permute-start(bf16[8,1,149,512]{3,0,2,1:T(8,128)(2,1)} %copy.384), channel_id=1, source_target_pairs={{1,0},{2,1},{3,2},{4,3},{5,4},{6,5},{7,6},{9,8},{10,9},{11,10},{12... | collective-permute-start | bytes 3661832 | tf_op jit(solution)/shard_map/ppermute | solution.py:36
  698.0 18.4 %copy-start.28 = (bf16[8,1,149,1152]{3,2,0,1:T(8,128)(2,1)S(1)}, bf16[8,1,149,1152]{3,2,0,1:T(8,128)(2,1)}, u32[]{:S(2)}) copy-start(bf16[8,1,149,1152]{3,2,0,1:T(8,128)(2,1)} %copy-done.27) | copy-start | bytes 8239108
  728.7 500.3 %reduce-scatter.21.cloned.1.call-start = ((), (), s32[]{:S(2)}) async-start(), calls=%async_computation.16 | async-start | bytes 3981312 | tf_op jit(solution)/shard_map/reduce_scatter | solution.py:190
  949.3 669.8 %reduce-scatter.19.cloned.1.call-start = ((), (), s32[]{:S(2)}) async-start(), calls=%async_computation.15 | async-start | bytes 11943936 | tf_op jit(solution)/shard_map/reduce_scatter | solution.py:190
  1031.4 611.8 %reduce-scatter.23.cloned.1.call-start = ((), (), s32[]{:S(2)}) async-start(), calls=%async_computation.17 | async-start | bytes 11943936 | tf_op jit(solution)/shard_map/reduce_scatter | solution.py:190
  1070.9 42.7 %collective-permute-start.7 = (bf16[8,1,149,512]{3,0,2,1:T(8,128)(2,1)}, bf16[8,1,149,512]{3,0,2,1:T(8,128)(2,1)}, u32[]{:S(2)}, u32[]{:S(2)}) collective-permute-start(bf16[8,1,149,512]{3,0,2,1:T(8,128)(2,1)} %copy.396), channel_id=1, source_target_pairs={{0,1},{1,2},{2,3},{3,4},{4,5},{5,6},{6,7},{8,9},{9,10},{10,11},{11... | collective-permute-start | bytes 3661832 | tf_op jit(solution)/shard_map/ppermute | solution.py:35
  1073.7 41.8 %collective-permute-start.6 = (bf16[8,1,149,512]{3,0,2,1:T(8,128)(2,1)}, bf16[8,1,149,512]{3,0,2,1:T(8,128)(2,1)}, u32[]{:S(2)}, u32[]{:S(2)}) collective-permute-start(bf16[8,1,149,512]{3,0,2,1:T(8,128)(2,1)} %copy.396), channel_id=1, source_target_pairs={{1,0},{2,1},{3,2},{4,3},{5,4},{6,5},{7,6},{9,8},{10,9},{11,10},{12... | collective-permute-start | bytes 3661832 | tf_op jit(solution)/shard_map/ppermute | solution.py:36
  1219.3 451.0 %reduce-scatter.25.cloned.1.call-start = ((), (), s32[]{:S(2)}) async-start(), calls=%async_computation.18 | async-start | bytes 655360
  1221.5 450.5 %reduce-scatter.29.cloned.1.call-start = ((), (), s32[]{:S(2)}) async-start(), calls=%async_computation.20 | async-start | bytes 655360
  1231.2 442.5 %reduce-scatter.27.cloned.1.call-start = ((), (), s32[]{:S(2)}) async-start(), calls=%async_computation.19 | async-start | bytes 1843200
  1621.8 67.6 %reduce-scatter.31.cloned.1.call-start = ((), (), s32[]{:S(2)}) async-start(), calls=%async_computation.21 | async-start | bytes 1843200
  1673.7 61.8 %copy-start.132 = (f32[576,288]{1,0:T(8,128)S(1)}, f32[576,288]{1,0:T(8,128)}, u32[]{:S(2)}) copy-start(f32[576,288]{1,0:T(8,128)} %copy.453) | copy-start | bytes 1990660
  (179 other events, 719.4 us)
Sparse Core Ops, SparseCore 0:
  9.6 38.1 all-gather.6
  49.4 44.6 all-gather.12
  96.6 61.8 all-gather.8
  160.2 34.1 all-gather.16
  196.1 35.0 all-gather.10
  233.5 105.6 all-gather.14
  728.8 51.3 reduce-scatter.16
  949.4 48.1 reduce-scatter.20
  1031.5 99.2 reduce-scatter.18
  1219.4 118.6 reduce-scatter.22
  1341.0 24.4 reduce-scatter.24
  1368.1 21.0 reduce-scatter.28
  1622.0 32.4 reduce-scatter.26
  1656.8 32.6 reduce-scatter.30

commit v2 on v1

--- a/solution.py
+++ b/solution.py
@@ -1158,30 +1158,571 @@
     return w.astype(BF).reshape(w.shape[0], 2, s.nb).transpose(1, 0, 2)
 
 
+def add_into(dst, src, rows, step):
+    def body(i, _):
+        at = pl.ds(pl.multiple_of(i * step, 16), step)
+        dst[at, :] = (dst[at, :].astype(F32) + src[at, :].astype(F32)).astype(BF)
+        return 0
+
+    lax.fori_loop(0, rows // step, body, 0)
+
+
+class Scatter:
+    def __init__(self, place, index, part, bufs, cut, rows, step, sems):
+        self.p, self.n, self.part, self.cut, self.rows, self.step = place, index, part, cut, rows, step
+        self.tr, self.fx, self.fa, self.rx, self.ry, self.ru, self.rd = bufs
+        self.twin_s, self.twin_r, self.block_s, self.block_r = sems
+        self.half = place.batches // 2
+
+    FAR, SIDE, DEEP, RISE, FALL = range(5)
+
+    def twin_copy(self, rel):
+        p = self.p
+        return send(self.part(rel, 1 - p.core), self.tr.at[rel], self.twin_s.at[self.n, rel],
+                    self.twin_r.at[self.n, rel], p.device(TWIN))
+
+    def block_copy(self, kind, b, src, dst, way):
+        return send(src, dst, self.block_s.at[self.n, kind, b], self.block_r.at[self.n, kind, b],
+                    self.p.device(way))
+
+    def own(self, rel, b):
+        return self.cut(self.part(rel, self.p.core), b)
+
+    def far_copy(self, b):
+        if b < self.half:
+            return self.block_copy(self.FAR, b, self.own(3, b), self.cut(self.fx, b), ACROSS)
+        return self.block_copy(self.FAR, b, self.own(3, b), self.cut(self.fa, b - self.half), ALONG)
+
+    def side_copy(self, b):
+        return self.block_copy(self.SIDE, b, self.own(1, b), self.cut(self.rx, b), ACROSS)
+
+    def deep_copy(self, b):
+        return self.block_copy(self.DEEP, b, self.own(2, b), self.cut(self.ry, b), ALONG)
+
+    def rise_copy(self, b):
+        return self.block_copy(self.RISE, b, self.own(0, b), self.cut(self.ru, b), UP)
+
+    def fall_copy(self, b):
+        return self.block_copy(self.FALL, b, self.own(0, b), self.cut(self.rd, b), DOWN)
+
+    def arrive(self, kind, b, ref):
+        self.block_copy(kind, b, ref, ref, TWIN).wait_recv()
+
+    def add(self, dst, src):
+        add_into(dst, src, self.rows, self.step)
+
+    def order(self):
+        n = self.p.batches
+        out = []
+        for i in range(n // 2):
+            out += [n - 1 - i, i]
+        return out
+
+    def twin(self, rel):
+        self.twin_copy(rel).start()
+
+    def join(self, rel):
+        p = self.p
+        self.twin_copy(rel).wait_recv()
+        for b in self.order():
+            self.add(self.own(rel, b), self.cut(self.tr.at[rel], b))
+            if rel == 3:
+                self.far_copy(b).start()
+            if rel == 1 and b < self.half:
+                self.side_copy(b).start()
+            if rel == 2 and b >= self.half:
+                self.deep_copy(b).start()
+
+    def relay(self, b):
+        if b < self.half:
+            src = self.cut(self.fx, b)
+            self.arrive(self.FAR, b, src)
+            self.add(self.own(2, b), src)
+            self.deep_copy(b).start()
+        else:
+            src = self.cut(self.fa, b - self.half)
+            self.arrive(self.FAR, b, src)
+            self.add(self.own(1, b), src)
+            self.side_copy(b).start()
+
+    def collect(self, b):
+        for kind, buf in ((self.SIDE, self.rx), (self.DEEP, self.ry)):
+            src = self.cut(buf, b)
+            self.arrive(kind, b, src)
+            self.add(self.own(0, b), src)
+
+    def chain(self, b):
+        p = self.p
+
+        @pl.when(p.z < b)
+        def _():
+            @pl.when(p.z > 0)
+            def _():
+                self.arrive(self.RISE, b, self.cut(self.ru, b))
+                self.add(self.own(0, b), self.cut(self.ru, b))
+
+            self.rise_copy(b).start()
+
+        @pl.when(p.z > b)
+        def _():
+            @pl.when(p.z < p.batches - 1)
+            def _():
+                self.arrive(self.FALL, b, self.cut(self.rd, b))
+                self.add(self.own(0, b), self.cut(self.rd, b))
+
+            self.fall_copy(b).start()
+
+    def result(self):
+        p = self.p
+        pl.when(p.z > 0)(lambda: self.arrive(self.RISE, p.z, self.cut(self.ru, p.z)))
+        pl.when(p.z < p.batches - 1)(lambda: self.arrive(self.FALL, p.z, self.cut(self.rd, p.z)))
+
+        @pl.when(p.z == 0)
+        def _():
+            ref = self.cut(self.ru, p.z)
+            ref[...] = jnp.zeros(ref.shape, BF)
+
+        @pl.when(p.z == p.batches - 1)
+        def _():
+            ref = self.cut(self.rd, p.z)
+            ref[...] = jnp.zeros(ref.shape, BF)
+
+        return (
+            self.own(0, p.z)[...].astype(F32)
+            + self.cut(self.ru, p.z)[...].astype(F32)
+            + self.cut(self.rd, p.z)[...].astype(F32)
+        )
+
+    def sent(self):
+        p = self.p
+        for rel in range(4):
+            self.twin_copy(rel).wait_send()
+        for b in range(p.batches):
+            self.far_copy(b).wait_send()
+            self.side_copy(b).wait_send()
+            self.deep_copy(b).wait_send()
+            pl.when(p.z < b)(lambda b=b: self.rise_copy(b).wait_send())
+            pl.when(p.z > b)(lambda b=b: self.fall_copy(b).wait_send())
+
+    def steps(self):
+        part = functools.partial
+        out = [part(self.join, rel) for rel in (3, 1, 2, 0)]
+        out += [part(self.relay, b) for b in self.order()]
+        for b in self.order():
+            out += [part(self.collect, b), part(self.chain, b)]
+        return out
+
+
+def rows_of_grid(s, grids, group, r0):
+    side = s.sides[group]
+    base = 0 if group == 0 else s.rows[0]
+    first = (r0 - base) // 8
+    cells = [grids[group][1 + (first + n) // side, 1 + lax.rem(first + n, side)] for n in range(10)]
+    return jnp.concatenate(cells, axis=0)
+
+
+def slope(v):
+    gate = sigmoid(v)
+    return gate * (1.0 + v * (1.0 - gate))
+
+
+def backward_kernel(s, *refs):
+    (gs1, gu1, gs2, gu2, taps1, taps2, xh1, xh2, xh3, xh4, z1, z3, dpre,
+     r1, r2, r3, r4, last, norm, live_ref, inverse,
+     dx, gsh1, gsh2, guo1, guo2, ng, square,
+     ps, tr, fx, fa, rx, ry, ru, rd, pu, utr, ufx, ufa, urx, ury, uru, urd,
+     nat, flip, d3, turn, planes, lines,
+     load, tap_sem, tile_sem, halo_send, halo_recv, twin_s, twin_r, block_s, block_r, half_s, half_r,
+     pl_send, pl_recv, ln_send, ln_recv) = refs
+    p = Place(s.batches, s.slots)
+    live = [live_ref[g] for g in range(2)]
+    inv = [inverse[g] for g in range(2)]
+    totals = Totals(p, 4, planes, lines, (pl_send, pl_recv, ln_send, ln_recv))
+    d, mid, m = s.d, s.mid, s.m
+    bounds = (0, mid, mid + d, 2 * mid + d, 2 * mid + 2 * d)
+
+    def gain_bias(n):
+        return norm[0:1, bounds[n] : bounds[n + 1]], norm[1:2, bounds[n] : bounds[n + 1]]
+
+    p.greet()
+    queue = []
+
+    def tick(count):
+        for _ in range(count):
+            if queue:
+                queue.pop(0)()
+
+    def flush():
+        while queue:
+            queue.pop(0)()
+
+    def cut_rows(ref, b):
+        at = b * s.nb if isinstance(b, int) else pl.multiple_of(b * s.nb, 16)
+        return ref.at[pl.ds(at, s.nb)]
+
+    def cut_lanes(ref, b):
+        at = b * s.uc if isinstance(b, int) else pl.multiple_of(b * s.uc, 128)
+        return ref.at[:, pl.ds(at, s.uc)]
+
+    def part_s(rel, core):
+        return ps.at[rel, core]
+
+    def part_u(rel, core):
+        return pu.at[pl.ds(pl.multiple_of((p.rel[rel] * 2 + core) * s.ur, 16), s.ur)]
+
+    sems = (twin_s, twin_r, block_s, block_r)
+
+    def scatter(n):
+        if n % 2 == 0:
+            return Scatter(p, n, part_s, (tr, fx, fa, rx, ry, ru, rd), cut_rows, s.nb, 48, sems)
+        return Scatter(p, n, part_u, (utr, ufx, ufa, urx, ury, uru, urd), cut_lanes, s.ur, 144, sems)
+
+    for side, edge in ((0, p.slots - 1), (2, 0)):
+        @pl.when(p.t == edge)
+        def _(side=side):
+            d3[side] = jnp.zeros(d3.shape[1:], BF)
+
+    def norm_back(n, total, scale, dh, xhat, store, size, width):
+        gain, _ = gain_bias(n)
+        ng[0:1, bounds[n] : bounds[n + 1]] = total[2:3, :] + total[3:4, :]
+        ng[1:2, bounds[n] : bounds[n + 1]] = total[0:1, :] + total[1:2, :]
+        lead = [gain * scale[g : g + 1, :] for g in range(2)]
+        mean = [total[g : g + 1, :] * inv[g] for g in range(2)]
+        cross = [total[2 + g : 3 + g, :] * inv[g] for g in range(2)]
+
+        def rows(group, r0, c):
+            at = pl.ds(r0, size)
+            v = lead[group] * (dh[at, :] - mean[group] - xhat[at, :] * cross[group])
+            v = v.reshape(size // 8, 8, width) * live[group][None]
+            store(at, v.reshape(size, width))
+            return c
+
+        chunks(s, size, rows)
+
+    def upstream(n, dz, xhat, fetch, size, width):
+        gain, bias = gain_bias(n)
+
+        def body(group, r0, c):
+            at = pl.ds(r0, size)
+            xv = xhat[at, :]
+            v = fetch(group, r0) * slope(xv * gain + bias)
+            dz[at, :] = v
+            return (c[0] + jnp.sum(v.reshape(size // 8, 8, width), axis=0),
+                    c[1] + jnp.sum((v * xv).reshape(size // 8, 8, width), axis=0))
+
+        zero = jnp.zeros((8, width), F32)
+        small, large = chunks(s, size, body, (zero, zero))
+        rows = [jnp.sum(v * live[g], axis=0, keepdims=True) for v, g in
+                ((small[0], 0), (large[0], 1), (small[1], 0), (large[1], 1))]
+        return jnp.concatenate(rows, axis=0)
+
+    def transpose():
+        def body(j, _):
+            at = pl.ds(pl.multiple_of(j * 128, 128), 128)
+            flip[at, :] = nat[:, at].T
+            return 0
+
+        lax.fori_loop(0, mid // 128, body, 0)
+
+    def fetch_into(src, dst, sem):
+        c = pltpu.make_async_copy(src, dst, load.at[sem])
+        c.start()
+        return c
+
+    def narrow_store(at, v):
+        d3[1, at, :] = v.astype(BF)
+
+    def nat_store(at, v):
+        nat[at, :] = v.astype(BF)
+
+    def first(up, xh):
+        c1, c2 = fetch_into(dpre, up, 0), fetch_into(xh4, xh, 1)
+        c1.wait()
+        c2.wait()
+        norm_back(3, last[...], r4[...], up, xh, narrow_store, 80, d)
+
+    pl.run_scoped(first, pltpu.VMEM((m, d), F32), pltpu.VMEM((m, d), F32))
+    zero_padding(s, d3.at[1], d)
+
+    def temporal(stage, index, n, whole, zs, xhs, scale):
+        def halo(side):
+            to = p.t + 1 if side == 2 else p.t - 1
+            return send(d3.at[1], d3.at[side], halo_send.at[stage, side // 2], halo_recv.at[stage, side // 2],
+                        (p.z, to))
+
+        def run(dz, xh, wu):
+            pl.when(p.t < p.slots - 1)(lambda: halo(2).start())
+            pl.when(p.t > 0)(lambda: halo(0).start())
+            cz = fetch_into(zs, nat, 2)
+            cw = fetch_into(whole, wu, 3)
+            cx = fetch_into(xhs, xh, 4)
+            cz.wait()
+            transpose()
+            cw.wait()
+
+            def grads(k):
+                for lo, width in wide_cuts(mid):
+                    y = lax.dot_general(d3[k], wu[k * mid + lo : k * mid + lo + width, :], NT_DIMS,
+                                        preferred_element_type=F32)
+                    if k == 1:
+                        dz[:, lo : lo + width] = y
+                    else:
+                        dz[:, lo : lo + width] += y
+                pu[k * mid : (k + 1) * mid, :] = jnp.dot(
+                    flip[...], d3[k], preferred_element_type=F32
+                ).astype(BF)
+
+            grads(1)
+            tick(2)
+            pl.when(p.t < p.slots - 1)(lambda: halo(0).wait_recv())
+            grads(0)
+            pl.when(p.t > 0)(lambda: halo(2).wait_recv())
+            grads(2)
+            sc = scatter(index)
+            for rel in (3, 1, 2, 0):
+                sc.twin(rel)
+            queue.extend(sc.steps())
+            cx.wait()
+
+            def fetch(group, r0):
+                return dz[pl.ds(r0, 16), :]
+
+            total = totals.run(2 * stage, upstream(n, dz, xh, fetch, 16, mid))
+            norm_back(n, total, scale, dz, xh, nat_store, 16, mid)
+
+        pl.run_scoped(run, pltpu.VMEM((m, mid), F32), pltpu.VMEM((m, mid), F32), pltpu.VMEM((3 * mid, d), BF))
+        zero_padding(s, nat, mid)
+        pl.when(p.t < p.slots - 1)(lambda: halo(2).wait_send())
+        pl.when(p.t > 0)(lambda: halo(0).wait_send())
+
+    def finish_u(n, ref):
+        sc = scatter(n)
+        g = sc.result()
+        ref[...] = g
+        sc.sent()
+        return jnp.sum(g * g, axis=0, keepdims=True)
+
+    def finish_s(n, ref):
+        sc = scatter(n)
+        g = sc.result()
+        turn[...] = g.T
+        mine = turn[pl.ds(pl.multiple_of(p.core * (s.kw // 2), 16), s.kw // 2), :]
+        ref[p.core] = mine
+        copy = send(turn.at[pl.ds(pl.multiple_of((1 - p.core) * (s.kw // 2), 16), s.kw // 2)], ref.at[p.core],
+                    half_s.at[n // 2], half_r.at[n // 2], p.device(TWIN))
+        copy.start()
+        sc.sent()
+        send(turn.at[pl.ds(0, s.kw // 2)], ref.at[1 - p.core], half_s.at[n // 2], half_r.at[n // 2],
+             p.device(TWIN)).wait_recv()
+        copy.wait_send()
+        return jnp.sum(jnp.sum((g * g).reshape(s.nb, s.kw // 128, 128), axis=0), axis=0, keepdims=True)
+
+    pieces = []
+    for tap in range(9):
+        lo, end, found = tap * d, (tap + 1) * d, []
+        while lo < end:
+            hi = min(end, (lo // s.kw + 1) * s.kw)
+            found.append((lo // s.kw, lo % s.kw, lo - tap * d, hi - lo))
+            lo = hi
+        pieces.append(found)
+
+    def spatial(index, whole, taps, grids, tap_buf, tile):
+        rels = (3, 1, 2, 0)
+
+        def tap_load(i):
+            return pltpu.make_async_copy(taps.at[p.rel[rels[i]]], tap_buf.at[i % 2], tap_sem.at[i])
+
+        def tile_loads(tap):
+            return [
+                pltpu.make_async_copy(
+                    whole.at[slab, :, pl.ds(lane, width)], tile.at[tap % 2, :, pl.ds(at, width)],
+                    tile_sem.at[tap, n],
+                )
+                for n, (slab, lane, at, width) in enumerate(pieces[tap])
+            ]
+
+        tap_load(0).start()
+        tap_load(1).start()
+        for c in tile_loads(0):
+            c.start()
+        transpose()
+        for grid in grids:
+            def clear(i, _, grid=grid):
+                grid[i] = jnp.zeros(grid.shape[1:], F32)
+                return 0
+
+            lax.fori_loop(0, grid.shape[0], clear, 0)
+        sc = scatter(index)
+        for i, rel in enumerate(rels):
+            tap_load(i).wait()
+            for lo, width in wide_cuts(s.kw):
+                y = jnp.dot(flip[...], tap_buf[i % 2, :, lo : lo + width], preferred_element_type=F32).astype(BF)
+                for n in range(2 * s.batches):
+                    b, core = n // 2, n % 2
+                    ps[rel, core, b * s.nb : (b + 1) * s.nb, lo : lo + width] = y[n * s.nb : (n + 1) * s.nb]
+            sc.twin(rel)
+            if i + 2 < 4:
+                tap_load(i + 2).start()
+        queue.extend(sc.steps())
+        for tap in range(9):
+            if tap + 1 < 9:
+                for c in tile_loads(tap + 1):
+                    c.start()
+            for c in tile_loads(tap):
+                c.wait()
+            i, j = tap // 3, tap % 3
+            y = jnp.dot(nat[...], tile[tap % 2], preferred_element_type=F32)
+            base = 0
+            for group in range(2):
+                side = s.sides[group]
+                part = y[base : base + s.cells[group] * 8].reshape(side, side, 8, d)
+                grids[group][i : i + side, j : j + side] += part
+                base += s.rows[group]
+            tick(1)
+        clear_pad_cells(s, grids)
+
+    def spatial_types():
+        return (
+            pltpu.VMEM((s.sides[0] + 2, s.sides[0] + 2, 8, d), F32),
+            pltpu.VMEM((s.sides[1] + 2, s.sides[1] + 2, 8, d), F32),
+            pltpu.VMEM((2, m, s.kw), BF), pltpu.VMEM((2, mid, d), BF),
+            pltpu.VMEM((m, d), F32), pltpu.VMEM((m, d), F32),
+        )
+
+    temporal(0, 3, 2, gu2, z3, xh3, r3[...])
+
+    def second(grid_s, grid_l, tap_buf, tile, b, xh):
+        cx = fetch_into(xh2, xh, 5)
+        flush()
+        sums = finish_u(3, guo2)
+        spatial(2, gs2, taps2, (grid_s, grid_l), tap_buf, tile)
+        cx.wait()
+
+        def fetch(group, r0):
+            return rows_of_grid(s, (grid_s, grid_l), group, r0)
+
+        total = totals.run(1, upstream(1, b, xh, fetch, 80, d))
+        norm_back(1, total, r2[...], b, xh, narrow_store, 80, d)
+        return sums
+
+    sums = pl.run_scoped(second, *spatial_types())
+    zero_padding(s, d3.at[1], d)
+    temporal(1, 1, 0, gu1, z1, xh1, r1[...])
+
+    def final(grid_s, grid_l, tap_buf, tile, b, up, sums=sums):
+        cx = fetch_into(dpre, up, 6)
+        flush()
+        sums = sums + finish_u(1, guo1) + finish_s(2, gsh2)
+        totals.run(4, jnp.broadcast_to(sums, (4, 128)))
+        spatial(0, gs1, taps1, (grid_s, grid_l), tap_buf, tile)
+        cx.wait()
+
+        def rows(group, r0, c):
+            dx[pl.ds(r0, 80), :] = rows_of_grid(s, (grid_s, grid_l), group, r0) + up[pl.ds(r0, 80), :]
+            return c
+
+        chunks(s, 80, rows)
+        flush()
+        return sums + finish_s(0, gsh1)
+
+    sums = pl.run_scoped(final, *spatial_types())
+    square[...] = totals.run(3, jnp.broadcast_to(sums, (4, 128)))
+
+
+def backward_call(s, saved, norm, live, inverse):
+    any_, vmem, smem = (pl.BlockSpec(memory_space=m) for m in (pl.ANY, pltpu.VMEM, pltpu.SMEM))
+    S, V, dma = jax.ShapeDtypeStruct, pltpu.VMEM, pltpu.SemaphoreType.DMA
+    m, d, mid, nb, kw = s.m, s.d, s.mid, s.batches, s.kw
+    half = nb // 2
+    outs = (S((m, d), F32), S((2, kw // 2, s.nb), F32), S((2, kw // 2, s.nb), F32),
+            S((s.ur, s.uc), F32), S((s.ur, s.uc), F32), S((2, 2 * (mid + d)), F32), S((4, 128), F32))
+    rows = nb * s.nb
+    scratch = [
+        V((4, 2, rows, kw), BF), V((4, rows, kw), BF), V((half * s.nb, kw), BF), V((half * s.nb, kw), BF),
+        V((rows, kw), BF), V((rows, kw), BF), V((rows, kw), BF), V((rows, kw), BF),
+        V((3 * mid, d), BF), V((4, s.ur, d), BF), V((s.ur, d // 2), BF), V((s.ur, d // 2), BF),
+        V((s.ur, d), BF), V((s.ur, d), BF), V((s.ur, d), BF), V((s.ur, d), BF),
+        V((m, mid), BF), V((mid, m), BF), V((3, m, d), BF), V((kw, s.nb), F32),
+        V((5, s.slots, 4, mid), F32), V((5, nb, 4, mid), F32),
+        dma((8,)), dma((4,)), dma((9, 3)), dma((2, 2)), dma((2, 2)),
+        dma((4, 4)), dma((4, 4)), dma((4, 5, nb)), dma((4, 5, nb)), dma((2,)), dma((2,)),
+        dma((5, s.slots)), dma((5, s.slots)), dma((5, nb)), dma((5, nb)),
+    ]
+    return pl.pallas_call(
+        functools.partial(backward_kernel, s),
+        out_shape=outs,
+        in_specs=[any_] * 13 + [vmem] * 7 + [smem],
+        out_specs=(vmem,) * 7,
+        scratch_shapes=scratch,
+        compiler_params=pltpu.CompilerParams(
+            collective_id=1, has_side_effects=True, vmem_limit_bytes=63 * 2**20
+        ),
+        name="backward",
+    )(*saved, norm, live, inverse)
+
+
 def body(batches, slots, *args):
     x_small, x_large = args[0], args[1]
-    plain = plain_body(*args)
     if not fits(x_small.shape, x_large.shape, batches, slots):
-        return plain
-    fast = fast_body(Shape(x_small.shape, x_large.shape, batches, slots), *args)
-    return tuple(fast[:2]) + tuple(plain[2:])
-
-
-def fast_body(s, x_small, x_large, grad_small, grad_large, clip_counts, first_spatial, first_temporal,
-              second_spatial, second_temporal, norm_params, *states):
+        return plain_body(*args)
+    return fast_body(Shape(x_small.shape, x_large.shape, batches, slots), *args)
+
+
+def fast_body(
+    s,
+    x_small,
+    x_large,
+    grad_small,
+    grad_large,
+    clip_counts,
+    first_spatial,
+    first_temporal,
+    second_spatial,
+    second_temporal,
+    norm_params,
+    first_spatial_momentum,
+    first_temporal_momentum,
+    second_spatial_momentum,
+    second_temporal_momentum,
+    norm_momentum,
+    first_spatial_variance,
+    first_temporal_variance,
+    second_spatial_variance,
+    second_temporal_variance,
+    norm_variance,
+):
     z = lax.axis_index("batch")
     slots = jnp.arange(s.clips, dtype=jnp.int32)
     counts = lax.dynamic_index_in_dim(clip_counts, z, 1, keepdims=False)
     live = (slots[None, :] < counts[:, None]).astype(F32)[:, :, None]
     totals = jnp.sum(clip_counts, axis=1).astype(F32) * (s.slots * jnp.array(s.cells, F32))
+    inverse = 1.0 / totals
     x = cell_major(s, x_small, x_large)
     grad = cell_major(s, grad_small, grad_large)
     res = forward_call(
         s, x, grad, halves(s, first_spatial), first_temporal.astype(BF), halves(s, second_spatial),
-        second_temporal.astype(BF), norm_params, live, 1.0 / totals,
+        second_temporal.astype(BF), norm_params, live, inverse,
     )
     out_small, out_large = clip_major(s, res[12])
-    return (out_small, out_large) + tuple(res)
+    saved = res[:12] + res[13:]
+    dx, gs1, gs2, gu1, gu2, grad_params, square = backward_call(s, saved, norm_params, live, inverse)
+    in_small, in_large = clip_major(s, dx)
+
+    def whole(g):
+        return g.transpose(1, 0, 2).reshape(g.shape[1], 2 * g.shape[2])
+
+    grad_norm = jnp.sqrt(jnp.sum(square[0]) + jnp.sum(grad_params * grad_params))
+    factor = THRESHOLD / jnp.maximum(grad_norm, THRESHOLD)
+    one = adamw(first_spatial, whole(gs1), first_spatial_momentum, first_spatial_variance, factor,
+                WEIGHT_RATE, WEIGHT_DECAY)
+    two = adamw(first_temporal, gu1, first_temporal_momentum, first_temporal_variance, factor,
+                WEIGHT_RATE, WEIGHT_DECAY)
+    three = adamw(second_spatial, whole(gs2), second_spatial_momentum, second_spatial_variance, factor,
+                  WEIGHT_RATE, WEIGHT_DECAY)
+    four = adamw(second_temporal, gu2, second_temporal_momentum, second_temporal_variance, factor,
+                 WEIGHT_RATE, WEIGHT_DECAY)
+    norms = adamw(norm_params, grad_params, norm_momentum, norm_variance, factor, NORM_RATE, 0.0)
+    return (out_small, out_large, in_small, in_large, grad_norm) + one + two + three + four + norms
 
 
 def solution(mesh):

time: 1780 us -> 736 us (0.41)
  blocking collectives: 472 us -> 0 us
  local copies, waits for them, and re-layouts: 414 us -> 15.9 us
  Pallas kernels: 370 us -> 692 us
  matrix products: 228 us -> 0 us
  other arithmetic: 152 us -> 17.1 us
  waiting for transfers between devices: 85.2 us -> 0 us
  starting transfers between devices: 21.2 us -> 0 us
  between operations: 24.3 us -> 3.82 us
    psum x9 -> x0, blocking collectives: 429 us -> none  [the longest x4 221 us: norm_forward_pass(): lax.psum((running_sums, squared_values), ('batch', 'tm'))]
    pallas_call x0 -> x1, Pallas kernels: none -> 359 us  [backward_call(): pl.pallas_call(functools.partial(backward_kernel, s), out_shape=outs, in_...]
    dot_general x18 -> x0, matrix products: 228 us -> none  [the longest x6 86.1 us: reduce_weight(): lax.dot_general(left, right, (((0,), (0,)), ((), ())), preferred_element_...]
    unnamed x532 -> x48, local copies, waits for them, and re-layouts: 120 us -> 9.87 us
    concatenate x55 -> x0, local copies, waits for them, and re-layouts: 88.2 us -> none  [the longest x44 58 us: spatial_taps(): jnp.concatenate(pieces, axis=-1)]
    all_gather x6 -> x0, waiting for transfers between devices: 73.2 us -> none  [the longest x1 36.7 us: plain_body(): lax.all_gather(columns[0], 'tm', axis=0, tiled=True)]
    convert_element_type x17 -> x0, other arithmetic: 72.1 us -> none  [the longest x2 18.3 us: plain_body(): grad_conv_four = grad_conv_four.astype(jnp.bfloat16)]
    slice x66 -> x0, local copies, waits for them, and re-layouts: 58.1 us -> none  [the longest x36 51.1 us: spatial_taps(): padded[:, :, row:row + side, column:column + side, :]]
  transfers between devices with their start and end apart: 22 -> 0, of which waited for: 3 -> 0; matrix products, arithmetic and copies ran while one was open for 38% -> 0% of each run, Pallas kernels for 21% -> 0%
where the time goes in v2:
time: 736 us; the launch traced here: 729 us
  Pallas kernels  692 us (94%)
  other arithmetic  17.1 us (2%)
  local copies, waits for them, and re-layouts  15.9 us (2%)
    pallas_call x1, Pallas kernels, backward_call(): pl.pallas_call(functools.partial(backward_kernel, s), out_shape=outs, in_...  359 us
    pallas_call x1, Pallas kernels, forward_call(): pl.pallas_call(functools.partial(forward_kernel, s), out_shape=outs, in_s...  333 us

profile of v2, /device:TPU:0, one launch (start us, length us, event | category | flops | bytes accessed | tf_op | source)
XLA Modules:
  0.0 728.6 jit_solution(6737886603228838418)
XLA Ops:
  0.7 0.0 copy-start
  0.7 0.0 copy-start.7
  0.7 0.0 copy-start.1
  0.7 3.3 fusion.3
  4.0 0.0 copy-start.8
  4.0 0.0 copy-done
  4.1 1.1 copy.45
  5.2 0.0 copy-done.7
  5.2 0.7 convert_element_type.29.refs_3_
  5.8 0.0 copy-done.1
  5.9 1.1 copy.46
  6.9 0.0 copy-done.8
  6.9 0.7 convert_element_type.31.refs_5_
  7.6 0.0 copy-done.20
  7.6 0.2 dynamic-slice_reduce_fusion
  7.8 0.7 fusion.13.refs_7_.refs_19_
  8.4 0.1 reduce_sum.27
  8.6 0.0 copy-done.21
  8.6 0.5 multiply_divide_fusion.refs_8_.refs_20_
  9.1 332.8 %forward.1 = (bf16[4,1152,1152]{2,1,0:T(8,128)(2,1)}, bf16[3456,512]{1,0:T(8,128)(2,1)}, bf16[4,1152,1152]{2,1,0:T(8,128)(2,1)}, bf16[3456,512]{1,0:T(8,128)(2,1...) custom-call(bf16[1200,512]{1,0:T(8,128)(2,1)} %get-tuple-element.107, ...), custom_call_target="tpu_custom_call" | custom-call | tf_op jit(solution)/shard_map/forward/pallas_call | solution.py:1126
  341.9 0.0 copy-start.4
  341.9 1.3 slice_bitcast_fusion.3
  343.2 1.7 copy.49
  344.9 0.0 copy-done.4
  344.9 0.1 slice_bitcast_fusion.1
  345.1 2.8 copy.50
  347.9 359.0 %backward.1 = (f32[1200,512]{1,0:T(8,128)}, f32[2,576,144]{2,1,0:T(8,128)}, f32[2,576,144]{2,1,0:T(8,128)}, f32[432,128]{1,0:T(8,128)}, f32[432,128]{1,0:T(8,128)}, /*index=5*/f32[2,3328]{1,0:T(2,128)}, f32[4,128]{1,0:T(4,128)}) custom-call(bf16[4,1152,1152]{2,1,0:T(8,128)(2,1)} %get-tuple-element.47.refs_0_, bf16[3456,512]{1,0:T(8,128)(2,1)} %get-tuple-element.48.refs_1_, ...), custom_call_target="tpu_custom_call" | custom-call | tf_op jit(solution)/shard_map/backward/pallas_call | solution.py:1651
  706.9 0.0 copy-start.3
  706.9 1.3 slice_bitcast_fusion.2
  708.3 1.7 copy.51
  710.0 0.0 copy-done.3
  710.0 0.1 slice_bitcast_fusion
  710.1 0.0 copy-start.17
  710.1 0.0 copy-start.6
  710.1 2.8 copy.52
  713.0 1.3 slice_reduce_fusion
  714.3 0.0 copy-done.17
  714.3 0.6 multiply_reduce_fusion
  716.3 0.0 copy-done.6
  716.3 0.1 multiply_bitcast_fusion.1
  716.4 0.4 copy.47
  716.8 0.0 copy-start.5
  716.8 3.2 multiply_subtract_fusion.1
  720.0 0.0 copy-done.11
  720.0 0.0 copy-done.12
  720.0 0.0 copy-done.16
  720.0 0.9 multiply_subtract_fusion.3
  720.9 0.0 copy-done.5
  720.9 0.1 multiply_bitcast_fusion
  721.0 0.4 copy.48
  721.4 0.7 copy-done.2
  722.0 0.0 copy-start.10
  722.1 0.0 copy-start.18
  722.1 0.0 copy-start.19
  722.1 3.2 multiply_subtract_fusion
  725.3 0.0 copy-done.9
  725.3 0.0 copy-done.13
  725.3 0.0 copy-done.14
  725.3 0.0 copy-done.15
  725.3 0.9 multiply_subtract_fusion.2
  726.3 0.0 copy-done.10
  726.3 0.0 copy-done.18
  726.3 0.0 copy-done.19
  726.3 0.7 multiply_subtract_fusion.4
  (12 shorter events, 0.1 us)
Async XLA Ops:
  0.7 3.4 copy-start
  0.7 4.5 copy-start.7
  0.7 5.1 copy-start.1
  4.0 2.9 copy-start.8
  4.0 3.6 copy-start.20
  4.0 4.5 copy-start.21
  341.9 3.1 copy-start.4
  706.9 3.1 copy-start.3
  710.1 4.1 copy-start.17
  710.1 6.1 copy-start.6
  716.7 3.2 copy-start.11
  716.7 3.2 copy-start.12
  716.7 3.2 copy-start.16
  716.8 4.2 copy-start.5
  720.9 1.1 copy-start.2
  722.0 3.3 copy-start.9
  722.0 3.3 copy-start.13
  722.0 3.3 copy-start.14
  722.0 3.3 copy-start.15
  722.0 4.2 copy-start.10
  722.1 4.2 copy-start.18
  722.1 4.2 copy-start.19

commit v3 on v2

--- a/solution.py
+++ b/solution.py
@@ -1,3 +1,4 @@
+import contextlib
 import functools
 import math
 
@@ -469,6 +470,7 @@
 MESH_ID = pl.DeviceIdType.MESH
 NT_DIMS = (((1,), (1,)), ((), ()))
 NN_DIMS = (((1,), (0,)), ((), ()))
+scope = lambda name: contextlib.nullcontext()
 UP, DOWN, ACROSS, ALONG, TWIN = range(5)
 
 
@@ -607,12 +609,15 @@
         pl.when(p.z - k >= 0)(lambda: fn(p.z - k))
         pl.when(p.z + k < p.batches)(lambda: fn(p.z + k))
 
-    def start(self):
+    def start_line(self):
         p = self.p
         pl.when(p.z < p.batches - 1)(lambda: self.copy(UP, 0, p.z, self.own).start())
         pl.when(p.z > 0)(lambda: self.copy(DOWN, 0, p.z, self.own).start())
-        for way in (ACROSS, ALONG, TWIN):
-            self.copy(way, 0, p.z, self.own).start()
+        self.copy(TWIN, 0, p.z, self.own).start()
+
+    def start_plane(self):
+        for way in (ACROSS, ALONG):
+            self.copy(way, 0, self.p.z, self.own).start()
 
     def hop(self, k):
         p = self.p
@@ -620,30 +625,52 @@
         def below(b):
             self.wait(0, b)
             pl.when(p.z < p.batches - 1)(lambda: self.copy(UP, 0, b).start())
-            for way in (ACROSS, ALONG, TWIN):
-                self.copy(way, 0, b).start()
+            self.copy(TWIN, 0, b).start()
 
         def above(b):
             self.wait(0, b)
             pl.when(p.z > 0)(lambda: self.copy(DOWN, 0, b).start())
-            for way in (ACROSS, ALONG, TWIN):
-                self.copy(way, 0, b).start()
+            self.copy(TWIN, 0, b).start()
 
         pl.when(p.z - k >= 0)(lambda: below(p.z - k))
         pl.when(p.z + k < p.batches)(lambda: above(p.z + k))
 
-    def plane(self, k):
+    def spread(self, k, ways=(ACROSS, ALONG)):
+        def one(b):
+            for way in ways:
+                self.copy(way, 0, b).start()
+
+        self.at(k, one)
+
+    def across(self, k):
+        self.spread(k, (ACROSS,))
+
+    def along(self, k):
+        self.spread(k, (ALONG,))
+
+    def from_side(self, k):
         half = self.p.batches // 2
 
         def one(b):
             self.wait(1, b)
             pl.when(b < half)(lambda: self.copy(ALONG, 1, b).start())
             self.copy(TWIN, 1, b).start()
+
+        self.at(k, one)
+
+    def from_deep(self, k):
+        half = self.p.batches // 2
+
+        def one(b):
             self.wait(2, b)
             pl.when(b >= half)(lambda: self.copy(ACROSS, 2, b).start())
             self.copy(TWIN, 2, b).start()
 
         self.at(k, one)
+
+    def plane(self, k):
+        self.from_side(k)
+        self.from_deep(k)
 
     def far(self, k):
         def one(b):
@@ -659,16 +686,15 @@
 
         lax.fori_loop(0, self.p.batches, body, 0)
 
-    def steps(self):
-        batches = self.p.batches
-        order = [self.start]
-        for k in range(batches):
-            if k:
-                order.append(functools.partial(self.hop, k))
-                order.append(functools.partial(self.far, k - 1))
-            order.append(functools.partial(self.plane, k))
-        order.append(functools.partial(self.far, batches - 1))
-        return order
+    def act(self, word):
+        kind = word[0]
+        if kind == "z":
+            self.start_line()
+        elif kind == "x":
+            self.start_plane()
+        else:
+            {"h": self.hop, "s": self.spread, "a": self.across, "l": self.along, "p": self.plane, "f": self.far,
+             "u": self.from_side, "v": self.from_deep}[kind](int(word[1]))
 
     def finish(self):
         p = self.p
@@ -686,6 +712,74 @@
             return 0
 
         lax.fori_loop(0, p.batches, body, 0)
+
+
+class Halo:
+    def __init__(self, place, stage, src, dst, relay, sems, cut):
+        self.p, self.n, self.src, self.dst, self.buf, self.cut = place, stage, src, dst, relay, cut
+        self.send_sem, self.recv_sem, self.pass_send, self.pass_recv = sems
+        self.mid = place.slots // 2
+
+    def part(self, ref, piece):
+        rows = ref.shape[0]
+        return ref.at[pl.ds(0, self.cut)] if piece == 0 else ref.at[pl.ds(self.cut, rows - self.cut)]
+
+    def piece(self, side, piece, to):
+        return send(self.part(self.src(side), piece), self.part(self.dst(side), piece),
+                    self.send_sem.at[self.n, side, piece], self.recv_sem.at[self.n, side, piece],
+                    (self.p.z, to))
+
+    def detour(self, side):
+        to = self.p.slots - 1 if side == 0 else 0
+        return send(self.part(self.src(side), 1), self.buf, self.send_sem.at[self.n, side, 1],
+                    self.pass_recv.at[self.n], (self.p.z, to))
+
+    def passing(self, side):
+        to = self.mid if side == 0 else self.mid - 1
+        return send(self.buf, self.part(self.dst(side), 1), self.pass_send.at[self.n],
+                    self.recv_sem.at[self.n, side, 1], (self.p.z, to))
+
+    def sends(self, side):
+        return self.p.t < self.p.slots - 1 if side == 0 else self.p.t > 0
+
+    def receives(self, side):
+        return self.p.t > 0 if side == 0 else self.p.t < self.p.slots - 1
+
+    def start(self, side):
+        p = self.p
+        to = p.t + 1 if side == 0 else p.t - 1
+        crossing = p.t == (self.mid - 1 if side == 0 else self.mid)
+
+        @pl.when(self.sends(side))
+        def _():
+            pl.when(crossing)(lambda: self.detour(side).start())
+            self.piece(side, 0, to).start()
+            pl.when(jnp.logical_not(crossing))(lambda: self.piece(side, 1, to).start())
+
+    def relay(self):
+        p = self.p
+        for side, t in ((0, p.slots - 1), (1, 0)):
+            @pl.when(p.t == t)
+            def _(side=side):
+                send(self.buf, self.buf, self.pass_send.at[self.n], self.pass_recv.at[self.n],
+                     p.device(TWIN)).wait_recv()
+                self.passing(side).start()
+
+    def wait(self, side):
+        @pl.when(self.receives(side))
+        def _():
+            for piece in range(2):
+                self.piece(side, piece, self.p.twin).wait_recv()
+
+    def done(self):
+        p = self.p
+        for side in range(2):
+            @pl.when(self.sends(side))
+            def _(side=side):
+                for piece in range(2):
+                    self.piece(side, piece, p.twin).wait_send()
+        for side, t in ((0, p.slots - 1), (1, 0)):
+            pl.when(p.t == t)(lambda side=side: self.passing(side).wait_send())
 
 
 def sigmoid(v):
@@ -709,12 +803,13 @@
         self.nb = self.mid // (2 * batches)
         self.ur = 3 * self.mid // slots
         self.uc = self.d // batches
+        self.cut = -(-self.m // 32) * 16
 
 
 def fits(x_small, x_large, batches, slots):
     s = Shape(x_small, x_large, batches, slots)
     return (
-        s.clips == 8 and x_small[1] == 1 and slots == 8 and batches >= 2 and batches % 2 == 0
+        s.clips == 8 and x_small[1] == 1 and slots == 8 and batches == 4
         and all(side * side == cells for side, cells in zip(s.sides, s.cells))
         and all(r % 80 == 0 for r in s.rows)
         and s.kw % 128 == 0 and s.mid % (32 * batches) == 0 and s.ur % 16 == 0 and s.uc % 128 == 0
@@ -830,10 +925,10 @@
 
 def forward_kernel(s, *refs):
     (x, grad, sw1, uw1, sw2, uw2, norm, live_ref, inverse,
-     gs1, gu1, gs2, gu2, taps1_o, taps2_o, xh1_o, xh2_o, xh3_o, xh4_o, z1_o, z3_o, out, dpre,
+     gs1, gu1, gs2, gu2, taps1_o, taps2_o, xh1_o, xh2_o, xh3_o, xh4_o, z1_o, z3_o, out_o, dpre_o,
      r1_o, r2_o, r3_o, r4_o, last_o,
      tb1, tb2, own1, own2, wb, wub, taps, a, z, grid_s, grid_l, b, hs, hr, planes, lines,
-     ag_send, ag_recv, ag_twin, tb_send, tb_recv, local, load, hs_send, hs_recv,
+     ag_send, ag_recv, ag_twin, tb_send, tb_recv, local, load, hs_send, hs_recv, pass_send, pass_recv, relay, out, dpre,
      pl_send, pl_recv, ln_send, ln_recv) = refs
     p = Place(s.batches, s.slots)
     live = [live_ref[g] for g in range(2)]
@@ -845,7 +940,8 @@
     def gain_bias(n):
         return norm[0:1, bounds[n] : bounds[n + 1]], norm[1:2, bounds[n] : bounds[n + 1]]
 
-    p.greet()
+    with scope("greet"):
+        p.greet()
 
     def twin_copy(n, src, dst):
         return send(
@@ -882,28 +978,21 @@
         g = gather[n]
         return pltpu.make_async_copy(g.own, g.whole.at[g.block(p.slab, p.core, p.z)], local.at[n])
 
-    twin_wait(0, sw1, tb1)
-    own1[...] = tb1[...].T
-    queue = [(0, step) for step in gather[0].steps()]
-    queue.pop(0)[1]()
-    keep_own(0).start()
-    twin_wait(1, sw2, tb2)
-    own2[...] = tb2[...].T
+    def go(words):
+        with scope("gather " + words):
+            for word in words.split():
+                gather[int(word[0])].act(word[1:])
+
+    with scope("own"):
+        twin_wait(0, sw1, tb1)
+        own1[...] = tb1[...].T
+        go("0z 0x")
+        keep_own(0).start()
+        twin_wait(1, sw2, tb2)
+        own2[...] = tb2[...].T
     keep_own(1).start()
     keep_own(2).start()
     keep_own(3).start()
-    for n in (1, 2, 3):
-        queue += [(n, step) for step in gather[n].steps()]
-
-    def tick(count):
-        for _ in range(count):
-            if queue:
-                queue.pop(0)[1]()
-
-    def flush(n):
-        while queue and queue[0][0] <= n:
-            queue.pop(0)[1]()
-
     for side, edge in ((0, 0), (1, p.slots - 1)):
         @pl.when(p.t == edge)
         def _(side=side):
@@ -921,56 +1010,55 @@
         grid_of_rows(s, grids, group, r0, x[pl.ds(r0, 80), :].astype(F32))
         return c
 
-    chunks(s, 80, x_rows)
-    clear_pad_cells(s, grids)
-    build_taps(s, grids, taps)
+    with scope("taps x"):
+        chunks(s, 80, x_rows)
+        clear_pad_cells(s, grids)
+        build_taps(s, grids, taps)
     taps_copy = pltpu.make_async_copy(taps, taps1_o, local.at[4])
     taps_copy.start()
 
-    def slab_load(whole, rel):
-        return pltpu.make_async_copy(whole.at[p.rel[rel]], wb.at[rel], load.at[rel])
-
-    def conv_slab(rel):
-        for lo, width in wide_cuts(mid):
+    def slab_load(whole, rel, half):
+        lo, width = wide_cuts(mid)[half]
+        rows = pl.ds(lo, width)
+        return pltpu.make_async_copy(whole.at[p.rel[rel], rows], wb.at[rel, rows], load.at[rel, half])
+
+    def conv_slab(whole, rel, first):
+        for half, (lo, width) in enumerate(wide_cuts(mid)):
+            slab_load(whole, rel, half).wait()
             y = lax.dot_general(taps[p.rel[rel]], wb[rel, lo : lo + width, :], NT_DIMS, preferred_element_type=F32)
-            if rel == 0:
+            if first:
                 a[:, lo : lo + width] = y
             else:
                 a[:, lo : lo + width] += y
 
-    def spatial(n, whole, spare):
+    def spatial(n, whole, order, words):
         g = gather[n]
-        while queue and queue[0][0] <= n and len([q for q in queue if q[0] <= n]) > 1:
-            queue.pop(0)[1]()
-        g.twins(0)
-        if n == 0:
-            keep_own(0).wait()
-        else:
-            keep_own(2).wait()
-        slab_load(whole, 0).start()
-        g.twins(1)
-        slab_load(whole, 1).start()
-        g.twins(2)
-        slab_load(whole, 2).start()
-        slab_load(whole, 0).wait()
-        conv_slab(0)
-        flush(n)
-        g.twins(3)
-        slab_load(whole, 3).start()
-        for rel in (1, 2, 3):
-            tick(spare)
-            slab_load(whole, rel).wait()
-            conv_slab(rel)
+        keep_own(n).wait()
+        for i, rel in enumerate(order):
+            go(words[2 * i])
+            with scope("twins"):
+                g.twins(rel)
+            for half in range(2):
+                slab_load(whole, rel, half).start()
+            go(words[2 * i + 1])
+            with scope("slab"):
+                conv_slab(whole, rel, i == 0)
 
     def stats(load_rows, width):
         return sums_of(s, load_rows, live, width)
 
-    def wide_norm(index, n, zo, xo, ro, sem):
+    def wide_norm(index, n, zo, xo, ro, sem, words, weight):
         def load_rows(group, r0, size):
             v = a[pl.ds(r0, size), :]
             return v, v * v
 
-        total = totals.run(index, stats(load_rows, mid))
+        with scope("wide stats"):
+            local_sums = stats(load_rows, mid)
+        go(words[0])
+        with scope("total"):
+            total = totals.run(index, local_sums)
+        weight_load(*weight)
+        go(words[1])
         mean, scale = moments(total, inv, mid)
         ro[...] = jnp.concatenate(scale, axis=0)
         gain, bias = gain_bias(n)
@@ -982,7 +1070,8 @@
             z[pl.ds(r0, 16), :] = (h * sigmoid(h)).astype(BF)
             return c
 
-        chunks(s, 16, rows)
+        with scope("wide norm"):
+            chunks(s, 16, rows)
         zero_padding(s, z, mid)
         xc = pltpu.make_async_copy(a, xo, local.at[sem])
         zc = pltpu.make_async_copy(z, zo, local.at[sem + 1])
@@ -991,28 +1080,34 @@
         return xc, zc
 
     def u_load(n, whole):
-        return pltpu.make_async_copy(whole, wub, load.at[4 + n])
-
-    def halo(n, side):
-        to = p.t + 1 if side == 0 else p.t - 1
-        return send(hs.at[side], hr.at[side], hs_send.at[n, side], hs_recv.at[n, side], (p.z, to))
-
-    def temporal(n, index, between):
-        flush(index)
-        for rel in range(4):
-            gather[index].twins(rel)
-        keep_own(index).wait()
-        load_w = u_load(n, gather[index].whole)
-        load_w.start()
-        load_w.wait()
-        hs[0] = jnp.dot(z[...], wub[:mid, :], preferred_element_type=F32).astype(BF)
-        pl.when(p.t < p.slots - 1)(lambda: halo(n, 0).start())
-        hs[1] = jnp.dot(z[...], wub[2 * mid :, :], preferred_element_type=F32).astype(BF)
-        pl.when(p.t > 0)(lambda: halo(n, 1).start())
-        b[...] = jnp.dot(z[...], wub[mid : 2 * mid, :], preferred_element_type=F32)
-        between()
-        pl.when(p.t > 0)(lambda: halo(n, 0).wait_recv())
-        pl.when(p.t < p.slots - 1)(lambda: halo(n, 1).wait_recv())
+        return pltpu.make_async_copy(whole, wub, load.at[4, n])
+
+    halos = [
+        Halo(p, n, lambda side: hs.at[side], lambda side: hr.at[side], relay,
+             (hs_send, hs_recv, pass_send, pass_recv), s.cut)
+        for n in range(2)
+    ]
+
+    def weight_load(n, index):
+        with scope("u weight"):
+            for rel in range(4):
+                gather[index].twins(rel)
+            keep_own(index).wait()
+            u_load(n, gather[index].whole).start()
+
+    def temporal(n, words):
+        with scope("u conv"):
+            u_load(n, gather[1].whole).wait()
+            hs[0] = jnp.dot(z[...], wub[:mid, :], preferred_element_type=F32).astype(BF)
+            halos[n].start(0)
+            hs[1] = jnp.dot(z[...], wub[2 * mid :, :], preferred_element_type=F32).astype(BF)
+            halos[n].start(1)
+            b[...] = jnp.dot(z[...], wub[mid : 2 * mid, :], preferred_element_type=F32)
+        go(words)
+        with scope("halo wait"):
+            halos[n].relay()
+            halos[n].wait(0)
+            halos[n].wait(1)
 
     def narrow_total(index):
         def load_rows(group, r0, size):
@@ -1020,19 +1115,17 @@
             b[pl.ds(r0, size), :] = v
             return v, v * v
 
-        return totals.run(index, stats(load_rows, d))
-
-    def halo_done(n):
-        pl.when(p.t < p.slots - 1)(lambda: halo(n, 0).wait_send())
-        pl.when(p.t > 0)(lambda: halo(n, 1).wait_send())
-
-    spatial(0, gs1, 4)
-    tick(1)
-    xc1, zc1 = wide_norm(0, 0, z1_o, xh1_o, r1_o, 5)
-    tick(2)
-    temporal(0, 1, lambda: tick(2))
+        with scope("narrow stats"):
+            local_sums = stats(load_rows, d)
+        with scope("total"):
+            return totals.run(index, local_sums)
+
+    go("1z 0h1 0s1 0p0 1h1 0h2 0s2 0p1 0f0 1h2 0h3 0s3 1h3")
+    spatial(0, gs1, (0, 1, 2, 3), ("0p2 0f1", "", "0p3", "1x 1s1 1s2 1s3", "0f2", "", "0f3 2z", "1p0 1f0"))
+    xc1, zc1 = wide_norm(0, 0, z1_o, xh1_o, r1_o, 5, ("1p1 1f1 1p2 1f2 1p3 1f3", "2x"), (0, 1))
+    temporal(0, "2h1 2l1 2h2 2l2 2h3 2l3")
     total = narrow_total(1)
-    tick(1)
+    go("2a1 2a2 2a3 3z")
     mean2, scale2 = moments(total, inv, d)
     r2_o[...] = jnp.concatenate(scale2, axis=0)
     gain2, bias2 = gain_bias(1)
@@ -1044,24 +1137,23 @@
         grid_of_rows(s, grids, group, r0, (h * sigmoid(h)).astype(BF).astype(F32))
         return c
 
-    chunks(s, 80, second)
-    clear_pad_cells(s, grids)
+    with scope("norm2"):
+        chunks(s, 80, second)
+        clear_pad_cells(s, grids)
     xc2 = pltpu.make_async_copy(b, xh2_o, local.at[7])
     xc2.start()
-    halo_done(0)
-    tick(2)
+    halos[0].done()
     taps_copy.wait()
-    build_taps(s, grids, taps)
+    with scope("taps z2"):
+        build_taps(s, grids, taps)
     taps_copy2 = pltpu.make_async_copy(taps, taps2_o, local.at[8])
     taps_copy2.start()
     xc1.wait()
-    spatial(2, gs2, 4)
-    tick(2)
+    spatial(2, gs2, (0, 2, 1, 3), ("", "2v0 2v1 2v2 2v3", "2u0 2u1 3h1", "", "2u2 2u3 3h2", "3x 3s1 3s2", "2f0 2f1 2f2 2f3 3h3 3s3", ""))
     zc1.wait()
-    xc3, zc3 = wide_norm(2, 2, z3_o, xh3_o, r3_o, 9)
-    tick(2)
+    xc3, zc3 = wide_norm(2, 2, z3_o, xh3_o, r3_o, 9, ("3p0 3f0 3p1 3f1 3p2 3f2 3p3 3f3", ""), (1, 3))
     xc2.wait()
-    temporal(1, 3, lambda: None)
+    temporal(1, "")
     total = narrow_total(3)
     mean4, scale4 = moments(total, inv, d)
     r4_o[...] = jnp.concatenate(scale4, axis=0)
@@ -1078,22 +1170,30 @@
         dpre[pl.ds(r0, 80), :] = up
         return c
 
-    chunks(s, 80, last)
-    zero_padding(s, dpre, d)
+    with scope("norm4"):
+        chunks(s, 80, last)
+        zero_padding(s, dpre, d)
     xc4 = pltpu.make_async_copy(b, xh4_o, local.at[11])
     xc4.start()
+    outs = [pltpu.make_async_copy(out, out_o, local.at[12]), pltpu.make_async_copy(dpre, dpre_o, local.at[13])]
+    for c in outs:
+        c.start()
 
     def last_rows(group, r0, size):
         v = dpre[pl.ds(r0, size), :]
         return v, v * b[pl.ds(r0, size), :]
 
-    last_o[...] = totals.run(4, stats(last_rows, d))
-    halo_done(1)
-    for g in gather:
-        g.finish()
+    with scope("last stats"):
+        local_sums = stats(last_rows, d)
+    with scope("total"):
+        last_o[...] = totals.run(4, local_sums)
+    halos[1].done()
+    with scope("finish"):
+        for g in gather:
+            g.finish()
     for n, src, dst in ((0, sw1, tb1), (1, sw2, tb2)):
         twin_copy(n, src, dst).wait_send()
-    for c in (taps_copy2, zc3, xc3, xc4):
+    for c in (taps_copy2, zc3, xc3, xc4, *outs):
         c.wait()
 
 
@@ -1108,7 +1208,7 @@
     zs = S((m, mid), BF)
     outs = (gs, gu, gs, gu, taps, taps, wide, narrow, wide, narrow, zs, zs, narrow, narrow,
             S((2, mid), F32), S((2, d), F32), S((2, mid), F32), S((2, d), F32), S((4, d), F32))
-    specs = (any_,) * 12 + (vmem,) * 7
+    specs = (any_,) * 14 + (vmem,) * 5
     dma, V = pltpu.SemaphoreType.DMA, pltpu.VMEM
     nb = s.batches
     n_sums = 5
@@ -1119,8 +1219,9 @@
         V((s.sides[0] + 2, s.sides[0] + 2, 8, d), F32), V((s.sides[1] + 2, s.sides[1] + 2, 8, d), F32),
         V((m, d), F32), V((2, m, d), BF), V((2, m, d), BF),
         V((n_sums, s.slots, 4, mid), F32), V((n_sums, nb, 4, mid), F32),
-        dma((4, 5, 4, nb)), dma((4, 4, nb)), dma((4, 4, nb)), dma((2,)), dma((2,)), dma((12,)), dma((6,)),
-        dma((2, 2)), dma((2, 2)),
+        dma((4, 5, 4, nb)), dma((4, 4, nb)), dma((4, 4, nb)), dma((2,)), dma((2,)), dma((14,)), dma((5, 2)),
+        dma((2, 2, 2)), dma((2, 2, 2)), dma((2,)), dma((2,)), V((m - s.cut, d), BF),
+        V((m, d), F32), V((m, d), F32),
         dma((n_sums, s.slots)), dma((n_sums, s.slots)), dma((n_sums, nb)), dma((n_sums, nb)),
     ]
     return pl.pallas_call(
@@ -1272,6 +1373,21 @@
 
             self.fall_copy(b).start()
 
+    def tail(self):
+        p = self.p
+
+        @pl.when(p.z < self.half)
+        def _():
+            for b in range(p.batches - 1, -1, -1):
+                self.collect(b)
+                self.chain(b)
+
+        @pl.when(p.z >= self.half)
+        def _():
+            for b in range(p.batches):
+                self.collect(b)
+                self.chain(b)
+
     def result(self):
         p = self.p
         pl.when(p.z > 0)(lambda: self.arrive(self.RISE, p.z, self.cut(self.ru, p.z)))
@@ -1304,13 +1420,111 @@
             pl.when(p.z < b)(lambda b=b: self.rise_copy(b).wait_send())
             pl.when(p.z > b)(lambda b=b: self.fall_copy(b).wait_send())
 
-    def steps(self):
-        part = functools.partial
-        out = [part(self.join, rel) for rel in (3, 1, 2, 0)]
-        out += [part(self.relay, b) for b in self.order()]
-        for b in self.order():
-            out += [part(self.collect, b), part(self.chain, b)]
-        return out
+    def act(self, word):
+        if word == "t":
+            self.tail()
+        else:
+            {"j": self.join, "r": self.relay}[word[0]](int(word[1]))
+
+
+class LineScatter(Scatter):
+    def rise(self, rel, b):
+        return send(self.own(rel, b), self.cut(self.ru.at[rel], b), self.line_s.at[self.n, 0, rel, b],
+                    self.line_r.at[self.n, 0, rel, b], self.p.device(UP))
+
+    def fall(self, rel, b):
+        return send(self.own(rel, b), self.cut(self.rd.at[rel], b), self.line_s.at[self.n, 1, rel, b],
+                    self.line_r.at[self.n, 1, rel, b], self.p.device(DOWN))
+
+    def landed(self, way, rel, b):
+        buf = (self.ru, self.rd)[way]
+        ref = self.cut(buf.at[rel], b)
+        send(ref, ref, self.line_s.at[self.n, way, rel, b], self.line_r.at[self.n, way, rel, b],
+             self.p.device(TWIN)).wait_recv()
+        return ref
+
+    def join(self, rel):
+        p = self.p
+        self.twin_copy(rel).wait_recv()
+        add_into(self.part(rel, p.core), self.tr.at[rel], self.rows, self.step)
+
+    def ends(self, up, down):
+        p = self.p
+
+        @pl.when(p.z == 0)
+        def _():
+            for rel in (3, 1, 2, 0):
+                self.rise(rel, up).start()
+
+        @pl.when(p.z == p.batches - 1)
+        def _():
+            for rel in (3, 1, 2, 0):
+                self.fall(rel, down).start()
+
+    def chain(self, stage):
+        p = self.p
+
+        @pl.when(p.z == stage)
+        def _():
+            for b in range(p.batches - 1, stage, -1):
+                for rel in (3, 1, 2, 0):
+                    self.add(self.own(rel, b), self.landed(0, rel, b))
+                    self.rise(rel, b).start()
+
+        @pl.when(p.z == p.batches - 1 - stage)
+        def _():
+            for b in range(p.batches - 1 - stage):
+                for rel in (3, 1, 2, 0):
+                    self.add(self.own(rel, b), self.landed(1, rel, b))
+                    self.fall(rel, b).start()
+
+    def settle(self, rel):
+        p = self.p
+        at = self.own(rel, p.z)
+        pl.when(p.z > 0)(lambda: self.add(at, self.landed(0, rel, p.z)))
+        pl.when(p.z < p.batches - 1)(lambda: self.add(at, self.landed(1, rel, p.z)))
+
+    def cross(self, kind, rel, dst, way):
+        return self.block_copy(kind, 0, self.own(rel, self.p.z), dst, way)
+
+    def corner(self):
+        self.settle(3)
+        self.cross(self.FAR, 3, self.fx, ACROSS).start()
+        self.settle(1)
+        self.cross(self.SIDE, 1, self.rx, ACROSS).start()
+        self.settle(2)
+
+    def turn(self):
+        self.arrive(self.FAR, 0, self.fx)
+        self.add(self.own(2, self.p.z), self.fx)
+        self.cross(self.DEEP, 2, self.ry, ALONG).start()
+        self.settle(0)
+
+    def result(self):
+        self.arrive(self.SIDE, 0, self.rx)
+        self.arrive(self.DEEP, 0, self.ry)
+        return (self.own(0, self.p.z)[...].astype(F32) + self.rx[...].astype(F32) + self.ry[...].astype(F32))
+
+    def sent(self):
+        p = self.p
+        for rel in range(4):
+            self.twin_copy(rel).wait_send()
+            for b in range(p.batches):
+                pl.when(p.z < b)(lambda rel=rel, b=b: self.rise(rel, b).wait_send())
+                pl.when(p.z > b)(lambda rel=rel, b=b: self.fall(rel, b).wait_send())
+        self.cross(self.FAR, 3, self.fx, ACROSS).wait_send()
+        self.cross(self.SIDE, 1, self.rx, ACROSS).wait_send()
+        self.cross(self.DEEP, 2, self.ry, ALONG).wait_send()
+
+    def act(self, word):
+        if word[0] == "j":
+            self.join(int(word[1]))
+        elif word[0] == "k":
+            self.chain(int(word[1]))
+        elif word[0] == "z":
+            self.ends(int(word[1]), int(word[2]))
+        else:
+            {"c": self.corner, "t": self.turn}[word]()
 
 
 def rows_of_grid(s, grids, group, r0):
@@ -1329,10 +1543,10 @@
 def backward_kernel(s, *refs):
     (gs1, gu1, gs2, gu2, taps1, taps2, xh1, xh2, xh3, xh4, z1, z3, dpre,
      r1, r2, r3, r4, last, norm, live_ref, inverse,
-     dx, gsh1, gsh2, guo1, guo2, ng, square,
-     ps, tr, fx, fa, rx, ry, ru, rd, pu, utr, ufx, ufa, urx, ury, uru, urd,
-     nat, flip, d3, turn, planes, lines,
-     load, tap_sem, tile_sem, halo_send, halo_recv, twin_s, twin_r, block_s, block_r, half_s, half_r,
+     dx, gso1, gso2, guo1, guo2, ng, square,
+     ps, tr, fx, fa, rx, ry, ru, rd, pu, utr, ufx, urx, ury, uru, urd, relay,
+     nat, flip, d3, turn, gsh, planes, lines,
+     load, tap_sem, tile_sem, halo_send, halo_recv, pass_send, pass_recv, line_s, line_r, twin_s, twin_r, block_s, block_r, half_s, half_r,
      pl_send, pl_recv, ln_send, ln_recv) = refs
     p = Place(s.batches, s.slots)
     live = [live_ref[g] for g in range(2)]
@@ -1344,17 +1558,12 @@
     def gain_bias(n):
         return norm[0:1, bounds[n] : bounds[n + 1]], norm[1:2, bounds[n] : bounds[n + 1]]
 
-    p.greet()
-    queue = []
-
-    def tick(count):
-        for _ in range(count):
-            if queue:
-                queue.pop(0)()
-
-    def flush():
-        while queue:
-            queue.pop(0)()
+    with scope("greet"):
+        p.greet()
+    def go(words):
+        with scope("reduce " + words):
+            for word in words.split():
+                scatter(int(word[0])).act(word[1:])
 
     def cut_rows(ref, b):
         at = b * s.nb if isinstance(b, int) else pl.multiple_of(b * s.nb, 16)
@@ -1375,7 +1584,9 @@
     def scatter(n):
         if n % 2 == 0:
             return Scatter(p, n, part_s, (tr, fx, fa, rx, ry, ru, rd), cut_rows, s.nb, 48, sems)
-        return Scatter(p, n, part_u, (utr, ufx, ufa, urx, ury, uru, urd), cut_lanes, s.ur, 144, sems)
+        sc = LineScatter(p, n, part_u, (utr, ufx, None, urx, ury, uru, urd), cut_lanes, s.ur, 144, sems)
+        sc.line_s, sc.line_r = line_s, line_r
+        return sc
 
     for side, edge in ((0, p.slots - 1), (2, 0)):
         @pl.when(p.t == edge)
@@ -1422,7 +1633,8 @@
             flip[at, :] = nat[:, at].T
             return 0
 
-        lax.fori_loop(0, mid // 128, body, 0)
+        with scope("transpose"):
+            lax.fori_loop(0, mid // 128, body, 0)
 
     def fetch_into(src, dst, sem):
         c = pltpu.make_async_copy(src, dst, load.at[sem])
@@ -1441,19 +1653,21 @@
         c2.wait()
         norm_back(3, last[...], r4[...], up, xh, narrow_store, 80, d)
 
-    pl.run_scoped(first, pltpu.VMEM((m, d), F32), pltpu.VMEM((m, d), F32))
+    fetch_into(z3, nat, 2)
+    with scope("norm4 back"):
+        pl.run_scoped(first, pltpu.VMEM((m, d), F32), pltpu.VMEM((m, d), F32))
     zero_padding(s, d3.at[1], d)
 
-    def temporal(stage, index, n, whole, zs, xhs, scale):
-        def halo(side):
-            to = p.t + 1 if side == 2 else p.t - 1
-            return send(d3.at[1], d3.at[side], halo_send.at[stage, side // 2], halo_recv.at[stage, side // 2],
-                        (p.z, to))
+    def temporal(stage, index, n, whole, zs, xhs, scale, words, before, finish):
+        halo = Halo(p, stage, lambda side: d3.at[1], lambda side: d3.at[2 - 2 * side], relay,
+                    (halo_send, halo_recv, pass_send, pass_recv), s.cut)
 
         def run(dz, xh, wu):
-            pl.when(p.t < p.slots - 1)(lambda: halo(2).start())
-            pl.when(p.t > 0)(lambda: halo(0).start())
-            cz = fetch_into(zs, nat, 2)
+            halo.start(0)
+            halo.start(1)
+            cz = pltpu.make_async_copy(zs, nat, load.at[2])
+            if stage:
+                cz.start()
             cw = fetch_into(whole, wu, 3)
             cx = fetch_into(xhs, xh, 4)
             cz.wait()
@@ -1472,28 +1686,43 @@
                     flip[...], d3[k], preferred_element_type=F32
                 ).astype(BF)
 
-            grads(1)
-            tick(2)
-            pl.when(p.t < p.slots - 1)(lambda: halo(0).wait_recv())
-            grads(0)
-            pl.when(p.t > 0)(lambda: halo(2).wait_recv())
-            grads(2)
+            extra = before()
+            with scope("u grads"):
+                grads(1)
+            go(words[0])
+            with scope("halo wait"):
+                halo.relay()
+                halo.wait(1)
+            with scope("u grads"):
+                grads(0)
+            with scope("halo wait"):
+                halo.wait(0)
+            go(words[3])
+            with scope("u grads"):
+                grads(2)
             sc = scatter(index)
             for rel in (3, 1, 2, 0):
                 sc.twin(rel)
-            queue.extend(sc.steps())
+            go(words[1])
             cx.wait()
 
             def fetch(group, r0):
                 return dz[pl.ds(r0, 16), :]
 
-            total = totals.run(2 * stage, upstream(n, dz, xh, fetch, 16, mid))
-            norm_back(n, total, scale, dz, xh, nat_store, 16, mid)
-
-        pl.run_scoped(run, pltpu.VMEM((m, mid), F32), pltpu.VMEM((m, mid), F32), pltpu.VMEM((3 * mid, d), BF))
+            with scope("upstream"):
+                local_sums = upstream(n, dz, xh, fetch, 16, mid)
+            go(words[2])
+            extra = extra + finish()
+            with scope("total"):
+                total = totals.run(2 * stage, local_sums)
+            with scope("norm back"):
+                norm_back(n, total, scale, dz, xh, nat_store, 16, mid)
+            return extra
+
+        extra = pl.run_scoped(run, pltpu.VMEM((m, mid), F32), pltpu.VMEM((m, mid), F32), pltpu.VMEM((3 * mid, d), BF))
         zero_padding(s, nat, mid)
-        pl.when(p.t < p.slots - 1)(lambda: halo(2).wait_send())
-        pl.when(p.t > 0)(lambda: halo(0).wait_send())
+        halo.done()
+        return extra
 
     def finish_u(n, ref):
         sc = scatter(n)
@@ -1502,8 +1731,9 @@
         sc.sent()
         return jnp.sum(g * g, axis=0, keepdims=True)
 
-    def finish_s(n, ref):
+    def finish_s(n, out):
         sc = scatter(n)
+        ref = gsh
         g = sc.result()
         turn[...] = g.T
         mine = turn[pl.ds(pl.multiple_of(p.core * (s.kw // 2), 16), s.kw // 2), :]
@@ -1515,6 +1745,9 @@
         send(turn.at[pl.ds(0, s.kw // 2)], ref.at[1 - p.core], half_s.at[n // 2], half_r.at[n // 2],
              p.device(TWIN)).wait_recv()
         copy.wait_send()
+        keep = pltpu.make_async_copy(ref, out, load.at[8])
+        keep.start()
+        keep.wait()
         return jnp.sum(jnp.sum((g * g).reshape(s.nb, s.kw // 128, 128), axis=0), axis=0, keepdims=True)
 
     pieces = []
@@ -1526,7 +1759,7 @@
             lo = hi
         pieces.append(found)
 
-    def spatial(index, whole, taps, grids, tap_buf, tile):
+    def spatial(index, whole, taps, grids, tap_buf, tile, words, tap_words, early):
         rels = (3, 1, 2, 0)
 
         def tap_load(i):
@@ -1545,6 +1778,7 @@
         tap_load(1).start()
         for c in tile_loads(0):
             c.start()
+        go(early)
         transpose()
         for grid in grids:
             def clear(i, _, grid=grid):
@@ -1555,15 +1789,16 @@
         sc = scatter(index)
         for i, rel in enumerate(rels):
             tap_load(i).wait()
-            for lo, width in wide_cuts(s.kw):
-                y = jnp.dot(flip[...], tap_buf[i % 2, :, lo : lo + width], preferred_element_type=F32).astype(BF)
-                for n in range(2 * s.batches):
-                    b, core = n // 2, n % 2
-                    ps[rel, core, b * s.nb : (b + 1) * s.nb, lo : lo + width] = y[n * s.nb : (n + 1) * s.nb]
+            with scope("dw slab"):
+                for lo, width in wide_cuts(s.kw):
+                    y = jnp.dot(flip[...], tap_buf[i % 2, :, lo : lo + width], preferred_element_type=F32).astype(BF)
+                    for n in range(2 * s.batches):
+                        b, core = n // 2, n % 2
+                        ps[rel, core, b * s.nb : (b + 1) * s.nb, lo : lo + width] = y[n * s.nb : (n + 1) * s.nb]
             sc.twin(rel)
             if i + 2 < 4:
                 tap_load(i + 2).start()
-        queue.extend(sc.steps())
+            go(words[i])
         for tap in range(9):
             if tap + 1 < 9:
                 for c in tile_loads(tap + 1):
@@ -1571,14 +1806,15 @@
             for c in tile_loads(tap):
                 c.wait()
             i, j = tap // 3, tap % 3
-            y = jnp.dot(nat[...], tile[tap % 2], preferred_element_type=F32)
-            base = 0
-            for group in range(2):
-                side = s.sides[group]
-                part = y[base : base + s.cells[group] * 8].reshape(side, side, 8, d)
-                grids[group][i : i + side, j : j + side] += part
-                base += s.rows[group]
-            tick(1)
+            with scope("dx tap"):
+                y = jnp.dot(nat[...], tile[tap % 2], preferred_element_type=F32)
+                base = 0
+                for group in range(2):
+                    side = s.sides[group]
+                    part = y[base : base + s.cells[group] * 8].reshape(side, side, 8, d)
+                    grids[group][i : i + side, j : j + side] += part
+                    base += s.rows[group]
+            go(tap_words[tap])
         clear_pad_cells(s, grids)
 
     def spatial_types():
@@ -1589,44 +1825,68 @@
             pltpu.VMEM((m, d), F32), pltpu.VMEM((m, d), F32),
         )
 
-    temporal(0, 3, 2, gu2, z3, xh3, r3[...])
+    nothing = jnp.zeros((1, 128), F32)
+    temporal(0, 3, 2, gu2, z3, xh3, r3[...], ("", "", "3j3 3j1 3j2 3j0", ""), lambda: nothing, lambda: nothing)
 
     def second(grid_s, grid_l, tap_buf, tile, b, xh):
         cx = fetch_into(xh2, xh, 5)
-        flush()
-        sums = finish_u(3, guo2)
-        spatial(2, gs2, taps2, (grid_s, grid_l), tap_buf, tile)
+        spatial(2, gs2, taps2, (grid_s, grid_l), tap_buf, tile,
+                ("", "2j3", "2j1", "2j2"),
+                ("2j0 3k1", "", "2r0 2r1", "", "3k2", "", "", "", ""), "3z30 3z21 3z12")
         cx.wait()
 
         def fetch(group, r0):
             return rows_of_grid(s, (grid_s, grid_l), group, r0)
 
-        total = totals.run(1, upstream(1, b, xh, fetch, 80, d))
-        norm_back(1, total, r2[...], b, xh, narrow_store, 80, d)
+        with scope("upstream"):
+            local_sums = upstream(1, b, xh, fetch, 80, d)
+        with scope("total"):
+            total = totals.run(1, local_sums)
+        with scope("norm back"):
+            norm_back(1, total, r2[...], b, xh, narrow_store, 80, d)
+
+    pl.run_scoped(second, *spatial_types())
+    zero_padding(s, d3.at[1], d)
+
+    def finish_second():
+        with scope("finish s"):
+            return finish_s(2, gso2)
+
+    def finish_first():
+        go("3c 3t")
+        with scope("finish u"):
+            return finish_u(3, guo2)
+
+    sums = temporal(1, 1, 0, gu1, z1, xh1, r1[...],
+                    ("2r3 2r2", "", "2t 1j3 1j1 1j2 1j0", ""), finish_first, finish_second)
+
+    def final(grid_s, grid_l, tap_buf, tile, b, up):
+        cx = fetch_into(dpre, up, 6)
+        spatial(0, gs1, taps1, (grid_s, grid_l), tap_buf, tile,
+                ("", "0j3", "0j1", "0j2"),
+                ("0j0 1k1", "", "", "0r0 0r3 0r1 0r2", "", "1k2", "", "", ""), "1z30 1z21 1z12")
+        cx.wait()
+
+        def rows(group, r0, c):
+            b[pl.ds(r0, 80), :] = rows_of_grid(s, (grid_s, grid_l), group, r0) + up[pl.ds(r0, 80), :]
+            return c
+
+        with scope("dx"):
+            chunks(s, 80, rows)
+        cd = fetch_into(b, dx, 7)
+        go("0t")
+        go("1c")
+        go("1t")
+        with scope("finish u"):
+            sums = finish_u(1, guo1)
+        with scope("finish s"):
+            sums = sums + finish_s(0, gso1)
+        cd.wait()
         return sums
 
-    sums = pl.run_scoped(second, *spatial_types())
-    zero_padding(s, d3.at[1], d)
-    temporal(1, 1, 0, gu1, z1, xh1, r1[...])
-
-    def final(grid_s, grid_l, tap_buf, tile, b, up, sums=sums):
-        cx = fetch_into(dpre, up, 6)
-        flush()
-        sums = sums + finish_u(1, guo1) + finish_s(2, gsh2)
-        totals.run(4, jnp.broadcast_to(sums, (4, 128)))
-        spatial(0, gs1, taps1, (grid_s, grid_l), tap_buf, tile)
-        cx.wait()
-
-        def rows(group, r0, c):
-            dx[pl.ds(r0, 80), :] = rows_of_grid(s, (grid_s, grid_l), group, r0) + up[pl.ds(r0, 80), :]
-            return c
-
-        chunks(s, 80, rows)
-        flush()
-        return sums + finish_s(0, gsh1)
-
-    sums = pl.run_scoped(final, *spatial_types())
-    square[...] = totals.run(3, jnp.broadcast_to(sums, (4, 128)))
+    sums = sums + pl.run_scoped(final, *spatial_types())
+    with scope("total"):
+        square[...] = totals.run(3, jnp.broadcast_to(sums, (4, 128)))
 
 
 def backward_call(s, saved, norm, live, inverse):
@@ -1640,19 +1900,21 @@
     scratch = [
         V((4, 2, rows, kw), BF), V((4, rows, kw), BF), V((half * s.nb, kw), BF), V((half * s.nb, kw), BF),
         V((rows, kw), BF), V((rows, kw), BF), V((rows, kw), BF), V((rows, kw), BF),
-        V((3 * mid, d), BF), V((4, s.ur, d), BF), V((s.ur, d // 2), BF), V((s.ur, d // 2), BF),
-        V((s.ur, d), BF), V((s.ur, d), BF), V((s.ur, d), BF), V((s.ur, d), BF),
+        V((3 * mid, d), BF), V((4, s.ur, d), BF), V((s.ur, s.uc), BF), V((s.ur, s.uc), BF), V((s.ur, s.uc), BF),
+        V((4, s.ur, d), BF), V((4, s.ur, d), BF), V((m - s.cut, d), BF),
         V((m, mid), BF), V((mid, m), BF), V((3, m, d), BF), V((kw, s.nb), F32),
-        V((5, s.slots, 4, mid), F32), V((5, nb, 4, mid), F32),
-        dma((8,)), dma((4,)), dma((9, 3)), dma((2, 2)), dma((2, 2)),
+        V((2, kw // 2, s.nb), F32),
+        V((4, s.slots, 4, mid), F32), V((4, nb, 4, mid), F32),
+        dma((9,)), dma((4,)), dma((9, 3)), dma((2, 2, 2)), dma((2, 2, 2)), dma((2,)), dma((2,)),
+        dma((4, 2, 4, nb)), dma((4, 2, 4, nb)),
         dma((4, 4)), dma((4, 4)), dma((4, 5, nb)), dma((4, 5, nb)), dma((2,)), dma((2,)),
-        dma((5, s.slots)), dma((5, s.slots)), dma((5, nb)), dma((5, nb)),
+        dma((4, s.slots)), dma((4, s.slots)), dma((4, nb)), dma((4, nb)),
     ]
     return pl.pallas_call(
         functools.partial(backward_kernel, s),
         out_shape=outs,
         in_specs=[any_] * 13 + [vmem] * 7 + [smem],
-        out_specs=(vmem,) * 7,
+        out_specs=(any_,) * 3 + (vmem,) * 4,
         scratch_shapes=scratch,
         compiler_params=pltpu.CompilerParams(
             collective_id=1, has_side_effects=True, vmem_limit_bytes=63 * 2**20

time: 736 us -> 603 us (0.82)
  Pallas kernels: 692 us -> 563 us
    pallas_call x1, Pallas kernels: 359 us -> 290 us  [backward_call(): pl.pallas_call(functools.partial(backward_kernel, s), out_shape=outs, in_...]
    pallas_call x1, Pallas kernels: 333 us -> 274 us  [forward_call(): pl.pallas_call(functools.partial(forward_kernel, s), out_shape=outs, in_s...]
where the time goes in v3:
time: 603 us; the launch traced here: 600 us
  Pallas kernels  563 us (93%)
  other arithmetic  17.1 us (3%)
  local copies, waits for them, and re-layouts  15.9 us (3%)
    pallas_call x1, Pallas kernels, backward_call(): pl.pallas_call(functools.partial(backward_kernel, s), out_shape=outs, in_...  290 us
    pallas_call x1, Pallas kernels, forward_call(): pl.pallas_call(functools.partial(forward_kernel, s), out_shape=outs, in_s...  274 us

profile of v3, /device:TPU:0, one launch (start us, length us, event | category | flops | bytes accessed | tf_op | source)
XLA Modules:
  0.0 599.7 jit_solution(15607127754559317784)
XLA Ops:
  0.7 0.0 copy-start
  0.7 0.0 copy-start.7
  0.7 0.0 copy-start.1
  0.7 3.3 fusion.3
  4.0 0.0 copy-start.8
  4.0 0.0 copy-done
  4.1 1.1 copy.45
  5.2 0.0 copy-done.7
  5.2 0.7 convert_element_type.29.refs_3_
  5.8 0.0 copy-done.1
  5.9 1.1 copy.46
  6.9 0.0 copy-done.8
  6.9 0.7 convert_element_type.31.refs_5_
  7.6 0.0 copy-done.20
  7.6 0.2 dynamic-slice_reduce_fusion
  7.8 0.7 fusion.13.refs_7_.refs_19_
  8.4 0.1 reduce_sum.27
  8.6 0.0 copy-done.21
  8.6 0.5 multiply_divide_fusion.refs_8_.refs_20_
  9.1 273.5 %forward.1 = (bf16[4,1152,1152]{2,1,0:T(8,128)(2,1)}, bf16[3456,512]{1,0:T(8,128)(2,1)}, bf16[4,1152,1152]{2,1,0:T(8,128)(2,1)}, bf16[3456,512]{1,0:T(8,128)(2,1...) custom-call(bf16[1200,512]{1,0:T(8,128)(2,1)} %get-tuple-element.107, ...), custom_call_target="tpu_custom_call" | custom-call | tf_op jit(solution)/shard_map/forward/pallas_call | solution.py:1227
  282.6 0.0 copy-start.4
  282.6 1.3 slice_bitcast_fusion.3
  284.0 1.7 copy.49
  285.7 0.0 copy-done.4
  285.7 0.1 slice_bitcast_fusion.1
  285.8 2.8 copy.50
  288.7 289.6 %backward.1 = (f32[1200,512]{1,0:T(8,128)}, f32[2,576,144]{2,1,0:T(8,128)}, f32[2,576,144]{2,1,0:T(8,128)}, f32[432,128]{1,0:T(8,128)}, f32[432,128]{1,0:T(8,128)}, /*index=5*/f32[2,3328]{1,0:T(2,128)}, f32[4,128]{1,0:T(4,128)}) custom-call(bf16[4,1152,1152]{2,1,0:T(8,128)(2,1)} %get-tuple-element.47.refs_0_, bf16[3456,512]{1,0:T(8,128)(2,1)} %get-tuple-element.48.refs_1_, ...), custom_call_target="tpu_custom_call" | custom-call | tf_op jit(solution)/shard_map/backward/pallas_call | solution.py:1913
  578.3 0.0 copy-start.3
  578.3 1.3 slice_bitcast_fusion.2
  579.6 1.7 copy.51
  581.4 0.0 copy-done.3
  581.4 0.1 slice_bitcast_fusion
  581.5 0.0 copy-start.17
  581.5 0.0 copy-start.6
  581.5 2.8 copy.52
  584.4 1.3 slice_reduce_fusion
  585.6 0.0 copy-done.17
  585.6 0.6 multiply_reduce_fusion
  587.6 0.0 copy-done.6
  587.6 0.1 multiply_bitcast_fusion.1
  587.7 0.4 copy.47
  588.1 0.0 copy-start.5
  588.1 3.2 multiply_subtract_fusion.1
  591.3 0.0 copy-done.11
  591.3 0.0 copy-done.12
  591.3 0.0 copy-done.16
  591.3 0.9 multiply_subtract_fusion.3
  592.3 0.0 copy-done.5
  592.3 0.1 multiply_bitcast_fusion
  592.4 0.4 copy.48
  592.7 0.7 copy-done.2
  593.4 0.0 copy-start.10
  593.4 0.0 copy-start.18
  593.4 0.0 copy-start.19
  593.4 3.2 multiply_subtract_fusion
  596.7 0.0 copy-done.9
  596.7 0.0 copy-done.13
  596.7 0.0 copy-done.14
  596.7 0.0 copy-done.15
  596.7 0.9 multiply_subtract_fusion.2
  597.6 0.0 copy-done.10
  597.6 0.0 copy-done.18
  597.6 0.0 copy-done.19
  597.6 0.7 multiply_subtract_fusion.4
  (12 shorter events, 0.1 us)
Async XLA Ops:
  0.7 3.4 copy-start
  0.7 4.5 copy-start.7
  0.7 5.1 copy-start.1
  4.0 2.9 copy-start.8
  4.0 3.6 copy-start.20
  4.0 4.5 copy-start.21
  282.6 3.1 copy-start.4
  578.3 3.1 copy-start.3
  581.5 4.1 copy-start.17
  581.5 6.1 %copy-start.6 = (f32[2,576,144]{2,1,0:T(8,128)S(1)}, f32[2,576,144]{2,1,0:T(8,128)}, u32[]{:S(2)}) copy-start(f32[2,576,144]{2,1,0:T(8,128)} %get-tuple-element.68) | copy-start | bytes 1990660
  588.1 3.2 copy-start.11
  588.1 3.2 copy-start.12
  588.1 3.2 copy-start.16
  588.1 4.2 copy-start.5
  592.3 1.1 copy-start.2
  593.4 3.3 copy-start.9
  593.4 3.3 copy-start.13
  593.4 3.3 copy-start.14
  593.4 3.3 copy-start.15
  593.4 4.2 copy-start.10
  593.4 4.2 copy-start.18
  593.4 4.2 copy-start.19

commit v4 on v3

--- a/solution.py
+++ b/solution.py
@@ -525,55 +525,55 @@
 
 class Totals:
     def __init__(self, place, rows, planes, lines, sems):
-        self.place, self.rows, self.planes, self.lines = place, rows, planes, lines
+        self.p, self.rows, self.planes, self.lines = place, rows, planes, lines
         self.plane_send, self.plane_recv, self.line_send, self.line_recv = sems
 
-    def run(self, n, value):
-        p = self.place
+    def plane_copy(self, n, step, width):
+        p = self.p
+        to = lax.rem(p.t + step, p.slots)
+        ref = self.planes.at[n, p.t, :, pl.ds(0, width)]
+        return send(ref, ref, self.plane_send.at[n, step], self.plane_recv.at[n, p.t], (p.z, to))
+
+    def line_copy(self, n, step, width):
+        p = self.p
+        to = lax.rem(p.z + step, p.batches)
+        ref = self.lines.at[n, p.z, :, pl.ds(0, width)]
+        return send(ref, ref, self.line_send.at[n, step], self.line_recv.at[n, p.z], (to, p.t))
+
+    def run(self, n, value, first=None, second=None):
+        p = self.p
         width = value.shape[1]
         plane, line = self.planes.at[n], self.lines.at[n]
         plane[p.t, :, :width] = value
-
-        def plane_copy(step):
-            to = lax.rem(p.t + step, p.slots)
-            ref = plane.at[p.t, :, pl.ds(0, width)]
-            return send(ref, ref, self.plane_send.at[n, step], self.plane_recv.at[n, p.t], (p.z, to))
-
-        def plane_wait(step):
+        for step in range(1, p.slots):
+            self.plane_copy(n, step, width).start()
+        if first is not None:
+            first()
+        for step in range(1, p.slots):
             origin = lax.rem(p.t + p.slots - step, p.slots)
             ref = plane.at[origin, :, pl.ds(0, width)]
-            send(ref, ref, self.plane_send.at[n, step], self.plane_recv.at[n, origin], (p.z, p.twin)).wait_recv()
-
-        for step in range(1, p.slots):
-            plane_copy(step).start()
-        for step in range(1, p.slots):
-            plane_wait(step)
+            send(ref, ref, self.plane_send.at[n, step], self.plane_recv.at[n, origin],
+                 (p.z, p.twin)).wait_recv()
         total = plane[0, :, :width]
         for slot in range(1, p.slots):
             total = total + plane[slot, :, :width]
         line[p.z, :, :width] = total
-
-        def line_copy(step):
-            to = lax.rem(p.z + step, p.batches)
-            ref = line.at[p.z, :, pl.ds(0, width)]
-            return send(ref, ref, self.line_send.at[n, step], self.line_recv.at[n, p.z], (to, p.t))
-
-        def line_wait(step):
+        for step in range(1, p.batches):
+            self.line_copy(n, step, width).start()
+        if second is not None:
+            second()
+        for step in range(1, p.batches):
             origin = lax.rem(p.z + p.batches - step, p.batches)
             ref = line.at[origin, :, pl.ds(0, width)]
-            send(ref, ref, self.line_send.at[n, step], self.line_recv.at[n, origin], (p.z, p.twin)).wait_recv()
-
-        for step in range(1, p.batches):
-            line_copy(step).start()
-        for step in range(1, p.batches):
-            line_wait(step)
+            send(ref, ref, self.line_send.at[n, step], self.line_recv.at[n, origin],
+                 (p.z, p.twin)).wait_recv()
         total = line[0, :, :width]
         for slot in range(1, p.batches):
             total = total + line[slot, :, :width]
         for step in range(1, p.slots):
-            plane_copy(step).wait_send()
+            self.plane_copy(n, step, width).wait_send()
         for step in range(1, p.batches):
-            line_copy(step).wait_send()
+            self.line_copy(n, step, width).wait_send()
         return total
 
 
@@ -709,6 +709,84 @@
                 self.copy(TWIN, rel, b, self.own).wait_send()
             pl.when(b < half)(lambda: self.copy(ALONG, 1, b, self.own).wait_send())
             pl.when(b >= half)(lambda: self.copy(ACROSS, 2, b, self.own).wait_send())
+            return 0
+
+        lax.fori_loop(0, p.batches, body, 0)
+
+
+class FarLineGather(Gather):
+    def line(self, rel, b, up=True, down=True):
+        p = self.p
+        if up:
+            pl.when(p.z < p.batches - 1)(lambda: self.copy(UP, rel, b).start())
+        if down:
+            pl.when(p.z > 0)(lambda: self.copy(DOWN, rel, b).start())
+
+    def side_own(self):
+        z = self.p.z
+        self.wait(1, z)
+        self.copy(ALONG, 1, z).start()
+        self.copy(TWIN, 1, z).start()
+
+    def far_own(self):
+        z = self.p.z
+        self.wait(3, z)
+        self.copy(TWIN, 3, z).start()
+        self.line(3, z)
+
+    def far_hop(self, k):
+        p = self.p
+
+        def below(b):
+            self.wait(3, b)
+            self.line(3, b, down=False)
+            self.copy(TWIN, 3, b).start()
+
+        def above(b):
+            self.wait(3, b)
+            self.line(3, b, up=False)
+            self.copy(TWIN, 3, b).start()
+
+        pl.when(p.z - k >= 0)(lambda: below(p.z - k))
+        pl.when(p.z + k < p.batches)(lambda: above(p.z + k))
+
+    def from_side(self, k):
+        def one(b):
+            self.wait(1, b)
+            self.copy(TWIN, 1, b).start()
+
+        self.at(k, one)
+
+    def from_deep(self, k):
+        def one(b):
+            self.wait(2, b)
+            self.copy(TWIN, 2, b).start()
+
+        self.at(k, one)
+
+    def act(self, word):
+        if word == "c":
+            self.side_own()
+        elif word == "d":
+            self.far_own()
+        elif word[0] == "g":
+            self.far_hop(int(word[1]))
+        else:
+            super().act(word)
+
+    def finish(self):
+        p = self.p
+        self.copy(ALONG, 1, p.z, self.own).wait_send()
+
+        def body(b, _):
+            for rel in (0, 3):
+                pl.when((b <= p.z) & (p.z < p.batches - 1))(
+                    lambda: self.copy(UP, rel, b, self.own).wait_send())
+                pl.when((b >= p.z) & (p.z > 0))(lambda: self.copy(DOWN, rel, b, self.own).wait_send())
+            for way in (ACROSS, ALONG):
+                self.copy(way, 0, b, self.own).wait_send()
+            for rel in range(4):
+                self.copy(TWIN, rel, b, self.own).wait_send()
             return 0
 
         lax.fori_loop(0, p.batches, body, 0)
@@ -970,7 +1048,7 @@
     gather = [
         Gather(p, 0, own1, gs1, s_block, sems),
         Gather(p, 1, uw1, gu1, u_block, sems),
-        Gather(p, 2, own2, gs2, s_block, sems),
+        FarLineGather(p, 2, own2, gs2, s_block, sems),
         Gather(p, 3, uw2, gu2, u_block, sems),
     ]
 
@@ -1103,9 +1181,11 @@
             hs[1] = jnp.dot(z[...], wub[2 * mid :, :], preferred_element_type=F32).astype(BF)
             halos[n].start(1)
             b[...] = jnp.dot(z[...], wub[mid : 2 * mid, :], preferred_element_type=F32)
-        go(words)
+        go(words[0])
+        with scope("relay"):
+            halos[n].relay()
+        go(words[1])
         with scope("halo wait"):
-            halos[n].relay()
             halos[n].wait(0)
             halos[n].wait(1)
 
@@ -1120,12 +1200,12 @@
         with scope("total"):
             return totals.run(index, local_sums)
 
-    go("1z 0h1 0s1 0p0 1h1 0h2 0s2 0p1 0f0 1h2 0h3 0s3 1h3")
-    spatial(0, gs1, (0, 1, 2, 3), ("0p2 0f1", "", "0p3", "1x 1s1 1s2 1s3", "0f2", "", "0f3 2z", "1p0 1f0"))
-    xc1, zc1 = wide_norm(0, 0, z1_o, xh1_o, r1_o, 5, ("1p1 1f1 1p2 1f2 1p3 1f3", "2x"), (0, 1))
-    temporal(0, "2h1 2l1 2h2 2l2 2h3 2l3")
+    go("0h1 0s1 0p0 0h2 0s2 0p1 0f0 0h3 0s3 1z")
+    spatial(0, gs1, (0, 1, 2, 3), ("", "", "0p2 0f1 1h1 0p3 1h2", "1x 1s1 1h3 1s2 1s3", "0f2", "1p0", "0f3 1p1 1f0", "2z"))
+    xc1, zc1 = wide_norm(0, 0, z1_o, xh1_o, r1_o, 5, ("1p2 1f1 1p3 1f2 1f3", "2x 2h1 3z"), (0, 1))
+    temporal(0, ("", "2c 2l1 2h2 2l2 2d 3h1 2h3 2l3 2g1 3h2"))
     total = narrow_total(1)
-    go("2a1 2a2 2a3 3z")
+    go("2a1 3h3 3x 3s1 3s2 3s3 2a2 2a3 2g2")
     mean2, scale2 = moments(total, inv, d)
     r2_o[...] = jnp.concatenate(scale2, axis=0)
     gain2, bias2 = gain_bias(1)
@@ -1149,11 +1229,11 @@
     taps_copy2 = pltpu.make_async_copy(taps, taps2_o, local.at[8])
     taps_copy2.start()
     xc1.wait()
-    spatial(2, gs2, (0, 2, 1, 3), ("", "2v0 2v1 2v2 2v3", "2u0 2u1 3h1", "", "2u2 2u3 3h2", "3x 3s1 3s2", "2f0 2f1 2f2 2f3 3h3 3s3", ""))
+    spatial(2, gs2, (0, 2, 3, 1), ("", "2v0 2v1 2v2 2v3", "", "2g3", "", "3p0 3p1 3f0", "2u1 2u2 2u3", "3p2 3f1"))
     zc1.wait()
-    xc3, zc3 = wide_norm(2, 2, z3_o, xh3_o, r3_o, 9, ("3p0 3f0 3p1 3f1 3p2 3f2 3p3 3f3", ""), (1, 3))
+    xc3, zc3 = wide_norm(2, 2, z3_o, xh3_o, r3_o, 9, ("3p3 3f2 3f3", ""), (1, 3))
     xc2.wait()
-    temporal(1, "")
+    temporal(1, ("", ""))
     total = narrow_total(3)
     mean4, scale4 = moments(total, inv, d)
     r4_o[...] = jnp.concatenate(scale4, axis=0)
@@ -1271,7 +1351,7 @@
 class Scatter:
     def __init__(self, place, index, part, bufs, cut, rows, step, sems):
         self.p, self.n, self.part, self.cut, self.rows, self.step = place, index, part, cut, rows, step
-        self.tr, self.fx, self.fa, self.rx, self.ry, self.ru, self.rd = bufs
+        self.tr, self.fx, self.fa, self.rx, self.ry, self.ru, self.rd = bufs[:7]
         self.twin_s, self.twin_r, self.block_s, self.block_r = sems
         self.half = place.batches // 2
 
@@ -1301,10 +1381,10 @@
         return self.block_copy(self.DEEP, b, self.own(2, b), self.cut(self.ry, b), ALONG)
 
     def rise_copy(self, b):
-        return self.block_copy(self.RISE, b, self.own(0, b), self.cut(self.ru, b), UP)
+        return self.block_copy(self.RISE, b, self.own(0, b), self.cut(self.ru, b + 1), UP)
 
     def fall_copy(self, b):
-        return self.block_copy(self.FALL, b, self.own(0, b), self.cut(self.rd, b), DOWN)
+        return self.block_copy(self.FALL, b, self.own(0, b), self.cut(self.ru, b), DOWN)
 
     def arrive(self, kind, b, ref):
         self.block_copy(kind, b, ref, ref, TWIN).wait_recv()
@@ -1352,93 +1432,91 @@
             self.arrive(kind, b, src)
             self.add(self.own(0, b), src)
 
-    def chain(self, b):
-        p = self.p
-
-        @pl.when(p.z < b)
-        def _():
-            @pl.when(p.z > 0)
-            def _():
-                self.arrive(self.RISE, b, self.cut(self.ru, b))
-                self.add(self.own(0, b), self.cut(self.ru, b))
-
-            self.rise_copy(b).start()
-
-        @pl.when(p.z > b)
-        def _():
-            @pl.when(p.z < p.batches - 1)
-            def _():
-                self.arrive(self.FALL, b, self.cut(self.rd, b))
-                self.add(self.own(0, b), self.cut(self.rd, b))
-
-            self.fall_copy(b).start()
-
-    def tail(self):
-        p = self.p
+    def gather_own(self):
+        p = self.p
+        n = p.batches
 
         @pl.when(p.z < self.half)
         def _():
-            for b in range(p.batches - 1, -1, -1):
+            for b in range(n - 1, -1, -1):
                 self.collect(b)
-                self.chain(b)
+                if b:
+                    pl.when(p.z == 0)(lambda b=b: self.rise_copy(b).start())
 
         @pl.when(p.z >= self.half)
         def _():
-            for b in range(p.batches):
+            for b in range(n):
                 self.collect(b)
-                self.chain(b)
+                if b < n - 1:
+                    pl.when(p.z == n - 1)(lambda b=b: self.fall_copy(b).start())
+
+    def chain(self, stage):
+        p = self.p
+
+        @pl.when(p.z == stage)
+        def _():
+            for b in range(p.batches - 1, stage, -1):
+                src = self.cut(self.ru, b + 1)
+                self.arrive(self.RISE, b, src)
+                self.add(self.own(0, b), src)
+                self.rise_copy(b).start()
+
+        @pl.when(p.z == p.batches - 1 - stage)
+        def _():
+            for b in range(p.batches - 1 - stage):
+                src = self.cut(self.ru, b)
+                self.arrive(self.FALL, b, src)
+                self.add(self.own(0, b), src)
+                self.fall_copy(b).start()
 
     def result(self):
         p = self.p
-        pl.when(p.z > 0)(lambda: self.arrive(self.RISE, p.z, self.cut(self.ru, p.z)))
-        pl.when(p.z < p.batches - 1)(lambda: self.arrive(self.FALL, p.z, self.cut(self.rd, p.z)))
+        up, down = self.cut(self.ru, p.z + 1), self.cut(self.ru, p.z)
+        pl.when(p.z > 0)(lambda: self.arrive(self.RISE, p.z, up))
+        pl.when(p.z < p.batches - 1)(lambda: self.arrive(self.FALL, p.z, down))
 
         @pl.when(p.z == 0)
         def _():
-            ref = self.cut(self.ru, p.z)
-            ref[...] = jnp.zeros(ref.shape, BF)
+            up[...] = jnp.zeros(up.shape, BF)
 
         @pl.when(p.z == p.batches - 1)
         def _():
-            ref = self.cut(self.rd, p.z)
-            ref[...] = jnp.zeros(ref.shape, BF)
-
-        return (
-            self.own(0, p.z)[...].astype(F32)
-            + self.cut(self.ru, p.z)[...].astype(F32)
-            + self.cut(self.rd, p.z)[...].astype(F32)
-        )
-
-    def sent(self):
-        p = self.p
-        for rel in range(4):
-            self.twin_copy(rel).wait_send()
+            down[...] = jnp.zeros(down.shape, BF)
+
+        return self.own(0, p.z)[...].astype(F32) + up[...].astype(F32) + down[...].astype(F32)
+
+    def sent(self, rel):
+        p = self.p
+        self.twin_copy(rel).wait_send()
         for b in range(p.batches):
-            self.far_copy(b).wait_send()
-            self.side_copy(b).wait_send()
-            self.deep_copy(b).wait_send()
-            pl.when(p.z < b)(lambda b=b: self.rise_copy(b).wait_send())
-            pl.when(p.z > b)(lambda b=b: self.fall_copy(b).wait_send())
+            if rel == 3:
+                self.far_copy(b).wait_send()
+            elif rel == 1:
+                self.side_copy(b).wait_send()
+            elif rel == 2:
+                self.deep_copy(b).wait_send()
+            else:
+                pl.when(p.z < b)(lambda b=b: self.rise_copy(b).wait_send())
+                pl.when(p.z > b)(lambda b=b: self.fall_copy(b).wait_send())
 
     def act(self, word):
-        if word == "t":
-            self.tail()
+        if word == "c":
+            self.gather_own()
         else:
-            {"j": self.join, "r": self.relay}[word[0]](int(word[1]))
+            {"j": self.join, "r": self.relay, "k": self.chain}[word[0]](int(word[1]))
 
 
 class LineScatter(Scatter):
     def rise(self, rel, b):
-        return send(self.own(rel, b), self.cut(self.ru.at[rel], b), self.line_s.at[self.n, 0, rel, b],
+        return send(self.own(rel, b), self.cut(self.ru.at[rel], b + 1), self.line_s.at[self.n, 0, rel, b],
                     self.line_r.at[self.n, 0, rel, b], self.p.device(UP))
 
     def fall(self, rel, b):
-        return send(self.own(rel, b), self.cut(self.rd.at[rel], b), self.line_s.at[self.n, 1, rel, b],
+        return send(self.own(rel, b), self.cut(self.ru.at[rel], b), self.line_s.at[self.n, 1, rel, b],
                     self.line_r.at[self.n, 1, rel, b], self.p.device(DOWN))
 
     def landed(self, way, rel, b):
-        buf = (self.ru, self.rd)[way]
-        ref = self.cut(buf.at[rel], b)
+        ref = self.cut(self.ru.at[rel], b + 1 - way)
         send(ref, ref, self.line_s.at[self.n, way, rel, b], self.line_r.at[self.n, way, rel, b],
              self.p.device(TWIN)).wait_recv()
         return ref
@@ -1544,8 +1622,8 @@
     (gs1, gu1, gs2, gu2, taps1, taps2, xh1, xh2, xh3, xh4, z1, z3, dpre,
      r1, r2, r3, r4, last, norm, live_ref, inverse,
      dx, gso1, gso2, guo1, guo2, ng, square,
-     ps, tr, fx, fa, rx, ry, ru, rd, pu, utr, ufx, urx, ury, uru, urd, relay,
-     nat, flip, d3, turn, gsh, planes, lines,
+     ps, tr, fx, fa, rx1, ry1, rz1, rx2, ry2, rz2, pu, utr, ufx, urx, ury, urz, relay,
+     nat, flip, d3, turn, planes, lines,
      load, tap_sem, tile_sem, halo_send, halo_recv, pass_send, pass_recv, line_s, line_r, twin_s, twin_r, block_s, block_r, half_s, half_r,
      pl_send, pl_recv, ln_send, ln_recv) = refs
     p = Place(s.batches, s.slots)
@@ -1573,8 +1651,11 @@
         at = b * s.uc if isinstance(b, int) else pl.multiple_of(b * s.uc, 128)
         return ref.at[:, pl.ds(at, s.uc)]
 
-    def part_s(rel, core):
-        return ps.at[rel, core]
+    def slot(n, rel):
+        return 4 if n == 0 and rel == 0 else rel
+
+    def part_s(n, rel, core):
+        return ps.at[slot(n, rel), core]
 
     def part_u(rel, core):
         return pu.at[pl.ds(pl.multiple_of((p.rel[rel] * 2 + core) * s.ur, 16), s.ur)]
@@ -1583,8 +1664,9 @@
 
     def scatter(n):
         if n % 2 == 0:
-            return Scatter(p, n, part_s, (tr, fx, fa, rx, ry, ru, rd), cut_rows, s.nb, 48, sems)
-        sc = LineScatter(p, n, part_u, (utr, ufx, None, urx, ury, uru, urd), cut_lanes, s.ur, 144, sems)
+            rx, ry, rz = (rx1, ry1, rz1) if n == 0 else (rx2, ry2, rz2)
+            return Scatter(p, n, functools.partial(part_s, n), (tr, fx, fa, rx, ry, rz, None), cut_rows, s.nb, 48, sems)
+        sc = LineScatter(p, n, part_u, (utr, ufx, None, urx, ury, urz, None), cut_lanes, s.ur, 144, sems)
         sc.line_s, sc.line_r = line_s, line_r
         return sc
 
@@ -1658,7 +1740,7 @@
         pl.run_scoped(first, pltpu.VMEM((m, d), F32), pltpu.VMEM((m, d), F32))
     zero_padding(s, d3.at[1], d)
 
-    def temporal(stage, index, n, whole, zs, xhs, scale, words, before, finish):
+    def temporal(stage, index, n, whole, zs, xhs, scale, words, finish):
         halo = Halo(p, stage, lambda side: d3.at[1], lambda side: d3.at[2 - 2 * side], relay,
                     (halo_send, halo_recv, pass_send, pass_recv), s.cut)
 
@@ -1674,7 +1756,7 @@
             transpose()
             cw.wait()
 
-            def grads(k):
+            def field_grad(k):
                 for lo, width in wide_cuts(mid):
                     y = lax.dot_general(d3[k], wu[k * mid + lo : k * mid + lo + width, :], NT_DIMS,
                                         preferred_element_type=F32)
@@ -1682,41 +1764,44 @@
                         dz[:, lo : lo + width] = y
                     else:
                         dz[:, lo : lo + width] += y
-                pu[k * mid : (k + 1) * mid, :] = jnp.dot(
-                    flip[...], d3[k], preferred_element_type=F32
-                ).astype(BF)
-
-            extra = before()
+
+            def weight_grad(k):
+                with scope("u weight grad"):
+                    pu[k * mid : (k + 1) * mid, :] = jnp.dot(
+                        flip[...], d3[k], preferred_element_type=F32
+                    ).astype(BF)
+
             with scope("u grads"):
-                grads(1)
+                field_grad(1)
+            with scope("relay"):
+                halo.relay()
             go(words[0])
             with scope("halo wait"):
-                halo.relay()
                 halo.wait(1)
             with scope("u grads"):
-                grads(0)
+                field_grad(0)
             with scope("halo wait"):
                 halo.wait(0)
-            go(words[3])
+            go(words[2])
             with scope("u grads"):
-                grads(2)
+                field_grad(2)
+            cx.wait()
+
+            def fetch(group, r0):
+                return dz[pl.ds(r0, 16), :]
+
+            with scope("upstream"):
+                local_sums = upstream(n, dz, xh, fetch, 16, mid)
+            extra = finish()
+            with scope("total"):
+                total = totals.run(2 * stage, local_sums, lambda: weight_grad(1),
+                                   lambda: (weight_grad(0), weight_grad(2)) and None)
             sc = scatter(index)
             for rel in (3, 1, 2, 0):
                 sc.twin(rel)
-            go(words[1])
-            cx.wait()
-
-            def fetch(group, r0):
-                return dz[pl.ds(r0, 16), :]
-
-            with scope("upstream"):
-                local_sums = upstream(n, dz, xh, fetch, 16, mid)
-            go(words[2])
-            extra = extra + finish()
-            with scope("total"):
-                total = totals.run(2 * stage, local_sums)
             with scope("norm back"):
                 norm_back(n, total, scale, dz, xh, nat_store, 16, mid)
+            go(words[1])
             return extra
 
         extra = pl.run_scoped(run, pltpu.VMEM((m, mid), F32), pltpu.VMEM((m, mid), F32), pltpu.VMEM((3 * mid, d), BF))
@@ -1733,20 +1818,19 @@
 
     def finish_s(n, out):
         sc = scatter(n)
-        ref = gsh
         g = sc.result()
         turn[...] = g.T
-        mine = turn[pl.ds(pl.multiple_of(p.core * (s.kw // 2), 16), s.kw // 2), :]
-        ref[p.core] = mine
-        copy = send(turn.at[pl.ds(pl.multiple_of((1 - p.core) * (s.kw // 2), 16), s.kw // 2)], ref.at[p.core],
-                    half_s.at[n // 2], half_r.at[n // 2], p.device(TWIN))
+        rows = s.kw // 2
+
+        def half(core):
+            return turn.at[pl.ds(pl.multiple_of(core * rows, 16), rows)]
+
+        keep = pltpu.make_async_copy(half(p.core), out.at[p.core], load.at[8])
+        keep.start()
+        copy = send(half(1 - p.core), out.at[p.core], half_s.at[n // 2], half_r.at[n // 2], p.device(TWIN))
         copy.start()
-        sc.sent()
-        send(turn.at[pl.ds(0, s.kw // 2)], ref.at[1 - p.core], half_s.at[n // 2], half_r.at[n // 2],
-             p.device(TWIN)).wait_recv()
+        send(half(p.core), out.at[1 - p.core], half_s.at[n // 2], half_r.at[n // 2], p.device(TWIN)).wait_recv()
         copy.wait_send()
-        keep = pltpu.make_async_copy(ref, out, load.at[8])
-        keep.start()
         keep.wait()
         return jnp.sum(jnp.sum((g * g).reshape(s.nb, s.kw // 128, 128), axis=0), axis=0, keepdims=True)
 
@@ -1759,7 +1843,7 @@
             lo = hi
         pieces.append(found)
 
-    def spatial(index, whole, taps, grids, tap_buf, tile, words, tap_words, early):
+    def spatial(index, whole, taps, grids, tap_buf, tile, words, tap_words, early, ready):
         rels = (3, 1, 2, 0)
 
         def tap_load(i):
@@ -1789,12 +1873,13 @@
         sc = scatter(index)
         for i, rel in enumerate(rels):
             tap_load(i).wait()
+            ready(rel)
             with scope("dw slab"):
                 for lo, width in wide_cuts(s.kw):
                     y = jnp.dot(flip[...], tap_buf[i % 2, :, lo : lo + width], preferred_element_type=F32).astype(BF)
                     for n in range(2 * s.batches):
                         b, core = n // 2, n % 2
-                        ps[rel, core, b * s.nb : (b + 1) * s.nb, lo : lo + width] = y[n * s.nb : (n + 1) * s.nb]
+                        ps[slot(index, rel), core, b * s.nb : (b + 1) * s.nb, lo : lo + width] = y[n * s.nb : (n + 1) * s.nb]
             sc.twin(rel)
             if i + 2 < 4:
                 tap_load(i + 2).start()
@@ -1817,74 +1902,89 @@
             go(tap_words[tap])
         clear_pad_cells(s, grids)
 
-    def spatial_types():
-        return (
-            pltpu.VMEM((s.sides[0] + 2, s.sides[0] + 2, 8, d), F32),
-            pltpu.VMEM((s.sides[1] + 2, s.sides[1] + 2, 8, d), F32),
-            pltpu.VMEM((2, m, s.kw), BF), pltpu.VMEM((2, mid, d), BF),
-            pltpu.VMEM((m, d), F32), pltpu.VMEM((m, d), F32),
+    grid_types = (
+        pltpu.VMEM((s.sides[0] + 2, s.sides[0] + 2, 8, d), F32),
+        pltpu.VMEM((s.sides[1] + 2, s.sides[1] + 2, 8, d), F32),
+    )
+    load_types = (pltpu.VMEM((2, m, s.kw), BF), pltpu.VMEM((2, mid, d), BF))
+    narrow_types = (pltpu.VMEM((m, d), F32), pltpu.VMEM((m, d), F32))
+
+    nothing = jnp.zeros((1, 128), F32)
+    temporal(0, 3, 2, gu2, z3, xh3, r3[...], ("", "3j3 3j1 3j2 3j0", ""), lambda: nothing)
+
+    def second(*grids):
+        pl.run_scoped(
+            lambda tap_buf, tile: spatial(
+                2, gs2, taps2, grids, tap_buf, tile, ("", "2j3", "2j1 3k1", "2j2"),
+                ("2j0", "", "", "", "3k2", "", "", "", ""), "3z30 3z21 3z12", lambda rel: None),
+            *load_types,
         )
 
-    nothing = jnp.zeros((1, 128), F32)
-    temporal(0, 3, 2, gu2, z3, xh3, r3[...], ("", "", "3j3 3j1 3j2 3j0", ""), lambda: nothing, lambda: nothing)
-
-    def second(grid_s, grid_l, tap_buf, tile, b, xh):
-        cx = fetch_into(xh2, xh, 5)
-        spatial(2, gs2, taps2, (grid_s, grid_l), tap_buf, tile,
-                ("", "2j3", "2j1", "2j2"),
-                ("2j0 3k1", "", "2r0 2r1", "", "3k2", "", "", "", ""), "3z30 3z21 3z12")
-        cx.wait()
-
-        def fetch(group, r0):
-            return rows_of_grid(s, (grid_s, grid_l), group, r0)
-
-        with scope("upstream"):
-            local_sums = upstream(1, b, xh, fetch, 80, d)
-        with scope("total"):
-            total = totals.run(1, local_sums)
-        with scope("norm back"):
-            norm_back(1, total, r2[...], b, xh, narrow_store, 80, d)
-
-    pl.run_scoped(second, *spatial_types())
+        def rest(b, xh):
+            fetch_into(xh2, xh, 5).wait()
+
+            def fetch(group, r0):
+                return rows_of_grid(s, grids, group, r0)
+
+            with scope("upstream"):
+                local_sums = upstream(1, b, xh, fetch, 80, d)
+            with scope("total"):
+                total = totals.run(1, local_sums)
+            with scope("norm back"):
+                norm_back(1, total, r2[...], b, xh, narrow_store, 80, d)
+
+        pl.run_scoped(rest, *narrow_types)
+
+    pl.run_scoped(second, *grid_types)
     zero_padding(s, d3.at[1], d)
 
-    def finish_second():
-        with scope("finish s"):
-            return finish_s(2, gso2)
-
-    def finish_first():
-        go("3c 3t")
+    def finish_small():
         with scope("finish u"):
             return finish_u(3, guo2)
 
     sums = temporal(1, 1, 0, gu1, z1, xh1, r1[...],
-                    ("2r3 2r2", "", "2t 1j3 1j1 1j2 1j0", ""), finish_first, finish_second)
-
-    def final(grid_s, grid_l, tap_buf, tile, b, up):
-        cx = fetch_into(dpre, up, 6)
-        spatial(0, gs1, taps1, (grid_s, grid_l), tap_buf, tile,
-                ("", "0j3", "0j1", "0j2"),
-                ("0j0 1k1", "", "", "0r0 0r3 0r1 0r2", "", "1k2", "", "", ""), "1z30 1z21 1z12")
-        cx.wait()
-
-        def rows(group, r0, c):
-            b[pl.ds(r0, 80), :] = rows_of_grid(s, (grid_s, grid_l), group, r0) + up[pl.ds(r0, 80), :]
-            return c
-
-        with scope("dx"):
-            chunks(s, 80, rows)
-        cd = fetch_into(b, dx, 7)
-        go("0t")
-        go("1c")
-        go("1t")
-        with scope("finish u"):
-            sums = finish_u(1, guo1)
+                    ("3c 2r0 2r1 2r3 2r2", "2c 1j3 1j1 1j2 1j0 1z30 1z21 1z12", "3t"), finish_small)
+
+    def final(*grids):
+        def ready(rel):
+            if rel:
+                scatter(2).sent(rel)
+
+        pl.run_scoped(
+            lambda tap_buf, tile: spatial(
+                0, gs1, taps1, grids, tap_buf, tile, ("", "0j3 2k1", "0j1", "0j2 2k2"),
+                ("0j0", "", "0r0 0r3", "0r1 0r2", "1k1", "", "", "", "1k2"), "", ready),
+            *load_types,
+        )
         with scope("finish s"):
-            sums = sums + finish_s(0, gso1)
-        cd.wait()
-        return sums
-
-    sums = sums + pl.run_scoped(final, *spatial_types())
+            sums = finish_s(2, gso2)
+        scatter(2).sent(0)
+
+        def rest(b, up):
+            fetch_into(dpre, up, 6).wait()
+
+            def rows(group, r0, c):
+                b[pl.ds(r0, 80), :] = rows_of_grid(s, grids, group, r0) + up[pl.ds(r0, 80), :]
+                return c
+
+            with scope("dx"):
+                chunks(s, 80, rows)
+            cd = fetch_into(b, dx, 7)
+            go("1c 0c")
+            go("1t 0k1")
+            go("0k2")
+            with scope("finish u"):
+                part = finish_u(1, guo1)
+            with scope("finish s"):
+                part = part + finish_s(0, gso1)
+            cd.wait()
+            for rel in range(4):
+                scatter(0).sent(rel)
+            return part
+
+        return sums + pl.run_scoped(rest, *narrow_types)
+
+    sums = sums + pl.run_scoped(final, *grid_types)
     with scope("total"):
         square[...] = totals.run(3, jnp.broadcast_to(sums, (4, 128)))
 
@@ -1898,12 +1998,12 @@
             S((s.ur, s.uc), F32), S((s.ur, s.uc), F32), S((2, 2 * (mid + d)), F32), S((4, 128), F32))
     rows = nb * s.nb
     scratch = [
-        V((4, 2, rows, kw), BF), V((4, rows, kw), BF), V((half * s.nb, kw), BF), V((half * s.nb, kw), BF),
-        V((rows, kw), BF), V((rows, kw), BF), V((rows, kw), BF), V((rows, kw), BF),
+        V((5, 2, rows, kw), BF), V((4, rows, kw), BF), V((half * s.nb, kw), BF), V((half * s.nb, kw), BF),
+        V((rows, kw), BF), V((rows, kw), BF), V((rows + s.nb, kw), BF),
+        V((rows, kw), BF), V((rows, kw), BF), V((rows + s.nb, kw), BF),
         V((3 * mid, d), BF), V((4, s.ur, d), BF), V((s.ur, s.uc), BF), V((s.ur, s.uc), BF), V((s.ur, s.uc), BF),
-        V((4, s.ur, d), BF), V((4, s.ur, d), BF), V((m - s.cut, d), BF),
+        V((4, s.ur, d + s.uc), BF), V((m - s.cut, d), BF),
         V((m, mid), BF), V((mid, m), BF), V((3, m, d), BF), V((kw, s.nb), F32),
-        V((2, kw // 2, s.nb), F32),
         V((4, s.slots, 4, mid), F32), V((4, nb, 4, mid), F32),
         dma((9,)), dma((4,)), dma((9, 3)), dma((2, 2, 2)), dma((2, 2, 2)), dma((2,)), dma((2,)),
         dma((4, 2, 4, nb)), dma((4, 2, 4, nb)),

time: 603 us -> 555 us (0.920)
  Pallas kernels: 563 us -> 514 us
    pallas_call x1, Pallas kernels: 290 us -> 248 us  [backward_call(): pl.pallas_call(functools.partial(backward_kernel, s), out_shape=outs, in_...]
    pallas_call x1, Pallas kernels: 274 us -> 265 us  [forward_call(): pl.pallas_call(functools.partial(forward_kernel, s), out_shape=outs, in_s...]
where the time goes in v4:
time: 555 us; the launch traced here: 550 us
  Pallas kernels  514 us (93%)
  other arithmetic  17.1 us (3%)
  local copies, waits for them, and re-layouts  15.9 us (3%)
    pallas_call x1, Pallas kernels, forward_call(): pl.pallas_call(functools.partial(forward_kernel, s), out_shape=outs, in_s...  265 us
    pallas_call x1, Pallas kernels, backward_call(): pl.pallas_call(functools.partial(backward_kernel, s), out_shape=outs, in_...  248 us

profile of v4, /device:TPU:0, one launch (start us, length us, event | category | flops | bytes accessed | tf_op | source)
XLA Modules:
  0.0 550.1 jit_solution(1208795140155762883)
XLA Ops:
  0.7 0.0 copy-start
  0.7 0.0 copy-start.7
  0.7 0.0 copy-start.1
  0.7 3.3 fusion.3
  4.0 0.0 copy-start.8
  4.0 0.0 copy-done
  4.1 1.1 copy.45
  5.2 0.0 copy-done.7
  5.2 0.7 convert_element_type.29.refs_3_
  5.8 0.0 copy-done.1
  5.9 1.1 copy.46
  6.9 0.0 copy-done.8
  6.9 0.7 convert_element_type.31.refs_5_
  7.6 0.0 copy-done.20
  7.6 0.2 dynamic-slice_reduce_fusion
  7.8 0.7 fusion.13.refs_7_.refs_19_
  8.4 0.1 reduce_sum.27
  8.6 0.0 copy-done.21
  8.6 0.5 multiply_divide_fusion.refs_8_.refs_20_
  9.1 265.3 %forward.1 = (bf16[4,1152,1152]{2,1,0:T(8,128)(2,1)}, bf16[3456,512]{1,0:T(8,128)(2,1)}, bf16[4,1152,1152]{2,1,0:T(8,128)(2,1)}, bf16[3456,512]{1,0:T(8,128)(2,1...) custom-call(bf16[1200,512]{1,0:T(8,128)(2,1)} %get-tuple-element.107, ...), custom_call_target="tpu_custom_call" | custom-call | tf_op jit(solution)/shard_map/forward/pallas_call | solution.py:1307
  274.4 0.0 copy-start.4
  274.4 1.3 slice_bitcast_fusion.3
  275.7 1.7 copy.49
  277.4 0.0 copy-done.4
  277.4 0.1 slice_bitcast_fusion.1
  277.6 2.8 copy.50
  280.4 248.3 %backward.1 = (f32[1200,512]{1,0:T(8,128)}, f32[2,576,144]{2,1,0:T(8,128)}, f32[2,576,144]{2,1,0:T(8,128)}, f32[432,128]{1,0:T(8,128)}, f32[432,128]{1,0:T(8,128)}, /*index=5*/f32[2,3328]{1,0:T(2,128)}, f32[4,128]{1,0:T(4,128)}) custom-call(bf16[4,1152,1152]{2,1,0:T(8,128)(2,1)} %get-tuple-element.47.refs_0_, bf16[3456,512]{1,0:T(8,128)(2,1)} %get-tuple-element.48.refs_1_, ...), custom_call_target="tpu_custom_call" | custom-call | tf_op jit(solution)/shard_map/backward/pallas_call | solution.py:2013
  528.7 0.0 copy-start.3
  528.7 1.3 slice_bitcast_fusion.2
  530.0 1.7 copy.51
  531.7 0.0 copy-done.3
  531.7 0.1 slice_bitcast_fusion
  531.9 0.0 copy-start.17
  531.9 0.0 copy-start.6
  531.9 2.8 copy.52
  534.7 1.3 slice_reduce_fusion
  536.0 0.0 copy-done.17
  536.0 0.6 multiply_reduce_fusion
  538.0 0.0 copy-done.6
  538.0 0.1 multiply_bitcast_fusion.1
  538.1 0.4 copy.47
  538.5 0.0 copy-start.5
  538.5 3.2 multiply_subtract_fusion.1
  541.7 0.0 copy-done.11
  541.7 0.0 copy-done.12
  541.7 0.0 copy-done.16
  541.7 0.9 multiply_subtract_fusion.3
  542.7 0.0 copy-done.5
  542.7 0.1 multiply_bitcast_fusion
  542.7 0.4 copy.48
  543.1 0.7 copy-done.2
  543.8 0.0 copy-start.10
  543.8 0.0 copy-start.18
  543.8 0.0 copy-start.19
  543.8 3.2 multiply_subtract_fusion
  547.0 0.0 copy-done.9
  547.0 0.0 copy-done.13
  547.0 0.0 copy-done.14
  547.0 0.0 copy-done.15
  547.1 0.9 multiply_subtract_fusion.2
  548.0 0.0 copy-done.10
  548.0 0.0 copy-done.18
  548.0 0.0 copy-done.19
  548.0 0.7 multiply_subtract_fusion.4
  (12 shorter events, 0.1 us)
Async XLA Ops:
  0.7 3.4 copy-start
  0.7 4.5 copy-start.7
  0.7 5.1 copy-start.1
  4.0 2.9 copy-start.8
  4.0 3.6 copy-start.20
  4.0 4.5 copy-start.21
  274.4 3.1 copy-start.4
  528.7 3.1 copy-start.3
  531.9 4.1 copy-start.17
  531.9 6.1 %copy-start.6 = (f32[2,576,144]{2,1,0:T(8,128)S(1)}, f32[2,576,144]{2,1,0:T(8,128)}, u32[]{:S(2)}) copy-start(f32[2,576,144]{2,1,0:T(8,128)} %get-tuple-element.68) | copy-start | bytes 1990660
  538.5 3.2 copy-start.11
  538.5 3.2 copy-start.12
  538.5 3.2 copy-start.16
  538.5 4.2 copy-start.5
  542.7 1.1 copy-start.2
  543.8 3.3 copy-start.9
  543.8 3.3 copy-start.13
  543.8 3.3 copy-start.14
  543.8 3.3 copy-start.15
  543.8 4.2 copy-start.10
  543.8 4.2 copy-start.18
  543.8 4.2 copy-start.19

commit v5 on v4

--- a/solution.py
+++ b/solution.py
@@ -1203,9 +1203,9 @@
     go("0h1 0s1 0p0 0h2 0s2 0p1 0f0 0h3 0s3 1z")
     spatial(0, gs1, (0, 1, 2, 3), ("", "", "0p2 0f1 1h1 0p3 1h2", "1x 1s1 1h3 1s2 1s3", "0f2", "1p0", "0f3 1p1 1f0", "2z"))
     xc1, zc1 = wide_norm(0, 0, z1_o, xh1_o, r1_o, 5, ("1p2 1f1 1p3 1f2 1f3", "2x 2h1 3z"), (0, 1))
-    temporal(0, ("", "2c 2l1 2h2 2l2 2d 3h1 2h3 2l3 2g1 3h2"))
+    temporal(0, ("2c", "2d 2h2"))
     total = narrow_total(1)
-    go("2a1 3h3 3x 3s1 3s2 3s3 2a2 2a3 2g2")
+    go("2a1 2l1 2a2 2l2 2g1 2h3 2a3 2l3 3h1")
     mean2, scale2 = moments(total, inv, d)
     r2_o[...] = jnp.concatenate(scale2, axis=0)
     gain2, bias2 = gain_bias(1)
@@ -1223,13 +1223,15 @@
     xc2 = pltpu.make_async_copy(b, xh2_o, local.at[7])
     xc2.start()
     halos[0].done()
+    go("2g2 3h2")
     taps_copy.wait()
     with scope("taps z2"):
         build_taps(s, grids, taps)
     taps_copy2 = pltpu.make_async_copy(taps, taps2_o, local.at[8])
     taps_copy2.start()
     xc1.wait()
-    spatial(2, gs2, (0, 2, 3, 1), ("", "2v0 2v1 2v2 2v3", "", "2g3", "", "3p0 3p1 3f0", "2u1 2u2 2u3", "3p2 3f1"))
+    spatial(2, gs2, (0, 2, 3, 1), ("", "", "2v0 2v1 2v2 2v3", "2g3 3h3 3x 3s1 3s2 3s3", "", "2u1 2u2 2u3 3p0",
+                                   "", "3p1 3f0 3p2 3f1"))
     zc1.wait()
     xc3, zc3 = wide_norm(2, 2, z3_o, xh3_o, r3_o, 9, ("3p3 3f2 3f3", ""), (1, 3))
     xc2.wait()

time: 555 us -> 543 us (0.978)
  Pallas kernels: 514 us -> 501 us
    pallas_call x1, Pallas kernels: 265 us -> 252 us  [forward_call(): pl.pallas_call(functools.partial(forward_kernel, s), out_shape=outs, in_s...]
where the time goes in v5:
time: 543 us; the launch traced here: 537 us
  Pallas kernels  501 us (92%)
  other arithmetic  17.1 us (3%)
  local copies, waits for them, and re-layouts  15.9 us (3%)
    pallas_call x1, Pallas kernels, forward_call(): pl.pallas_call(functools.partial(forward_kernel, s), out_shape=outs, in_s...  252 us
    pallas_call x1, Pallas kernels, backward_call(): pl.pallas_call(functools.partial(backward_kernel, s), out_shape=outs, in_...  248 us

profile of v5, /device:TPU:0, one launch (start us, length us, event | category | flops | bytes accessed | tf_op | source)
XLA Modules:
  0.0 537.3 jit_solution(99988469560802)
XLA Ops:
  0.7 0.0 copy-start
  0.7 0.0 copy-start.7
  0.7 0.0 copy-start.1
  0.7 3.3 fusion.3
  4.0 0.0 copy-start.8
  4.0 0.0 copy-done
  4.1 1.1 copy.45
  5.2 0.0 copy-done.7
  5.2 0.7 convert_element_type.29.refs_3_
  5.8 0.0 copy-done.1
  5.9 1.1 copy.46
  6.9 0.0 copy-done.8
  6.9 0.7 convert_element_type.31.refs_5_
  7.6 0.0 copy-done.20
  7.6 0.2 dynamic-slice_reduce_fusion
  7.8 0.7 fusion.13.refs_7_.refs_19_
  8.4 0.1 reduce_sum.27
  8.6 0.0 copy-done.21
  8.6 0.5 multiply_divide_fusion.refs_8_.refs_20_
  9.1 252.4 %forward.1 = (bf16[4,1152,1152]{2,1,0:T(8,128)(2,1)}, bf16[3456,512]{1,0:T(8,128)(2,1)}, bf16[4,1152,1152]{2,1,0:T(8,128)(2,1)}, bf16[3456,512]{1,0:T(8,128)(2,1...) custom-call(bf16[1200,512]{1,0:T(8,128)(2,1)} %get-tuple-element.107, ...), custom_call_target="tpu_custom_call" | custom-call | tf_op jit(solution)/shard_map/forward/pallas_call | solution.py:1309
  261.5 0.0 copy-start.4
  261.5 1.3 slice_bitcast_fusion.3
  262.9 1.7 copy.49
  264.6 0.0 copy-done.4
  264.6 0.1 slice_bitcast_fusion.1
  264.7 2.8 copy.50
  267.6 248.2 %backward.1 = (f32[1200,512]{1,0:T(8,128)}, f32[2,576,144]{2,1,0:T(8,128)}, f32[2,576,144]{2,1,0:T(8,128)}, f32[432,128]{1,0:T(8,128)}, f32[432,128]{1,0:T(8,128)}, /*index=5*/f32[2,3328]{1,0:T(2,128)}, f32[4,128]{1,0:T(4,128)}) custom-call(bf16[4,1152,1152]{2,1,0:T(8,128)(2,1)} %get-tuple-element.47.refs_0_, bf16[3456,512]{1,0:T(8,128)(2,1)} %get-tuple-element.48.refs_1_, ...), custom_call_target="tpu_custom_call" | custom-call | tf_op jit(solution)/shard_map/backward/pallas_call | solution.py:2015
  515.8 0.0 copy-start.3
  515.8 1.3 slice_bitcast_fusion.2
  517.2 1.7 copy.51
  518.9 0.0 copy-done.3
  518.9 0.1 slice_bitcast_fusion
  519.0 0.0 copy-start.17
  519.0 0.0 copy-start.6
  519.1 2.8 copy.52
  521.9 1.3 slice_reduce_fusion
  523.2 0.0 copy-done.17
  523.2 0.6 multiply_reduce_fusion
  525.2 0.0 copy-done.6
  525.2 0.1 multiply_bitcast_fusion.1
  525.3 0.4 copy.47
  525.7 0.0 copy-start.5
  525.7 3.2 multiply_subtract_fusion.1
  528.9 0.0 copy-done.11
  528.9 0.0 copy-done.12
  528.9 0.0 copy-done.16
  528.9 0.9 multiply_subtract_fusion.3
  529.8 0.0 copy-done.5
  529.8 0.1 multiply_bitcast_fusion
  529.9 0.4 copy.48
  530.3 0.7 copy-done.2
  531.0 0.0 copy-start.10
  531.0 0.0 copy-start.18
  531.0 0.0 copy-start.19
  531.0 3.2 multiply_subtract_fusion
  534.2 0.0 copy-done.9
  534.2 0.0 copy-done.13
  534.2 0.0 copy-done.14
  534.2 0.0 copy-done.15
  534.2 0.9 multiply_subtract_fusion.2
  535.2 0.0 copy-done.10
  535.2 0.0 copy-done.18
  535.2 0.0 copy-done.19
  535.2 0.7 multiply_subtract_fusion.4
  (12 shorter events, 0.1 us)
Async XLA Ops:
  0.7 3.4 copy-start
  0.7 4.5 copy-start.7
  0.7 5.1 copy-start.1
  4.0 2.9 copy-start.8
  4.0 3.6 copy-start.20
  4.0 4.5 copy-start.21
  261.5 3.1 copy-start.4
  515.8 3.1 copy-start.3
  519.0 4.1 copy-start.17
  519.0 6.1 %copy-start.6 = (f32[2,576,144]{2,1,0:T(8,128)S(1)}, f32[2,576,144]{2,1,0:T(8,128)}, u32[]{:S(2)}) copy-start(f32[2,576,144]{2,1,0:T(8,128)} %get-tuple-element.68) | copy-start | bytes 1990660
  525.6 3.2 copy-start.11
  525.6 3.2 copy-start.12
  525.6 3.2 copy-start.16
  525.7 4.2 copy-start.5
  529.8 1.1 copy-start.2
  530.9 3.3 copy-start.9
  530.9 3.3 copy-start.13
  530.9 3.3 copy-start.14
  530.9 3.3 copy-start.15
  531.0 4.2 copy-start.10
  531.0 4.2 copy-start.18
  531.0 4.2 copy-start.19
